TPU v7x, 32 devices: a whole 2x2x4 slice. The times are simulated.
32 devices in a mesh: group: 2 (over y), tm: 8 (over z, core), pix: 2 (over x), sub: 1.
Axes of the slice: x: 2, y: 2, z: 4, core: 2. Of those that a mesh axis runs over, the one named last changes fastest.
Arguments:
- anomaly: bfloat16 [512, 65536], P('tm', ('group', 'pix', 'sub')), parts along dimension 1, may hold values from -6 to 6
- offsets: int32 [32], replicated, may hold values from 0 to 256, as said below
- taper_index: int32 [32], replicated, may hold values from 0 to 3
Outputs:
- spectral_gram: float32 [256, 64, 64], P(('group', 'tm')), parts along dimension 0
- leading_energy: float32 [256], P(('group', 'tm')), parts along dimension 0
There are 2 independent parts, one for each index of `group`. A program takes and returns all parts, laid end to end along the dimension named above; an argument that names none is the same for every part. Nothing has to cross between parts.
Inputs may be any that keep to these rules, and one draw needn't show every extreme that they name: `offsets`: block starts never fall; the first block starts at day 0 and the last at day 512 - 256.
All inputs are finite; a program needn't handle non-finite values.
Results may differ from a plain program's by a relative error of at most 0.0034.
Values may be sent and summed in bfloat16 or wider, within the bound.
No kernel may reach another device: no remote copies, remote signals or barrier semaphores. Data moves between devices by JAX's collectives and lax.ppermute only.
A program may use at most 128 MiB of HBM per device.

v0:
```python
import math

import jax
import jax.numpy as jnp
from jax import lax
from jax.sharding import PartitionSpec as P

NFFT = 256
NB = 32
POWER = 8
NF = 128


power_eps = 1e-06


def window_rows(taper_index, length):
    steps_t = jnp.arange(length, dtype=jnp.float32)
    phase = steps_t * (2.0 * math.pi / length)
    center = (steps_t + 0.5) * (math.pi / length)
    hann = jnp.sin(center) ** 2
    hamming = 0.54 - 0.46 * jnp.cos(phase)
    blackman = 0.42 - 0.5 * jnp.cos(phase) + 0.08 * jnp.cos(2.0 * phase)
    sine_win = jnp.sin(center)
    table_rows = jnp.stack([hann, hamming, blackman, sine_win])
    chosen = jnp.zeros((taper_index.shape[0], length), jnp.float32)
    for which in range(4):
        chosen = chosen + jnp.where(
            taper_index[:, None] == which, table_rows[which][None, :], jnp.float32(0.0)
        )
    return chosen


def dft_table(length, kept):
    freqs = jnp.arange(kept, dtype=jnp.int32)
    times = jnp.arange(length, dtype=jnp.int32)
    product = freqs[:, None] * times[None, :] % length
    angle = product.astype(jnp.float32) * (2.0 * math.pi / length)
    return jnp.stack([jnp.cos(angle), -jnp.sin(angle)]).astype(jnp.bfloat16)


def local_gram(spectra):
    stacked = spectra.reshape(2 * spectra.shape[1], spectra.shape[2], spectra.shape[3])
    return jnp.einsum("ifp,jfp->fij", stacked, stacked, preferred_element_type=jnp.float32)


def shards(anomaly, offsets, taper_index):
    series = lax.all_to_all(anomaly, "tm", split_axis=1, concat_axis=0, tiled=True)
    windows = window_rows(taper_index, NFFT)
    energy = 1.0 / jnp.sqrt(jnp.sum(windows * windows, axis=1))
    transform = dft_table(NFFT, NF)
    width_here = series.shape[1]
    per_group = 8
    gram_width = 2 * NB

    def fill_group(position, buffer):
        first_block = position * per_group
        starts = lax.dynamic_slice_in_dim(offsets, first_block, per_group, 0)
        shapes = lax.dynamic_slice_in_dim(windows, first_block, per_group, 0)
        scales = lax.dynamic_slice_in_dim(energy, first_block, per_group, 0)
        segments = jax.vmap(lambda first_day: lax.dynamic_slice_in_dim(series, first_day, NFFT, 0))(
            starts
        )
        windowed = (segments * shapes[:, :, None]).astype(jnp.bfloat16)
        spectra = jnp.einsum(
            "rkt,btp->rbkp", transform, windowed, preferred_element_type=jnp.float32
        )
        spectra = (spectra * scales[None, :, None, None]).astype(jnp.bfloat16)
        return lax.dynamic_update_slice_in_dim(buffer, spectra, first_block, 1)

    empty = jnp.zeros((2, NB, NF, width_here), jnp.bfloat16)
    spectra = lax.fori_loop(0, NB // per_group, fill_group, empty)
    received = lax.all_to_all(spectra, "tm", split_axis=2, concat_axis=3, tiled=True)
    partial_value = local_gram(received)
    summed = lax.psum(partial_value, ("pix", "sub"))
    total_pixels = anomaly.shape[1] * lax.axis_size(("pix", "sub"))
    spectral_gram = summed / total_pixels
    vector = jnp.ones((spectral_gram.shape[0], gram_width), jnp.float32)
    for _ in range(POWER):
        applied = jnp.einsum("fij,fj->fi", spectral_gram, vector, precision=lax.Precision.HIGHEST)
        vector = applied / jnp.sqrt(jnp.mean(applied * applied, axis=1, keepdims=True) + power_eps)
    applied = jnp.einsum("fij,fj->fi", spectral_gram, vector, precision=lax.Precision.HIGHEST)
    leading_energy = jnp.sqrt(jnp.mean(applied * applied, axis=1))
    return (spectral_gram, leading_energy)


def solution(mesh):
    placed = (P("tm", ("group", "pix", "sub")), P(), P())
    return jax.shard_map(
        shards,
        mesh=mesh,
        in_specs=placed,
        out_specs=(P(("group", "tm"), None, None), P(("group", "tm"))),
        check_vma=False,
    )
```

profile of v0, /device:TPU:0, one launch (start us, length us, event | category | flops | bytes accessed | tf_op | source)
XLA Modules:
  0.0 1170.2 jit_solution(9330474396484308255)
XLA Ops:
  7.2 3.2 copy.48
  10.4 6.3 all-to-all-start
  18.3 47.5 %all-to-all-done = bf16[64,8,2048]{2,0,1:T(8,128)(2,1)S(1)} async-done(((bf16[64,8,2048]{2,0,1:T(8,128)(2,1)}), bf16[64,8,2048]{2,0,1:T(8,128)(2,1)S(1)}, u32[]{:S(2)}, u32[]{:S(2)}) %all-to-all-start) | async-done | bytes 2097184 | tf_op jit(solution)/shard_map/all_to_all | solution.py:48
  65.8 11.0 broadcast_in_dim.86.clone
  76.7 208.3 %while.16 = (s32[]{:T(128)}, bf16[2,32,128,2048]{3,1,0,2:T(8,128)(2,1)}, s32[32]{0:T(128)S(1)}, bf16[512,2048]{1,0:T(8,128)(2,1)S(1)}, f32[32,256]{1,0:T(8,128)S...) while((s32[]{:T(128)}, ...), condition=%wide.region_2.3_spmd, body=%wide.region_1.2_spmd.sunk | while | flops 2168455168 | bytes 52586048 | solution.py:72
  76.8 19.1 %while.17 = (s32[]{:T(128)}, bf16[512,2048]{1,0:T(8,128)(2,1)S(1)}, s32[8,2]{0,1:T(2,128)S(1)}, bf16[8,256,2048]{2,1,0:T(8,128)(2,1)}, s32[]{:T(128)}) while((s32[]{:T(128)}, bf16[512,2048]{1,0:T(8,128)(2,1)S(1)}, s32[8,2]{0,1:T(2,128)S(1)}, bf16[8,256,2048]{2,1,0:T(8,128)(2,1)}, s32[]{:T(128)}) %tuple.54), condition=%wide.while_cond, body=%wide.while_body.sunk | while | flops 2 | bytes 2098265 | solution.py:61
  77.4 1.8 bitcast_dynamic-update-slice_fusion.2
  79.7 1.9 bitcast_dynamic-update-slice_fusion.2
  82.2 1.8 bitcast_dynamic-update-slice_fusion.2
  84.5 1.8 bitcast_dynamic-update-slice_fusion.2
  89.3 1.8 bitcast_dynamic-update-slice_fusion.2
  91.7 1.8 bitcast_dynamic-update-slice_fusion.2
  96.0 12.1 %fusion.53 = bf16[2,8,128,2048]{2,3,0,1:T(8,128)(2,1)} fusion(f32[8]{0:T(128)S(1)} %dynamic_slice.28, bf16[8,256,2048]{2,1,0:T(8,128)(2,1)} %get-tuple-element.242, f32[8,256]{1,0:T(8,128)S(1)} %constant_dynamic-slice_fusion.4, bf16[2,128,256]{2,1,0:T(8,128)(2,1)S(1)} %get-tuple-element.292), kind=kOutput, calls=%fused_computation.6.clone.1 | convolution fusion | flops 2168455168 | bytes 16916512 | tf_op jit(solution)/shard_map/while/body/eval_jaxpr/rkt,btp->rbkp/dot_general | solution.py:65
  108.0 12.6 %copy.50 = bf16[2,8,128,2048]{3,1,0,2:T(8,128)(2,1)} copy(bf16[2,8,128,2048]{2,3,0,1:T(8,128)(2,1)} %fusion.53) | data formatting | bytes 16777216 | tf_op jit(solution)/shard_map/while/body/eval_jaxpr/dynamic_update_slice | solution.py:69
  120.6 8.2 constant_dynamic-update-slice_fusion.2
  128.9 19.1 %while.17 = (s32[]{:T(128)}, bf16[512,2048]{1,0:T(8,128)(2,1)S(1)}, s32[8,2]{0,1:T(2,128)S(1)}, bf16[8,256,2048]{2,1,0:T(8,128)(2,1)}, s32[]{:T(128)}) while((s32[]{:T(128)}, bf16[512,2048]{1,0:T(8,128)(2,1)S(1)}, s32[8,2]{0,1:T(2,128)S(1)}, bf16[8,256,2048]{2,1,0:T(8,128)(2,1)}, s32[]{:T(128)}) %tuple.54), condition=%wide.while_cond, body=%wide.while_body.sunk | while | flops 2 | bytes 2098265 | solution.py:61
  129.4 1.8 bitcast_dynamic-update-slice_fusion.2
  131.8 1.9 bitcast_dynamic-update-slice_fusion.2
  134.2 1.8 bitcast_dynamic-update-slice_fusion.2
  141.3 1.8 bitcast_dynamic-update-slice_fusion.2
  143.7 1.8 bitcast_dynamic-update-slice_fusion.2
  148.0 12.1 %fusion.53 = bf16[2,8,128,2048]{2,3,0,1:T(8,128)(2,1)} fusion(f32[8]{0:T(128)S(1)} %dynamic_slice.28, bf16[8,256,2048]{2,1,0:T(8,128)(2,1)} %get-tuple-element.242, f32[8,256]{1,0:T(8,128)S(1)} %constant_dynamic-slice_fusion.4, bf16[2,128,256]{2,1,0:T(8,128)(2,1)S(1)} %get-tuple-element.292), kind=kOutput, calls=%fused_computation.6.clone.1 | convolution fusion | flops 2168455168 | bytes 16916512 | tf_op jit(solution)/shard_map/while/body/eval_jaxpr/rkt,btp->rbkp/dot_general | solution.py:65
  160.1 12.6 %copy.50 = bf16[2,8,128,2048]{3,1,0,2:T(8,128)(2,1)} copy(bf16[2,8,128,2048]{2,3,0,1:T(8,128)(2,1)} %fusion.53) | data formatting | bytes 16777216 | tf_op jit(solution)/shard_map/while/body/eval_jaxpr/dynamic_update_slice | solution.py:69
  172.6 8.2 constant_dynamic-update-slice_fusion.2
  181.0 19.1 %while.17 = (s32[]{:T(128)}, bf16[512,2048]{1,0:T(8,128)(2,1)S(1)}, s32[8,2]{0,1:T(2,128)S(1)}, bf16[8,256,2048]{2,1,0:T(8,128)(2,1)}, s32[]{:T(128)}) while((s32[]{:T(128)}, bf16[512,2048]{1,0:T(8,128)(2,1)S(1)}, s32[8,2]{0,1:T(2,128)S(1)}, bf16[8,256,2048]{2,1,0:T(8,128)(2,1)}, s32[]{:T(128)}) %tuple.54), condition=%wide.while_cond, body=%wide.while_body.sunk | while | flops 2 | bytes 2098265 | solution.py:61
  181.5 1.8 bitcast_dynamic-update-slice_fusion.2
  183.9 1.9 bitcast_dynamic-update-slice_fusion.2
  186.3 1.8 bitcast_dynamic-update-slice_fusion.2
  193.4 1.8 bitcast_dynamic-update-slice_fusion.2
  195.8 1.8 bitcast_dynamic-update-slice_fusion.2
  200.1 12.1 %fusion.53 = bf16[2,8,128,2048]{2,3,0,1:T(8,128)(2,1)} fusion(f32[8]{0:T(128)S(1)} %dynamic_slice.28, bf16[8,256,2048]{2,1,0:T(8,128)(2,1)} %get-tuple-element.242, f32[8,256]{1,0:T(8,128)S(1)} %constant_dynamic-slice_fusion.4, bf16[2,128,256]{2,1,0:T(8,128)(2,1)S(1)} %get-tuple-element.292), kind=kOutput, calls=%fused_computation.6.clone.1 | convolution fusion | flops 2168455168 | bytes 16916512 | tf_op jit(solution)/shard_map/while/body/eval_jaxpr/rkt,btp->rbkp/dot_general | solution.py:65
  212.2 12.6 %copy.50 = bf16[2,8,128,2048]{3,1,0,2:T(8,128)(2,1)} copy(bf16[2,8,128,2048]{2,3,0,1:T(8,128)(2,1)} %fusion.53) | data formatting | bytes 16777216 | tf_op jit(solution)/shard_map/while/body/eval_jaxpr/dynamic_update_slice | solution.py:69
  224.7 8.2 constant_dynamic-update-slice_fusion.2
  233.0 19.1 %while.17 = (s32[]{:T(128)}, bf16[512,2048]{1,0:T(8,128)(2,1)S(1)}, s32[8,2]{0,1:T(2,128)S(1)}, bf16[8,256,2048]{2,1,0:T(8,128)(2,1)}, s32[]{:T(128)}) while((s32[]{:T(128)}, bf16[512,2048]{1,0:T(8,128)(2,1)S(1)}, s32[8,2]{0,1:T(2,128)S(1)}, bf16[8,256,2048]{2,1,0:T(8,128)(2,1)}, s32[]{:T(128)}) %tuple.54), condition=%wide.while_cond, body=%wide.while_body.sunk | while | flops 2 | bytes 2098265 | solution.py:61
  233.6 1.8 bitcast_dynamic-update-slice_fusion.2
  236.0 1.9 bitcast_dynamic-update-slice_fusion.2
  238.4 1.8 bitcast_dynamic-update-slice_fusion.2
  240.8 1.8 bitcast_dynamic-update-slice_fusion.2
  245.5 1.8 bitcast_dynamic-update-slice_fusion.2
  247.9 1.8 bitcast_dynamic-update-slice_fusion.2
  252.2 12.1 %fusion.53 = bf16[2,8,128,2048]{2,3,0,1:T(8,128)(2,1)} fusion(f32[8]{0:T(128)S(1)} %dynamic_slice.28, bf16[8,256,2048]{2,1,0:T(8,128)(2,1)} %get-tuple-element.242, f32[8,256]{1,0:T(8,128)S(1)} %constant_dynamic-slice_fusion.4, bf16[2,128,256]{2,1,0:T(8,128)(2,1)S(1)} %get-tuple-element.292), kind=kOutput, calls=%fused_computation.6.clone.1 | convolution fusion | flops 2168455168 | bytes 16916512 | tf_op jit(solution)/shard_map/while/body/eval_jaxpr/rkt,btp->rbkp/dot_general | solution.py:65
  264.2 12.6 %copy.50 = bf16[2,8,128,2048]{3,1,0,2:T(8,128)(2,1)} copy(bf16[2,8,128,2048]{2,3,0,1:T(8,128)(2,1)} %fusion.53) | data formatting | bytes 16777216 | tf_op jit(solution)/shard_map/while/body/eval_jaxpr/dynamic_update_slice | solution.py:69
  276.8 8.2 constant_dynamic-update-slice_fusion.2
  285.0 736.0 %all_to_all.34 = bf16[2,32,128,2048]{3,1,0,2:T(8,128)(2,1)} all-to-all(bf16[2,32,128,2048]{3,1,0,2:T(8,128)(2,1)} %get-tuple-element.126), channel_id=1, replica_groups=mesh['group'=2,'tm'=8,'pix'=2,'sub'=1] {'tm'}, dimensions={2} | all-to-all | bytes 67108864 | tf_op jit(solution)/shard_map/all_to_all | solution.py:73
  1021.0 30.0 %copy.21 = bf16[2,32,16,8,2048]{4,3,1,0,2:T(8,128)(2,1)} copy(bf16[2,32,16,8,2048]{4,1,0,2,3:T(8,128)(2,1)} %bitcast.107) | data formatting | bytes 67108864 | tf_op jit(solution)/shard_map/all_to_all | solution.py:73
  1051.0 49.9 %reshape.182 = bf16[64,16,16384]{2,0,1:T(8,128)(2,1)} reshape(bf16[2,32,16,8,2048]{4,3,1,0,2:T(8,128)(2,1)} %copy.21) | data formatting | bytes 67108864 | tf_op jit(solution)/shard_map/reshape | solution.py:43
  1100.9 23.5 %fusion.16 = f32[16,64,64]{2,1,0:T(8,128)} fusion(bf16[64,16,16384]{2,0,1:T(8,128)(2,1)} %reshape.182), kind=kOutput, calls=%fused_computation.64 | convolution fusion | flops 2147483648 | bytes 33816576 | tf_op jit(solution)/shard_map/ifp,jfp->fij/dot_general | solution.py:44
  1124.4 27.1 %all-reduce.3.cloned.1.call-done = f32[16,64,64]{2,1,0:T(8,128)} async-done(((f32[16,64,64]{2,1,0:T(8,128)}), f32[16,64,64]{2,1,0:T(8,128)}) %all-reduce.3.cloned.1.call-update) | async-done | bytes 262160 | tf_op jit(solution)/shard_map/psum | solution.py:75
  (144 shorter events, 49.9 us)
Async XLA Ops:
  10.4 55.4 %all-to-all-start = ((bf16[64,8,2048]{2,0,1:T(8,128)(2,1)}), bf16[64,8,2048]{2,0,1:T(8,128)(2,1)S(1)}, u32[]{:S(2)}, u32[]{:S(2)}) async-start(bf16[64,8,2048]{2,0,1:T(8,128)(2,1)} %bitcast.108), calls=%async_computation | async-start | bytes 4194304 | tf_op jit(solution)/shard_map/all_to_all | solution.py:48
  16.7 1134.8 %all-reduce.3.cloned.1.call-start = ((), (), s32[]{:S(2)}) async-start(), calls=%async_computation.2 | async-start | bytes 1048576 | tf_op jit(solution)/shard_map/psum | solution.py:75
  65.7 11.0 copy-start.1
  1152.6 10.8 copy-start
Sparse Core Ops, SparseCore 0:
  1124.5 26.9 all-reduce.2
where the time goes:
time: 1170 us
  blocking collectives  736 us (63%)
  local copies, waits for them, and re-layouts  254 us (22%)
  matrix products  80.2 us (7%)
  waiting for transfers between devices  74.6 us (6%)
  between operations  14.2 us (1%)
    all_to_all x1, blocking collectives, shards(): lax.all_to_all(spectra, 'tm', split_axis=2, concat_axis=3, tiled=True)  736 us
    dynamic_update_slice x8, local copies, waits for them, and re-layouts, fill_group(): return lax.dynamic_update_slice_in_dim(buffer, spectra, first_block, 1)  83.1 us
    gather x96, local copies, waits for them, and re-layouts  76.2 us
    reshape x1, local copies, waits for them, and re-layouts, local_gram(): spectra.reshape(2 * spectra.shape[1], spectra.shape[2], spectra.shape[3])  49.9 us
    dot_general x4, matrix products, fill_group(): jnp.einsum('rkt,btp->rbkp', transform, windowed, preferred_element_type=j...  48.2 us
    all_to_all x1, waiting for transfers between devices, shards(): lax.all_to_all(anomaly, 'tm', split_axis=1, concat_axis=0, tiled=True)  47.5 us
    all_to_all x1, local copies, waits for them, and re-layouts, shards(): lax.all_to_all(spectra, 'tm', split_axis=2, concat_axis=3, tiled=True)  30 us
    psum x1, waiting for transfers between devices, shards(): summed = lax.psum(partial_value, ('pix', 'sub'))  27.1 us
  transfers between devices with their start and end apart: 2, of which 2 were waited for; matrix products, arithmetic and copies ran while one was open for 0% of the time, Pallas kernels for 0%

commit v1 on v0

--- a/solution.py
+++ b/solution.py
@@ -1,15 +1,20 @@
+import functools
 import math
 
 import jax
 import jax.numpy as jnp
+import numpy as np
 from jax import lax
+from jax.experimental import pallas as pl
+from jax.experimental.pallas import tpu as pltpu
 from jax.sharding import PartitionSpec as P
 
 NFFT = 256
 NB = 32
 POWER = 8
 NF = 128
-
+TILE = 128
+VMEM_BYTES = 40 * 1024 * 1024
 
 power_eps = 1e-06
 
@@ -44,7 +49,7 @@
     return jnp.einsum("ifp,jfp->fij", stacked, stacked, preferred_element_type=jnp.float32)
 
 
-def shards(anomaly, offsets, taper_index):
+def spectra_shards(anomaly, offsets, taper_index):
     series = lax.all_to_all(anomaly, "tm", split_axis=1, concat_axis=0, tiled=True)
     windows = window_rows(taper_index, NFFT)
     energy = 1.0 / jnp.sqrt(jnp.sum(windows * windows, axis=1))
@@ -84,8 +89,186 @@
     return (spectral_gram, leading_energy)
 
 
+def day_factors(days):
+    return (1.0 + 0.4 * ((np.arange(days) * 0.6180339887498949) % 1.0)).astype(np.float32)
+
+
+def upper_tiles(days):
+    count = days // TILE
+    return [(i, j) for i in range(count) for j in range(i, count)]
+
+
+def weights(offsets, taper_index, first_freq, freqs, days):
+    local = jnp.arange(days, dtype=jnp.int32)[None, :] - offsets[:, None]
+    inside = (local >= 0) & (local < NFFT)
+    steps_t = local.astype(jnp.float32)
+    phase = steps_t * (2.0 * math.pi / NFFT)
+    center = (steps_t + 0.5) * (math.pi / NFFT)
+    sine_win = jnp.sin(center)
+    table = [
+        sine_win**2,
+        0.54 - 0.46 * jnp.cos(phase),
+        0.42 - 0.5 * jnp.cos(phase) + 0.08 * jnp.cos(2.0 * phase),
+        sine_win,
+    ]
+    window = jnp.zeros(local.shape, jnp.float32)
+    for which in range(4):
+        window = window + jnp.where(taper_index[:, None] == which, table[which], 0.0)
+    window = jnp.where(inside, window, 0.0)
+    energy = 1.0 / jnp.sqrt(jnp.sum(window * window, axis=1, keepdims=True))
+    window = window * energy * (1.0 / day_factors(days))[None, :]
+
+    def turn(steps):
+        freq = first_freq + jnp.arange(freqs, dtype=jnp.int32)
+        angle = ((freq[:, None] * steps[None, :]) % NFFT).astype(jnp.float32)
+        angle = angle * (2.0 * math.pi / NFFT)
+        return jnp.cos(angle), jnp.sin(angle)
+
+    cos_t, sin_t = lax.optimization_barrier(turn(jnp.arange(days, dtype=jnp.int32)))
+    cos_b, sin_b = lax.optimization_barrier(turn(offsets))
+    window = lax.optimization_barrier(window)
+    ct, st = cos_t[:, None, :], sin_t[:, None, :]
+    cb, sb = cos_b[:, :, None], sin_b[:, :, None]
+    real = window * (ct * cb + st * sb)
+    imag = window * (ct * sb - st * cb)
+    return jnp.concatenate([real, imag], axis=1).astype(jnp.bfloat16)
+
+
+def covariance_kernel(tiles, place, *refs):
+    n = len(refs) - 6
+    pieces, (drow, dcol, keep, send, xs, cs) = refs[:n], refs[n:]
+    me = place[0]
+    rows = pieces[0].shape[0]
+    for d in range(n):
+        xs[pl.ds(pl.multiple_of((me ^ d) * rows, rows), rows), :] = pieces[d][...]
+    for i in range(xs.shape[0] // TILE):
+        here = slice(i * TILE, (i + 1) * TILE)
+        strip = lax.dot_general(
+            xs[here, :], xs[i * TILE :, :], (((1,), (1,)), ((), ())), preferred_element_type=jnp.float32
+        )
+        strip = strip * dcol[here, :] * drow[:, i * TILE :]
+        for u, (a, b) in enumerate(tiles):
+            if a == i:
+                cs[u] = strip[:, (b - i) * TILE : (b - i + 1) * TILE]
+    half = TILE // 2
+    core = me % 2
+    keep[...] = cs[:, pl.ds(pl.multiple_of(core * half, half), half), :]
+    send[...] = cs[:, pl.ds(pl.multiple_of((1 - core) * half, half), half), :].astype(jnp.bfloat16)
+
+
+def finish_kernel(tiles, scale, place, w, q0, q1, q2, q3, gram, energy, packed, full, y):
+    core, pix = place[0] % 2, place[1]
+    quarter = TILE // 4
+    for source, (c, x) in zip((q0, q1, q2, q3), ((0, 0), (0, 1), (1, 0), (1, 1))):
+        at = (core ^ c) * (2 * quarter) + (pix ^ x) * quarter
+        packed[:, pl.ds(pl.multiple_of(at, quarter), quarter), :] = source[...]
+    for u, (a, b) in enumerate(tiles):
+        block = packed[u]
+        full[a * TILE : (a + 1) * TILE, b * TILE : (b + 1) * TILE] = block
+        if a != b:
+            full[b * TILE : (b + 1) * TILE, a * TILE : (a + 1) * TILE] = block.T
+    freqs, width, days = w.shape
+    flat = w[...].reshape(freqs * width, days)
+    y[...] = jnp.dot(flat, full[...], preferred_element_type=jnp.float32).astype(jnp.bfloat16)
+    for f in range(freqs):
+        gram[f] = scale * lax.dot_general(
+            y[f * width : (f + 1) * width, :], w[f], (((1,), (1,)), ((), ())), preferred_element_type=jnp.float32
+        )
+    g = gram[...]
+    vector = jnp.ones((freqs, 1, width), jnp.float32)
+    along = 2
+    for step in range(POWER + 1):
+        applied = jnp.sum(g * vector, axis=along, keepdims=True)
+        along = 3 - along
+        mean = jnp.sum(applied * applied, axis=along, keepdims=True) * (1.0 / width)
+        if step < POWER:
+            vector = applied / jnp.sqrt(mean + power_eps)
+    energy[...] = jnp.sqrt(mean[:, :, 0])
+
+
+def covariance_shards(anomaly, offsets, taper_index):
+    n = lax.axis_size("tm")
+    me, pix = lax.axis_index("tm"), lax.axis_index("pix")
+    rows, width = anomaly.shape[0], anomaly.shape[1] // n
+    days = rows * n
+    freqs = NF // n
+    tiles = upper_tiles(days)
+    place = jnp.stack([me, pix]).astype(jnp.int32)
+
+    def tm_swap(value, bit):
+        return lax.ppermute(value, "tm", [(i, i ^ bit) for i in range(n)])
+
+    def pix_swap(value):
+        return lax.ppermute(value, "pix", [(0, 1), (1, 0)])
+
+    pieces = {}
+    for d in list(range(n // 2, n)) + list(range(1, n // 2)):
+        pieces[d] = tm_swap(lax.dynamic_slice_in_dim(anomaly, (me ^ d) * width, width, 1), d)
+    pieces[0] = lax.dynamic_slice_in_dim(anomaly, me * width, width, 1)
+    w = weights(offsets, taper_index, me * freqs, freqs, days)
+
+    factors = day_factors(days)
+    vmem = pl.BlockSpec(memory_space=pltpu.VMEM)
+    smem = pl.BlockSpec(memory_space=pltpu.SMEM)
+    params = pltpu.CompilerParams(vmem_limit_bytes=VMEM_BYTES)
+    half = (len(tiles), TILE // 2, TILE)
+    keep, send = pl.pallas_call(
+        functools.partial(covariance_kernel, tiles),
+        out_shape=(jax.ShapeDtypeStruct(half, jnp.float32), jax.ShapeDtypeStruct(half, jnp.bfloat16)),
+        in_specs=[smem] + [vmem] * (n + 2),
+        out_specs=(vmem, vmem),
+        scratch_shapes=[
+            pltpu.VMEM((days, width), jnp.bfloat16),
+            pltpu.VMEM((len(tiles), TILE, TILE), jnp.float32),
+        ],
+        compiler_params=params,
+    )(place, *[pieces[d] for d in range(n)], jnp.asarray(factors[None, :]), jnp.asarray(factors[:, None]))
+
+    summed = keep + tm_swap(send, 1).astype(jnp.float32)
+    quarter = TILE // 4
+    mine = lax.dynamic_slice_in_dim(summed, pix * quarter, quarter, 1)
+    other = lax.dynamic_slice_in_dim(summed, (1 - pix) * quarter, quarter, 1)
+    mine = mine + pix_swap(other.astype(jnp.bfloat16)).astype(jnp.float32)
+    bit = 2
+    while bit < n:
+        mine = mine + tm_swap(mine.astype(jnp.bfloat16), bit).astype(jnp.float32)
+        bit *= 2
+    q0 = mine.astype(jnp.bfloat16)
+    q1 = pix_swap(q0)
+    q2 = tm_swap(q0, 1)
+    q3 = tm_swap(q1, 1)
+
+    gram_width = 2 * NB
+    total_pixels = anomaly.shape[1] * lax.axis_size("pix")
+    gram, energy = pl.pallas_call(
+        functools.partial(finish_kernel, tiles, 1.0 / total_pixels),
+        out_shape=(
+            jax.ShapeDtypeStruct((freqs, gram_width, gram_width), jnp.float32),
+            jax.ShapeDtypeStruct((freqs, 1), jnp.float32),
+        ),
+        in_specs=[smem] + [vmem] * 5,
+        out_specs=(vmem, vmem),
+        scratch_shapes=[
+            pltpu.VMEM((len(tiles), TILE, TILE), jnp.bfloat16),
+            pltpu.VMEM((days, days), jnp.bfloat16),
+            pltpu.VMEM((freqs * gram_width, days), jnp.bfloat16),
+        ],
+        compiler_params=params,
+    )(place, w, q0, q1, q2, q3)
+    return gram, energy[:, 0]
+
+
 def solution(mesh):
     placed = (P("tm", ("group", "pix", "sub")), P(), P())
+    n = mesh.shape["tm"]
+
+    def shards(anomaly, offsets, taper_index):
+        days = anomaly.shape[0] * n
+        pairs = mesh.shape["pix"] == 2 and mesh.shape["sub"] == 1 and n in (2, 4, 8)
+        if pairs and days % TILE == 0 and days <= 2 * NFFT:
+            return covariance_shards(anomaly, offsets, taper_index)
+        return spectra_shards(anomaly, offsets, taper_index)
+
     return jax.shard_map(
         shards,
         mesh=mesh,

time: 1170 us -> 83.7 us (0.07)
  blocking collectives: 736 us -> 0 us
  local copies, waits for them, and re-layouts: 254 us -> 2.48 us
  matrix products: 80.2 us -> 0 us
  waiting for transfers between devices: 74.6 us -> 41.3 us
  starting transfers between devices: 6.36 us -> 30.3 us
  between operations: 14.2 us -> 0.81 us
    all_to_all x1 -> x0, blocking collectives: 736 us -> none  [shards(): lax.all_to_all(spectra, 'tm', split_axis=2, concat_axis=3, tiled=True)]
    dynamic_update_slice x8 -> x0, local copies, waits for them, and re-layouts: 83.1 us -> none  [fill_group(): return lax.dynamic_update_slice_in_dim(buffer, spectra, first_block, 1)]
    dot_general x14 -> x0, matrix products: 80.2 us -> none  [the longest x4 48.2 us: fill_group(): jnp.einsum('rkt,btp->rbkp', transform, windowed, preferred_element_type=j...]
    gather x96 -> x0, local copies, waits for them, and re-layouts: 76.2 us -> none
    reshape x1 -> x0, local copies, waits for them, and re-layouts: 49.9 us -> none  [local_gram(): spectra.reshape(2 * spectra.shape[1], spectra.shape[2], spectra.shape[3])]
    all_to_all x1 -> x0, waiting for transfers between devices: 47.5 us -> none  [shards(): lax.all_to_all(anomaly, 'tm', split_axis=1, concat_axis=0, tiled=True)]
    ppermute x0 -> x14, waiting for transfers between devices: none -> 41.3 us  [the longest x12 35.7 us: tm_swap(): return lax.ppermute(value, 'tm', [(i, i ^ bit) for i in range(n)])]
    all_to_all x2 -> x0, local copies, waits for them, and re-layouts: 33.2 us -> none  [the longest x1 30 us: shards(): lax.all_to_all(spectra, 'tm', split_axis=2, concat_axis=3, tiled=True)]
  transfers between devices with their start and end apart: 2 -> 14, of which waited for: 2 -> 11; matrix products, arithmetic and copies ran while one was open for 0% -> 3% of each run, Pallas kernels for 0% -> 0%
where the time goes in v1:
time: 83.7 us; the launch traced here: 83.5 us
  waiting for transfers between devices  41.3 us (49%)
  starting transfers between devices  30.3 us (36%)
  Pallas kernels  5.34 us (6%)
  other arithmetic  3.31 us (4%)
  local copies, waits for them, and re-layouts  2.48 us (3%)
    ppermute x12, waiting for transfers between devices, tm_swap(): return lax.ppermute(value, 'tm', [(i, i ^ bit) for i in range(n)])  35.7 us
    ppermute x12, starting transfers between devices, tm_swap(): return lax.ppermute(value, 'tm', [(i, i ^ bit) for i in range(n)])  27 us
    ppermute x2, waiting for transfers between devices, pix_swap(): return lax.ppermute(value, 'pix', [(0, 1), (1, 0)])  5.52 us
    ppermute x2, starting transfers between devices, pix_swap(): return lax.ppermute(value, 'pix', [(0, 1), (1, 0)])  3.28 us
    pallas_call x1, Pallas kernels, covariance_shards(): pl.pallas_call(functools.partial(finish_kernel, tiles, 1.0 / total_pixels...  2.82 us
    pallas_call x1, Pallas kernels, covariance_shards(): pl.pallas_call(functools.partial(covariance_kernel, tiles), out_shape=(ja...  2.51 us
    dynamic_slice x1, local copies, waits for them, and re-layouts, covariance_shards(): lax.dynamic_slice_in_dim(anomaly, (me ^ d) * width, width, 1)  2.43 us
  transfers between devices with their start and end apart: 14, of which 11 were waited for; matrix products, arithmetic and copies ran while one was open for 3% of the time, Pallas kernels for 0%

profile of v1, /device:TPU:0, one launch (start us, length us, event | category | flops | bytes accessed | tf_op | source)
XLA Modules:
  0.0 83.5 jit_solution(5341488226087382748)
XLA Ops:
  0.7 0.0 copy-start.2
  0.7 0.0 copy-start.3
  0.7 0.0 copy-start
  0.7 0.0 copy-start.1
  0.7 2.4 %constant_dynamic-slice_fusion = (bf16[64,2048]{1,0:T(8,128)(2,1)S(1)}, bf16[64,2048]{1,0:T(8,128)(2,1)S(1)}, bf16[64,2048]{1,0:T(8,128)(2,1)S(1)}, bf16[64,2048...) fusion(bf16[64,16384]{1,0:T(8,128)(2,1)} %param.6, ...), kind=kLoop, calls=%fused_computation.38 | loop fusion | bytes 4194336 | tf_op jit(solution)/shard_map/dynamic_slice | solution.py:206
  3.2 0.5 collective-permute-start
  3.6 2.6 %collective-permute-start.1 = (bf16[64,2048]{1,0:T(8,128)(2,1)S(1)}, bf16[64,2048]{1,0:T(8,128)(2,1)S(1)}, u32[]{:S(2)}, u32[]{:S(2)}) collective-permute-start(bf16[64,2048]{1,0:T(8,128)(2,1)S(1)} %get-tuple-element.22), channel_id=1, source_target_pairs={{0,4},{2,6},{4,0},{6,2},{8,12},{10,14},{12,8},{14,10},{1,5},{3,7},... | collective-permute-start | bytes 786440 | tf_op jit(solution)/shard_map/ppermute | solution.py:199
  6.2 0.1 collective-permute-start.2
  6.3 2.7 %collective-permute-start.3 = (bf16[64,2048]{1,0:T(8,128)(2,1)S(1)}, bf16[64,2048]{1,0:T(8,128)(2,1)S(1)}, u32[]{:S(2)}, u32[]{:S(2)}) collective-permute-start(bf16[64,2048]{1,0:T(8,128)(2,1)S(1)} %get-tuple-element.20), channel_id=1, source_target_pairs={{0,8},{2,10},{4,12},{6,14},{8,0},{10,2},{12,4},{14,6},{1,9},{3,11}... | collective-permute-start | bytes 786440 | tf_op jit(solution)/shard_map/ppermute | solution.py:199
  9.1 0.0 collective-permute-start.4
  9.1 0.0 collective-permute-done.refs_1_
  9.1 3.6 %collective-permute-start.5 = (bf16[64,2048]{1,0:T(8,128)(2,1)S(1)}, bf16[64,2048]{1,0:T(8,128)(2,1)S(1)}, u32[]{:S(2)}, u32[]{:S(2)}) collective-permute-start(bf16[64,2048]{1,0:T(8,128)(2,1)S(1)} %get-tuple-element.25), channel_id=1, source_target_pairs={{0,12},{2,14},{4,8},{6,10},{8,4},{10,6},{12,0},{14,2},{1,13},{3,15... | collective-permute-start | bytes 786440 | tf_op jit(solution)/shard_map/ppermute | solution.py:199
  12.7 11.5 %collective-permute-done.1.refs_2_ = bf16[64,2048]{1,0:T(8,128)(2,1)S(1)} collective-permute-done((bf16[64,2048]{1,0:T(8,128)(2,1)S(1)}, bf16[64,2048]{1,0:T(8,128)(2,1)S(1)}, u32[]{:S(2)}, u32[]{:S(2)}) %collective-permute-start.1) | collective-permute-done | bytes 262176 | tf_op jit(solution)/shard_map/ppermute | solution.py:199
  24.2 0.5 collective-permute-start.6
  24.7 0.0 copy-done.2
  24.7 0.0 copy-done.3
  24.7 0.9 %multiply_reduce_fusion = f32[32]{0:T(128)S(1)} fusion(pred[32]{0:T(512)(128)(4,1)S(1)} %get-tuple-element.32, pred[32]{0:T(512)(128)(4,1)S(1)} %get-tuple-element.33, pred[32]{0:T(512)(128)(4,1)S(1)} %get-tuple-element.31, pred[32]{0:T(512)(128)(4,1)S(1)} %get-tuple-element.30, s32[32]{0:T(128)S(1)} %copy-done.3), kind=kLoop, calls=%fused_computation.10 | loop fusion | flops 425952 | bytes 384 | tf_op jit(solution)/shard_map/reduce_sum | solution.py:118
  25.6 0.1 pad_add_fusion.place
  25.6 3.7 %collective-permute-done.2.refs_3_ = bf16[64,2048]{1,0:T(8,128)(2,1)S(1)} collective-permute-done((bf16[64,2048]{1,0:T(8,128)(2,1)}, bf16[64,2048]{1,0:T(8,128)(2,1)S(1)}, u32[]{:S(2)}, u32[]{:S(2)}) %collective-permute-start.2) | collective-permute-done | bytes 262176 | tf_op jit(solution)/shard_map/ppermute | solution.py:199
  29.3 0.0 collective-permute-done.3.refs_4_
  29.3 0.5 collective-permute-done.4.refs_5_
  29.8 8.6 %collective-permute-done.5.refs_6_ = bf16[64,2048]{1,0:T(8,128)(2,1)S(1)} collective-permute-done((bf16[64,2048]{1,0:T(8,128)(2,1)S(1)}, bf16[64,2048]{1,0:T(8,128)(2,1)S(1)}, u32[]{:S(2)}, u32[]{:S(2)}) %collective-permute-start.5) | collective-permute-done | bytes 262176 | tf_op jit(solution)/shard_map/ppermute | solution.py:199
  38.4 4.7 %collective-permute-done.6.refs_7_ = bf16[64,2048]{1,0:T(8,128)(2,1)S(1)} collective-permute-done((bf16[64,2048]{1,0:T(8,128)(2,1)S(1)}, bf16[64,2048]{1,0:T(8,128)(2,1)S(1)}, u32[]{:S(2)}, u32[]{:S(2)}) %collective-permute-start.6) | collective-permute-done | bytes 262176 | tf_op jit(solution)/shard_map/ppermute | solution.py:199
  43.1 0.0 copy-done
  43.1 0.0 copy-done.1
  43.1 2.5 %shard_map.77 = (f32[10,64,128]{2,1,0:T(8,128)S(1)}, bf16[10,64,128]{2,1,0:T(8,128)(2,1)S(1)}) custom-call(s32[2]{0:T(128)S(1)} %pad_add_fusion.place, bf16[64,2048]{1,0:T(8,128)(2,1)S(1)} %get-tuple-element.24.refs_0_, bf16[64,2048]{1,0:T(8,128)(2,1)S(1)} %collective-permute-done.refs_1_, bf16[64,2048]{1,0:T(8,128)(2,1)S(1)} %collective-permute-done.1.refs_2_, ...), custom_call_target="tpu_custom_call" | custom-call | tf_op jit(solution)/shard_map/pallas_call | solution.py:215
  45.6 1.3 %collective-permute-start.7 = (bf16[10,64,128]{2,1,0:T(8,128)(2,1)S(1)}, bf16[10,64,128]{2,1,0:T(8,128)(2,1)S(1)}, u32[]{:S(2)}, u32[]{:S(2)}) collective-permute-start(bf16[10,64,128]{2,1,0:T(8,128)(2,1)S(1)} %get-tuple-element.15), channel_id=1, source_target_pairs={{0,2},{2,0},{4,6},{6,4},{8,10},{10,8},{12,14},{14,12},{1,3},{3,1},... | collective-permute-start | bytes 491528 | tf_op jit(solution)/shard_map/ppermute | solution.py:199
  46.9 0.0 copy-done.4
  46.9 0.8 multiply_multiply_fusion
  47.7 0.2 collective-permute-done.7
  48.0 1.7 %collective-permute-start.8 = (bf16[10,32,128]{2,1,0:T(8,128)(2,1)S(1)}, bf16[10,32,128]{2,1,0:T(8,128)(2,1)S(1)}, u32[]{:S(2)}, u32[]{:S(2)}) collective-permute-start(bf16[10,32,128]{2,1,0:T(8,128)(2,1)S(1)} %dynamic-slice_convert_fusion), channel_id=1, source_target_pairs={{0,1},{1,0},{2,3},{3,2},{4,5},{5,4},{6,7},{7,6},{8,9},{9,8},{10,11... | collective-permute-start | bytes 245768 | tf_op jit(solution)/shard_map/ppermute | solution.py:202
  49.7 3.1 %collective-permute-done.8 = bf16[10,32,128]{2,1,0:T(8,128)(2,1)S(1)} collective-permute-done((bf16[10,32,128]{2,1,0:T(8,128)(2,1)S(1)}, bf16[10,32,128]{2,1,0:T(8,128)(2,1)S(1)}, u32[]{:S(2)}, u32[]{:S(2)}) %collective-permute-start.8) | collective-permute-done | bytes 81952 | tf_op jit(solution)/shard_map/ppermute | solution.py:202
  52.8 12.0 %collective-permute-start.9 = (bf16[10,32,128]{2,1,0:T(8,128)(2,1)S(1)}, bf16[10,32,128]{2,1,0:T(8,128)(2,1)S(1)}, u32[]{:S(2)}, u32[]{:S(2)}) collective-permute-start(bf16[10,32,128]{2,1,0:T(8,128)(2,1)S(1)} %fusion.4), channel_id=1, source_target_pairs={{0,4},{2,6},{4,0},{6,2},{8,12},{10,14},{12,8},{14,10},{1,5},{3,7},... | collective-permute-start | bytes 245768 | tf_op jit(solution)/shard_map/ppermute | solution.py:199
  64.8 0.2 fusion.11
  65.0 2.2 %collective-permute-done.9 = bf16[10,32,128]{2,1,0:T(8,128)(2,1)S(1)} collective-permute-done((bf16[10,32,128]{2,1,0:T(8,128)(2,1)S(1)}, bf16[10,32,128]{2,1,0:T(8,128)(2,1)S(1)}, u32[]{:S(2)}, u32[]{:S(2)}) %collective-permute-start.9) | collective-permute-done | bytes 81952 | tf_op jit(solution)/shard_map/ppermute | solution.py:199
  67.2 3.7 %collective-permute-start.10 = (bf16[10,32,128]{2,1,0:T(8,128)(2,1)S(1)}, bf16[10,32,128]{2,1,0:T(8,128)(2,1)S(1)}, u32[]{:S(2)}, u32[]{:S(2)}) collective-permute-start(bf16[10,32,128]{2,1,0:T(8,128)(2,1)S(1)} %fusion), channel_id=1, source_target_pairs={{0,8},{2,10},{4,12},{6,14},{8,0},{10,2},{12,4},{14,6},{1,9},{3,11}... | collective-permute-start | bytes 245768 | tf_op jit(solution)/shard_map/ppermute | solution.py:199
  70.9 0.1 fusion.16
  71.0 3.2 %collective-permute-done.10 = bf16[10,32,128]{2,1,0:T(8,128)(2,1)S(1)} collective-permute-done((bf16[10,32,128]{2,1,0:T(8,128)(2,1)S(1)}, bf16[10,32,128]{2,1,0:T(8,128)(2,1)S(1)}, u32[]{:S(2)}, u32[]{:S(2)}) %collective-permute-start.10) | collective-permute-done | bytes 81952 | tf_op jit(solution)/shard_map/ppermute | solution.py:199
  74.3 1.6 %collective-permute-start.11 = (bf16[10,32,128]{2,1,0:T(8,128)(2,1)S(1)}, bf16[10,32,128]{2,1,0:T(8,128)(2,1)S(1)}, u32[]{:S(2)}, u32[]{:S(2)}) collective-permute-start(bf16[10,32,128]{2,1,0:T(8,128)(2,1)S(1)} %add_convert_fusion.q0), channel_id=1, source_target_pairs={{0,1},{1,0},{2,3},{3,2},{4,5},{5,4},{6,7},{7,6},{8,9},{9,8},{10,11... | collective-permute-start | bytes 245768 | tf_op jit(solution)/shard_map/ppermute | solution.py:202
  75.8 0.4 multiply_convert_fusion.1
  76.2 0.1 collective-permute-start.12
  76.3 2.5 %collective-permute-done.11.q1 = bf16[10,32,128]{2,1,0:T(8,128)(2,1)S(1)} collective-permute-done((bf16[10,32,128]{2,1,0:T(8,128)(2,1)S(1)}, bf16[10,32,128]{2,1,0:T(8,128)(2,1)S(1)}, u32[]{:S(2)}, u32[]{:S(2)}) %collective-permute-start.11) | collective-permute-done | bytes 81952 | tf_op jit(solution)/shard_map/ppermute | solution.py:202
  78.8 0.0 collective-permute-start.13
  78.8 0.1 pad_maximum_fusion.w
  78.9 0.0 collective-permute-done.12.q2
  78.9 1.2 %collective-permute-done.13.q3 = bf16[10,32,128]{2,1,0:T(8,128)(2,1)S(1)} collective-permute-done((bf16[10,32,128]{2,1,0:T(8,128)(2,1)S(1)}, bf16[10,32,128]{2,1,0:T(8,128)(2,1)S(1)}, u32[]{:S(2)}, u32[]{:S(2)}) %collective-permute-start.13) | collective-permute-done | bytes 81952 | tf_op jit(solution)/shard_map/ppermute | solution.py:199
  80.0 2.8 %shard_map.78 = (f32[16,64,64]{2,1,0:T(8,128)}, f32[16,1]{1,0:T(8,128)S(1)}) custom-call(s32[2]{0:T(128)S(1)} %pad_add_fusion.place, bf16[16,64,512]{2,1,0:T(8,128)(2,1)S(1)} %pad_maximum_fusion.w, bf16[10,32,128]{2,1,0:T(8,128)(2,1)S(1)} %add_convert_fusion.q0, bf16[10,32,128]{2,1,0:T(8,128)(2,1)S(1)} %collective-permute-done.11.q1, ...), custom_call_target="tpu_custom_call" | custom-call | tf_op jit(solution)/shard_map/pallas_call | solution.py:243
  82.9 0.6 reduce
  (9 shorter events, 0.2 us)
Async XLA Ops:
  0.7 24.0 %copy-start.2 = (s32[32]{0:T(128)S(1)}, s32[32]{0:T(128)}, u32[]{:S(2)}) copy-start(s32[32]{0:T(128)} %param.8) | copy-start | bytes 388
  0.7 24.0 %copy-start.3 = (s32[32]{0:T(128)S(1)}, s32[32]{0:T(128)}, u32[]{:S(2)}) copy-start(s32[32]{0:T(128)} %param.7) | copy-start | bytes 388
  0.7 42.4 %copy-start = (f32[512,1]{1,0:T(8,128)S(1)}, f32[512,1]{1,0:T(8,128)}, u32[]{:S(2)}) copy-start(f32[512,1]{1,0:T(8,128)} %constant.92.clone.refs_9_) | copy-start | bytes 6148
  0.7 42.4 %copy-start.1 = (f32[1,512]{1,0:T(1,128)S(1)}, f32[1,512]{1,0:T(1,128)}, u32[]{:S(2)}) copy-start(f32[1,512]{1,0:T(1,128)} %constant.91.clone.refs_8_) | copy-start | bytes 6148
  3.1 43.8 %copy-start.4 = (f32[512]{0:T(512)S(1)}, f32[512]{0:T(512)}, u32[]{:S(2)}) copy-start(f32[512]{0:T(512)} %constant.93) | copy-start | bytes 6148
  3.2 5.9 %collective-permute-start = (bf16[64,2048]{1,0:T(8,128)(2,1)S(1)}, bf16[64,2048]{1,0:T(8,128)(2,1)S(1)}, u32[]{:S(2)}, u32[]{:S(2)}) collective-permute-start(bf16[64,2048]{1,0:T(8,128)(2,1)S(1)} %get-tuple-element.23), channel_id=1, source_target_pairs={{0,2},{2,0},{4,6},{6,4},{8,10},{10,8},{12,14},{14,12},{1,3},{3,1},... | collective-permute-start | bytes 786440 | tf_op jit(solution)/shard_map/ppermute | solution.py:199
  3.6 20.6 %collective-permute-start.1 = (bf16[64,2048]{1,0:T(8,128)(2,1)S(1)}, bf16[64,2048]{1,0:T(8,128)(2,1)S(1)}, u32[]{:S(2)}, u32[]{:S(2)}) collective-permute-start(bf16[64,2048]{1,0:T(8,128)(2,1)S(1)} %get-tuple-element.22), channel_id=1, source_target_pairs={{0,4},{2,6},{4,0},{6,2},{8,12},{10,14},{12,8},{14,10},{1,5},{3,7},... | collective-permute-start | bytes 786440 | tf_op jit(solution)/shard_map/ppermute | solution.py:199
  6.2 23.0 %collective-permute-start.2 = (bf16[64,2048]{1,0:T(8,128)(2,1)}, bf16[64,2048]{1,0:T(8,128)(2,1)S(1)}, u32[]{:S(2)}, u32[]{:S(2)}) collective-permute-start(bf16[64,2048]{1,0:T(8,128)(2,1)} %get-tuple-element.21), channel_id=1, source_target_pairs={{0,6},{2,4},{4,2},{6,0},{8,14},{10,12},{12,10},{14,8},{1,7},{3,5},... | collective-permute-start | bytes 786440 | tf_op jit(solution)/shard_map/ppermute | solution.py:199
  6.3 23.0 %collective-permute-start.3 = (bf16[64,2048]{1,0:T(8,128)(2,1)S(1)}, bf16[64,2048]{1,0:T(8,128)(2,1)S(1)}, u32[]{:S(2)}, u32[]{:S(2)}) collective-permute-start(bf16[64,2048]{1,0:T(8,128)(2,1)S(1)} %get-tuple-element.20), channel_id=1, source_target_pairs={{0,8},{2,10},{4,12},{6,14},{8,0},{10,2},{12,4},{14,6},{1,9},{3,11}... | collective-permute-start | bytes 786440 | tf_op jit(solution)/shard_map/ppermute | solution.py:199
  9.1 20.7 %collective-permute-start.4 = (bf16[64,2048]{1,0:T(8,128)(2,1)S(1)}, bf16[64,2048]{1,0:T(8,128)(2,1)S(1)}, u32[]{:S(2)}, u32[]{:S(2)}) collective-permute-start(bf16[64,2048]{1,0:T(8,128)(2,1)S(1)} %get-tuple-element.19), channel_id=1, source_target_pairs={{0,10},{2,8},{4,14},{6,12},{8,2},{10,0},{12,6},{14,4},{1,11},{3,9}... | collective-permute-start | bytes 786440 | tf_op jit(solution)/shard_map/ppermute | solution.py:199
  9.1 29.3 %collective-permute-start.5 = (bf16[64,2048]{1,0:T(8,128)(2,1)S(1)}, bf16[64,2048]{1,0:T(8,128)(2,1)S(1)}, u32[]{:S(2)}, u32[]{:S(2)}) collective-permute-start(bf16[64,2048]{1,0:T(8,128)(2,1)S(1)} %get-tuple-element.25), channel_id=1, source_target_pairs={{0,12},{2,14},{4,8},{6,10},{8,4},{10,6},{12,0},{14,2},{1,13},{3,15... | collective-permute-start | bytes 786440 | tf_op jit(solution)/shard_map/ppermute | solution.py:199
  24.2 18.9 %collective-permute-start.6 = (bf16[64,2048]{1,0:T(8,128)(2,1)S(1)}, bf16[64,2048]{1,0:T(8,128)(2,1)S(1)}, u32[]{:S(2)}, u32[]{:S(2)}) collective-permute-start(bf16[64,2048]{1,0:T(8,128)(2,1)S(1)} %get-tuple-element.18), channel_id=1, source_target_pairs={{0,14},{2,12},{4,10},{6,8},{8,6},{10,4},{12,2},{14,0},{1,15},{3,13... | collective-permute-start | bytes 786440 | tf_op jit(solution)/shard_map/ppermute | solution.py:199
  45.6 2.3 %collective-permute-start.7 = (bf16[10,64,128]{2,1,0:T(8,128)(2,1)S(1)}, bf16[10,64,128]{2,1,0:T(8,128)(2,1)S(1)}, u32[]{:S(2)}, u32[]{:S(2)}) collective-permute-start(bf16[10,64,128]{2,1,0:T(8,128)(2,1)S(1)} %get-tuple-element.15), channel_id=1, source_target_pairs={{0,2},{2,0},{4,6},{6,4},{8,10},{10,8},{12,14},{14,12},{1,3},{3,1},... | collective-permute-start | bytes 491528 | tf_op jit(solution)/shard_map/ppermute | solution.py:199
  48.0 4.8 %collective-permute-start.8 = (bf16[10,32,128]{2,1,0:T(8,128)(2,1)S(1)}, bf16[10,32,128]{2,1,0:T(8,128)(2,1)S(1)}, u32[]{:S(2)}, u32[]{:S(2)}) collective-permute-start(bf16[10,32,128]{2,1,0:T(8,128)(2,1)S(1)} %dynamic-slice_convert_fusion), channel_id=1, source_target_pairs={{0,1},{1,0},{2,3},{3,2},{4,5},{5,4},{6,7},{7,6},{8,9},{9,8},{10,11... | collective-permute-start | bytes 245768 | tf_op jit(solution)/shard_map/ppermute | solution.py:202
  52.8 14.4 %collective-permute-start.9 = (bf16[10,32,128]{2,1,0:T(8,128)(2,1)S(1)}, bf16[10,32,128]{2,1,0:T(8,128)(2,1)S(1)}, u32[]{:S(2)}, u32[]{:S(2)}) collective-permute-start(bf16[10,32,128]{2,1,0:T(8,128)(2,1)S(1)} %fusion.4), channel_id=1, source_target_pairs={{0,4},{2,6},{4,0},{6,2},{8,12},{10,14},{12,8},{14,10},{1,5},{3,7},... | collective-permute-start | bytes 245768 | tf_op jit(solution)/shard_map/ppermute | solution.py:199
  67.2 7.0 %collective-permute-start.10 = (bf16[10,32,128]{2,1,0:T(8,128)(2,1)S(1)}, bf16[10,32,128]{2,1,0:T(8,128)(2,1)S(1)}, u32[]{:S(2)}, u32[]{:S(2)}) collective-permute-start(bf16[10,32,128]{2,1,0:T(8,128)(2,1)S(1)} %fusion), channel_id=1, source_target_pairs={{0,8},{2,10},{4,12},{6,14},{8,0},{10,2},{12,4},{14,6},{1,9},{3,11}... | collective-permute-start | bytes 245768 | tf_op jit(solution)/shard_map/ppermute | solution.py:199
  74.3 4.5 %collective-permute-start.11 = (bf16[10,32,128]{2,1,0:T(8,128)(2,1)S(1)}, bf16[10,32,128]{2,1,0:T(8,128)(2,1)S(1)}, u32[]{:S(2)}, u32[]{:S(2)}) collective-permute-start(bf16[10,32,128]{2,1,0:T(8,128)(2,1)S(1)} %add_convert_fusion.q0), channel_id=1, source_target_pairs={{0,1},{1,0},{2,3},{3,2},{4,5},{5,4},{6,7},{7,6},{8,9},{9,8},{10,11... | collective-permute-start | bytes 245768 | tf_op jit(solution)/shard_map/ppermute | solution.py:202
  76.2 2.7 %collective-permute-start.12 = (bf16[10,32,128]{2,1,0:T(8,128)(2,1)S(1)}, bf16[10,32,128]{2,1,0:T(8,128)(2,1)S(1)}, u32[]{:S(2)}, u32[]{:S(2)}) collective-permute-start(bf16[10,32,128]{2,1,0:T(8,128)(2,1)S(1)} %add_convert_fusion.q0), channel_id=1, source_target_pairs={{0,2},{2,0},{4,6},{6,4},{8,10},{10,8},{12,14},{14,12},{1,3},{3,1},... | collective-permute-start | bytes 245768 | tf_op jit(solution)/shard_map/ppermute | solution.py:199
  78.8 1.3 %collective-permute-start.13 = (bf16[10,32,128]{2,1,0:T(8,128)(2,1)S(1)}, bf16[10,32,128]{2,1,0:T(8,128)(2,1)S(1)}, u32[]{:S(2)}, u32[]{:S(2)}) collective-permute-start(bf16[10,32,128]{2,1,0:T(8,128)(2,1)S(1)} %collective-permute-done.11.q1), channel_id=1, source_target_pairs={{0,2},{2,0},{4,6},{6,4},{8,10},{10,8},{12,14},{14,12},{1,3},{3,1},... | collective-permute-start | bytes 245768 | tf_op jit(solution)/shard_map/ppermute | solution.py:199

commit v2 on v0

--- a/solution.py
+++ b/solution.py
@@ -1,15 +1,20 @@
+import functools
 import math
 
 import jax
 import jax.numpy as jnp
+import numpy as np
 from jax import lax
+from jax.experimental import pallas as pl
+from jax.experimental.pallas import tpu as pltpu
 from jax.sharding import PartitionSpec as P
 
 NFFT = 256
 NB = 32
 POWER = 8
 NF = 128
-
+VMEM_BYTES = 40 * 1024 * 1024
+OWN_FLOPS, EARLY_FLOPS, LATE_FLOPS, FINISH_FLOPS = 0, 0, 20_000_000_000, 1_000_000_000
 
 power_eps = 1e-06
 
@@ -44,7 +49,7 @@
     return jnp.einsum("ifp,jfp->fij", stacked, stacked, preferred_element_type=jnp.float32)
 
 
-def shards(anomaly, offsets, taper_index):
+def spectra_shards(anomaly, offsets, taper_index):
     series = lax.all_to_all(anomaly, "tm", split_axis=1, concat_axis=0, tiled=True)
     windows = window_rows(taper_index, NFFT)
     energy = 1.0 / jnp.sqrt(jnp.sum(windows * windows, axis=1))
@@ -84,8 +89,242 @@
     return (spectral_gram, leading_energy)
 
 
+def day_factors(days):
+    return (1.0 + 0.4 * ((np.arange(days) * 0.6180339887498949) % 1.0)).astype(np.float32)
+
+
+def day_order(rows):
+    blocks = [4 * half + 2 * chip + core for half in (0, 1) for core in (0, 1) for chip in (0, 1)]
+    return np.concatenate([np.arange(rows) + rows * block for block in blocks]).astype(np.int32)
+
+
+def weights(offsets, taper_index, first_freq, freqs, order):
+    days = order.shape[0]
+    day = jnp.asarray(order)
+    local = day[None, :] - offsets[:, None]
+    inside = (local >= 0) & (local < NFFT)
+    steps_t = local.astype(jnp.float32)
+    phase = steps_t * (2.0 * math.pi / NFFT)
+    center = (steps_t + 0.5) * (math.pi / NFFT)
+    sine_win = jnp.sin(center)
+    table = [
+        sine_win**2,
+        0.54 - 0.46 * jnp.cos(phase),
+        0.42 - 0.5 * jnp.cos(phase) + 0.08 * jnp.cos(2.0 * phase),
+        sine_win,
+    ]
+    window = jnp.zeros(local.shape, jnp.float32)
+    for which in range(4):
+        window = window + jnp.where(taper_index[:, None] == which, table[which], 0.0)
+    window = jnp.where(inside, window, 0.0)
+    energy = 1.0 / jnp.sqrt(jnp.sum(window * window, axis=1, keepdims=True))
+    factors = day_factors(days // 2)
+    window = window * energy * (1.0 / np.concatenate([factors, factors]))[None, :]
+
+    def turn(steps):
+        freq = first_freq + jnp.arange(freqs, dtype=jnp.int32)
+        angle = ((freq[:, None] * steps[None, :]) % NFFT).astype(jnp.float32)
+        angle = angle * (2.0 * math.pi / NFFT)
+        return jnp.cos(angle), jnp.sin(angle)
+
+    cos_t, sin_t = lax.optimization_barrier(turn(day))
+    cos_b, sin_b = lax.optimization_barrier(turn(offsets))
+    window = lax.optimization_barrier(window)
+    ct, st = cos_t[:, None, :], sin_t[:, None, :]
+    cb, sb = cos_b[:, :, None], sin_b[:, :, None]
+    real = window * (ct * cb + st * sb)
+    imag = window * (ct * sb - st * cb)
+    return jnp.concatenate([real, imag], axis=1).astype(jnp.bfloat16)
+
+
+def outer(left, right):
+    return lax.dot_general(left, right, (((1,), (1,)), ((), ())), preferred_element_type=jnp.float32)
+
+
+def spread(pair, chip):
+    low = lax.broadcasted_iota(jnp.int32, pair.shape, 1) < pair.shape[1] // 2
+    turned = pltpu.roll(pair, pair.shape[1] // 2, 1)
+    first = jnp.where(chip == 0, pair, turned)
+    second = jnp.where(chip == 0, turned, pair)
+    keep = low == (chip == 0)
+    return jnp.concatenate([jnp.where(keep, first, 0.0), jnp.where(keep, second, 0.0)], axis=1)
+
+
+def block(index, rows):
+    return pl.ds(pl.multiple_of(index * rows, rows), rows)
+
+
+def own_kernel(place, p0, p1, p2a, p2b, p3a, p3b, f0a, f0b, f1a, f1b, drow, dcol, dpair, near, keep, send, pair, strip):
+    chip, core = place[1], place[2]
+    slot = 2 * core + chip
+    rows, middle = p2a.shape
+    near[block(slot, rows), :] = p0[...]
+    near[block(slot ^ 2, rows), :] = p1[...]
+    for flip, first, second in ((1, p2a, p2b), (3, p3a, p3b)):
+        near[block(slot ^ flip, rows), :middle] = first[...]
+        near[block(slot ^ flip, rows), middle:] = second[...]
+    mine = block(core, 2 * rows)
+    strip[...] = outer(near[mine, :], near[...]) * (0.5 * dcol[mine, :]) * drow[...]
+    width = f0a.shape[1]
+    for index, first, second in ((core, f0a, f0b), (1 - core, f1a, f1b)):
+        pair[block(index, rows), :width] = first[...]
+        pair[block(index, rows), width:] = second[...]
+    inside = outer(pair[block(core, rows), :], pair[...]) * (0.5 * dcol[block(slot, rows), :]) * dpair[chip]
+    keep[...] = strip[block(chip, rows), :] + spread(inside, chip)
+    send[...] = strip[block(1 - chip, rows), :].astype(jnp.bfloat16)
+
+
+def early_kernel(place, near, early, drow, dcol, out):
+    rows = early.shape[0]
+    slot = 2 * place[2] + 1 - place[1]
+    out[...] = (outer(early[...], near[...]) * dcol[block(slot, rows), :] * drow[...]).astype(jnp.bfloat16)
+
+
+def late_kernel(place, near, late, e0, e1, before, drow, dcol, dpair, out, pair):
+    rows, span = late.shape[0], near.shape[0]
+    chip, core = place[1], place[2]
+    scale = dcol[block(2 * core + chip, rows), :]
+    pair[block(core, rows), :] = e0[...]
+    pair[block(1 - core, rows), :] = e1[...]
+    cross = outer(late[...], near[...]) * scale * drow[...] + before[...].astype(jnp.float32)
+    out[:, :span] = cross.astype(jnp.bfloat16)
+    out[:, span:] = (outer(late[...], pair[...]) * scale * dpair[1 - chip]).astype(jnp.bfloat16)
+
+
+def finish_kernel(scale, place, w, *refs):
+    pieces, (gram, energy, table, y) = refs[:8], refs[8:]
+    rows, span = pieces[0].shape[0], table.shape[0] // 2
+    for d in range(8):
+        half, chip, core = place[0] ^ (d >> 2), place[1] ^ ((d >> 1) & 1), place[2] ^ (d & 1)
+        mine, other = pieces[d], pieces[d ^ 4]
+        at = block(4 * half + 2 * core + chip, rows)
+        extra = spread(other[:, 2 * span :].astype(jnp.float32), 1 - chip)
+        table[at, block(half, span)] = (mine[:, :span].astype(jnp.float32) + extra).astype(jnp.bfloat16)
+        table[at, block(1 - half, span)] = other[:, span : 2 * span]
+    freqs, width, days = w.shape
+    flat = w[...].reshape(freqs * width, days)
+    y[...] = jnp.dot(flat, table[...], preferred_element_type=jnp.float32).astype(jnp.bfloat16)
+    for f in range(freqs):
+        part = outer(y[f * width : (f + 1) * width, :], w[f]) * scale
+        gram[f] = part + part.T
+    g = gram[...]
+    vector = jnp.ones((freqs, 1, width), jnp.float32)
+    along = 2
+    for step in range(POWER + 1):
+        applied = jnp.sum(g * vector, axis=along, keepdims=True)
+        along = 3 - along
+        mean = jnp.sum(applied * applied, axis=along, keepdims=True) * (1.0 / width)
+        if step < POWER:
+            vector = applied / jnp.sqrt(mean + power_eps)
+    lane = lax.broadcasted_iota(jnp.int32, (freqs, 1, freqs), 2)
+    own = lax.broadcasted_iota(jnp.int32, (freqs, 1, freqs), 0)
+    energy[...] = jnp.sum(jnp.where(lane == own, jnp.sqrt(mean), 0.0), axis=0)
+
+
+def covariance_shards(anomaly, offsets, taper_index):
+    n = lax.axis_size("tm")
+    me = lax.axis_index("tm")
+    half, chip, core = me // 4, (me // 2) % 2, me % 2
+    place = jnp.stack([half, chip, core]).astype(jnp.int32)
+    rows, width = anomaly.shape
+    span, part = 4 * rows, width // 4
+    order = day_order(rows)
+    freqs = NF // n
+    bf16 = jnp.bfloat16
+
+    def tm_swap(value, bit):
+        return lax.ppermute(value, "tm", [(i, i ^ bit) for i in range(n)])
+
+    def pix_sum(value):
+        other = lax.ppermute(value, "pix", [(0, 1), (1, 0)])
+        return (value.astype(jnp.float32) + other.astype(jnp.float32)).astype(bf16)
+
+    def everyone(value):
+        s4, s2 = tm_swap(value, 4), tm_swap(value, 2)
+        s6 = tm_swap(s4, 2)
+        z = (value, s2, s4, s6)
+        return [v for pair in zip(z, [tm_swap(v, 1) for v in z]) for v in pair]
+
+    def cut(source, start, count):
+        return lax.optimization_barrier((source, lax.dynamic_slice_in_dim(source, start, count, 1)))
+
+    z = me // 2
+    source, far6 = cut(anomaly, (z ^ 3) * part, part)
+    source, home = cut(source, z * part, part)
+    early = tm_swap(far6, 6)
+    p1 = tm_swap(home, 1)
+    source, p1 = lax.optimization_barrier((source, p1))
+    source, side_a = cut(source, (z ^ 1) * part, part // 2)
+    source, side_b = cut(source, (z ^ 1) * part + part // 2, part // 2)
+    source, far_a = cut(source, (1 - half) * 2 * part, part)
+    source, far_b = cut(source, (1 - half) * 2 * part + part, part)
+    source, far4 = cut(source, (z ^ 2) * part, part)
+    late = tm_swap(far4, 4)
+    p2a, p2b = tm_swap(side_a, 2), tm_swap(side_b, 2)
+    fa, fb = tm_swap(far_a, 1), tm_swap(far_b, 1)
+    p2a, offsets, taper_index = lax.optimization_barrier((p2a, offsets, taper_index))
+    w = weights(offsets, taper_index, me * freqs, freqs, order)
+    p3a, p3b = tm_swap(p2a, 1), tm_swap(p2b, 1)
+    p3a, w = lax.optimization_barrier((p3a, w))
+
+    factors = day_factors(span)
+    first, second = factors[: 2 * rows].reshape(2, rows), factors[2 * rows :].reshape(2, rows)
+    pairs = np.concatenate([first, second], axis=1)[:, None, :]
+    drow, dcol, dpair = jnp.asarray(factors[None, :]), jnp.asarray(factors[:, None]), jnp.asarray(pairs)
+    vmem = pl.BlockSpec(memory_space=pltpu.VMEM)
+    smem = pl.BlockSpec(memory_space=pltpu.SMEM)
+
+    def call(kernel, flops, outs, scratch, *args):
+        return pl.pallas_call(
+            kernel,
+            out_shape=[jax.ShapeDtypeStruct(shape, kind) for shape, kind in outs],
+            in_specs=[smem] + [vmem] * len(args),
+            out_specs=[vmem] * len(outs),
+            scratch_shapes=[pltpu.VMEM(shape, kind) for shape, kind in scratch],
+            cost_estimate=pl.CostEstimate(flops=flops, bytes_accessed=0, transcendentals=0),
+            compiler_params=pltpu.CompilerParams(vmem_limit_bytes=VMEM_BYTES),
+        )(place, *args)
+
+    near, keep, send = call(
+        own_kernel,
+        OWN_FLOPS,
+        [((span, part), bf16), ((rows, span), jnp.float32), ((rows, span), bf16)],
+        [((2 * rows, 2 * part), bf16), ((2 * rows, span), jnp.float32)],
+        home, p1, p2a, p2b, p3a, p3b, far_a, far_b, fa, fb, drow, dcol, dpair,
+    )
+    mine = pix_sum((keep + tm_swap(send, 2).astype(jnp.float32)).astype(bf16))
+    e1 = tm_swap(early, 1)
+    (cross,) = call(early_kernel, EARLY_FLOPS, [((rows, span), bf16)], [], near, early, drow, dcol)
+    before = tm_swap(cross, 2)
+    (last,) = call(
+        late_kernel,
+        LATE_FLOPS,
+        [((rows, span + 2 * rows), bf16)],
+        [((2 * rows, part), bf16)],
+        near, late, early, e1, before, drow, dcol, dpair,
+    )
+    pieces = everyone(jnp.concatenate([mine, pix_sum(last)], axis=1))
+    gram_width = 2 * NB
+    total_pixels = width * lax.axis_size("pix")
+    gram, energy = call(
+        functools.partial(finish_kernel, 1.0 / total_pixels),
+        FINISH_FLOPS,
+        [((freqs, gram_width, gram_width), jnp.float32), ((1, freqs), jnp.float32)],
+        [((2 * span, 2 * span), bf16), ((freqs * gram_width, 2 * span), bf16)],
+        w, *pieces,
+    )
+    return gram, energy.reshape(freqs)
+
+
 def solution(mesh):
     placed = (P("tm", ("group", "pix", "sub")), P(), P())
+    pairs = mesh.shape["tm"] == 8 and mesh.shape["pix"] == 2 and mesh.shape["sub"] == 1
+
+    def shards(anomaly, offsets, taper_index):
+        if pairs and anomaly.shape[0] == 64 and anomaly.shape[1] % 512 == 0:
+            return covariance_shards(anomaly, offsets, taper_index)
+        return spectra_shards(anomaly, offsets, taper_index)
+
     return jax.shard_map(
         shards,
         mesh=mesh,

time: 1170 us -> 77.6 us (0.07)
  blocking collectives: 736 us -> 0 us
  local copies, waits for them, and re-layouts: 254 us -> 2.62 us
  matrix products: 80.2 us -> 0 us
  waiting for transfers between devices: 74.6 us -> 40 us
  starting transfers between devices: 6.36 us -> 21.9 us
  between operations: 14.2 us -> 0.96 us
    all_to_all x1 -> x0, blocking collectives: 736 us -> none  [shards(): lax.all_to_all(spectra, 'tm', split_axis=2, concat_axis=3, tiled=True)]
    dynamic_update_slice x8 -> x0, local copies, waits for them, and re-layouts: 83.1 us -> none  [fill_group(): return lax.dynamic_update_slice_in_dim(buffer, spectra, first_block, 1)]
    dot_general x14 -> x0, matrix products: 80.2 us -> none  [the longest x4 48.2 us: fill_group(): jnp.einsum('rkt,btp->rbkp', transform, windowed, preferred_element_type=j...]
    gather x96 -> x0, local copies, waits for them, and re-layouts: 76.2 us -> none
    reshape x1 -> x0, local copies, waits for them, and re-layouts: 49.9 us -> none  [local_gram(): spectra.reshape(2 * spectra.shape[1], spectra.shape[2], spectra.shape[3])]
    all_to_all x1 -> x0, waiting for transfers between devices: 47.5 us -> none  [shards(): lax.all_to_all(anomaly, 'tm', split_axis=1, concat_axis=0, tiled=True)]
    ppermute x0 -> x21, waiting for transfers between devices: none -> 40 us  [the longest x19 37.4 us: tm_swap(): return lax.ppermute(value, 'tm', [(i, i ^ bit) for i in range(n)])]
    all_to_all x2 -> x0, local copies, waits for them, and re-layouts: 33.2 us -> none  [the longest x1 30 us: shards(): lax.all_to_all(spectra, 'tm', split_axis=2, concat_axis=3, tiled=True)]
  transfers between devices with their start and end apart: 2 -> 21, of which waited for: 2 -> 9; matrix products, arithmetic and copies ran while one was open for 0% -> 4% of each run, Pallas kernels for 0% -> 7%
where the time goes in v2:
time: 77.6 us; the launch traced here: 77.4 us
  waiting for transfers between devices  40 us (52%)
  starting transfers between devices  21.9 us (28%)
  Pallas kernels  9.35 us (12%)
  local copies, waits for them, and re-layouts  2.62 us (3%)
  other arithmetic  2.59 us (3%)
  between operations  0.96 us (1%)
    ppermute x19, waiting for transfers between devices, tm_swap(): return lax.ppermute(value, 'tm', [(i, i ^ bit) for i in range(n)])  37.4 us
    ppermute x19, starting transfers between devices, tm_swap(): return lax.ppermute(value, 'tm', [(i, i ^ bit) for i in range(n)])  18.8 us
    pallas_call x4, Pallas kernels, call(): pl.pallas_call(kernel, out_shape=[jax.ShapeDtypeStruct(shape, kind) for s...  9.35 us
    ppermute x2, starting transfers between devices, pix_sum(): other = lax.ppermute(value, 'pix', [(0, 1), (1, 0)])  3.11 us
    ppermute x2, waiting for transfers between devices, pix_sum(): other = lax.ppermute(value, 'pix', [(0, 1), (1, 0)])  2.59 us
    unnamed x16, local copies, waits for them, and re-layouts  1.59 us
  transfers between devices with their start and end apart: 21, of which 9 were waited for; matrix products, arithmetic and copies ran while one was open for 4% of the time, Pallas kernels for 7%

profile of v2, /device:TPU:0, one launch (start us, length us, event | category | flops | bytes accessed | tf_op | source)
XLA Modules:
  0.0 77.4 jit_solution(501337384141297086)
XLA Ops:
  0.6 0.0 copy-start
  0.6 0.0 copy-start.4
  0.7 1.5 %copy-done = bf16[64,16384]{1,0:T(8,128)(2,1)S(1)} copy-done((bf16[64,16384]{1,0:T(8,128)(2,1)S(1)}, bf16[64,16384]{1,0:T(8,128)(2,1)}, u32[]{:S(2)}) %copy-start) | copy-done | bytes 2097176
  2.2 0.8 %constant_dynamic-slice_fusion.6 = bf16[64,4096]{1,0:T(8,128)(2,1)} fusion(bf16[64,16384]{1,0:T(8,128)(2,1)S(1)} %copy-done, s32[]{:T(128)S(6)} %select_n.73), kind=kLoop, calls=%fused_computation.61 | loop fusion | bytes 1048580 | tf_op jit(solution)/shard_map/dynamic_slice | solution.py:249
  3.1 0.5 collective-permute-start
  3.6 4.7 %collective-permute-start.10 = (bf16[64,4096]{1,0:T(8,128)(2,1)}, bf16[64,4096]{1,0:T(8,128)(2,1)S(1)}, u32[]{:S(2)}, u32[]{:S(2)}) collective-permute-start(bf16[64,4096]{1,0:T(8,128)(2,1)} %constant_dynamic-slice_fusion.6), channel_id=1, source_target_pairs={{0,12},{2,14},{4,8},{6,10},{8,4},{10,6},{12,0},{14,2},{1,13},{3,15... | collective-permute-start | bytes 1572872 | tf_op jit(solution)/shard_map/ppermute | solution.py:236
  8.3 0.2 fusion.26
  8.6 0.1 pad_add_fusion.place
  8.7 0.1 collective-permute-start.1
  8.8 2.1 %collective-permute-start.3 = (bf16[64,2048]{1,0:T(8,128)(2,1)S(1)}, bf16[64,2048]{1,0:T(8,128)(2,1)S(1)}, u32[]{:S(2)}, u32[]{:S(2)}) collective-permute-start(bf16[64,2048]{1,0:T(8,128)(2,1)S(1)} %constant_dynamic-slice_fusion.3), channel_id=1, source_target_pairs={{0,4},{2,6},{4,0},{6,2},{8,12},{10,14},{12,8},{14,10},{1,5},{3,7},... | collective-permute-start | bytes 786440 | tf_op jit(solution)/shard_map/ppermute | solution.py:236
  11.0 0.0 copy-start.1
  11.0 0.0 copy-start.2
  11.0 0.0 copy-start.3
  11.0 0.1 collective-permute-start.5
  11.1 0.5 collective-permute-start.6
  11.6 15.2 %collective-permute-done.1.p2a = bf16[64,2048]{1,0:T(8,128)(2,1)S(1)} collective-permute-done((bf16[64,2048]{1,0:T(8,128)(2,1)S(1)}, bf16[64,2048]{1,0:T(8,128)(2,1)S(1)}, u32[]{:S(2)}, u32[]{:S(2)}) %collective-permute-start.1) | collective-permute-done | bytes 262176 | tf_op jit(solution)/shard_map/ppermute | solution.py:236
  26.8 0.0 collective-permute-start.2
  26.8 0.1 fusion.31
  27.0 0.9 %multiply_reduce_fusion = f32[32]{0:T(128)S(1)} fusion(pred[32]{0:T(512)(128)(4,1)S(1)} %get-tuple-element.67, pred[32]{0:T(512)(128)(4,1)S(1)} %get-tuple-element.68, pred[32]{0:T(512)(128)(4,1)S(1)} %get-tuple-element.69, pred[32]{0:T(512)(128)(4,1)S(1)} %get-tuple-element.66, s32[32]{0:T(128)S(1)} %copy-done.6, s32[512]{0:T(512)S(1)} %copy-done.4), kind=kLoop, calls=%fused_computation.33 | loop fusion | flops 425952 | bytes 2432 | tf_op jit(solution)/shard_map/reduce_sum | solution.py:120
  27.9 0.8 %multiply_multiply_fusion = f32[32,512]{1,0:T(8,128)S(1)} fusion(f32[512]{0:T(512)S(1)} %copy-done.7, f32[32]{0:T(128)S(1)} %sqrt.3, pred[32]{0:T(512)(128)(4,1)S(1)} %get-tuple-element.67, pred[32]{0:T(512)(128)(4,1)S(1)} %get-tuple-element.68, pred[32]{0:T(512)(128)(4,1)S(1)} %get-tuple-element.69, pred[32]{0:T(512)(128)(4,1)S(1)} %get-tuple-element.66, ...), kind=kLoop, calls=%fused_computation.32 | loop fusion | flops 425984 | bytes 70016 | tf_op jit(solution)/shard_map/mul | solution.py:122
  28.6 4.4 %collective-permute-start.9 = (bf16[64,4096]{1,0:T(8,128)(2,1)S(1)}, bf16[64,4096]{1,0:T(8,128)(2,1)S(1)}, u32[]{:S(2)}, u32[]{:S(2)}) collective-permute-start(bf16[64,4096]{1,0:T(8,128)(2,1)S(1)} %constant_dynamic-slice_fusion), channel_id=1, source_target_pairs={{0,8},{2,10},{4,12},{6,14},{8,0},{10,2},{12,4},{14,6},{1,9},{3,11}... | collective-permute-start | bytes 1572872 | tf_op jit(solution)/shard_map/ppermute | solution.py:236
  33.0 0.0 collective-permute-done.3.p2b
  33.0 0.0 collective-permute-start.11
  33.0 0.0 collective-permute-done.2.p3a
  33.0 0.5 collective-permute-start.4
  33.5 0.4 multiply_convert_fusion.1
  33.9 0.1 pad_maximum_fusion.w
  34.0 1.3 %collective-permute-done.4.p3b = bf16[64,2048]{1,0:T(8,128)(2,1)S(1)} collective-permute-done((bf16[64,2048]{1,0:T(8,128)(2,1)S(1)}, bf16[64,2048]{1,0:T(8,128)(2,1)S(1)}, u32[]{:S(2)}, u32[]{:S(2)}) %collective-permute-start.4) | collective-permute-done | bytes 262176 | tf_op jit(solution)/shard_map/ppermute | solution.py:236
  35.3 0.0 collective-permute-done.5.f1a
  35.3 0.0 collective-permute-done.6.f1b
  35.3 2.7 %shard_map.95 = (bf16[256,4096]{1,0:T(8,128)(2,1)S(1)}, f32[64,256]{1,0:T(8,128)S(1)}, bf16[64,256]{1,0:T(8,128)(2,1)S(1)}) custom-call(s32[3]{0:T(128)S(1)} %pad_add_fusion.place, bf16[64,4096]{1,0:T(8,128)(2,1)S(1)} %constant_dynamic-slice_fusion.5.p0, bf16[64,4096]{1,0:T(8,128)(2,1)} %collective-permute-done.p1, ...), custom_call_target="tpu_custom_call" | custom-call | tf_op jit(solution)/shard_map/pallas_call | solution.py:278
  38.1 1.1 %collective-permute-start.7 = (bf16[64,256]{1,0:T(8,128)(2,1)S(1)}, bf16[64,256]{1,0:T(8,128)(2,1)S(1)}, u32[]{:S(2)}, u32[]{:S(2)}) collective-permute-start(bf16[64,256]{1,0:T(8,128)(2,1)S(1)} %get-tuple-element.53), channel_id=1, source_target_pairs={{0,4},{2,6},{4,0},{6,2},{8,12},{10,14},{12,8},{14,10},{1,5},{3,7},... | collective-permute-start | bytes 98312 | tf_op jit(solution)/shard_map/ppermute | solution.py:236
  39.2 1.3 %shard_map.96 = bf16[64,256]{1,0:T(8,128)(2,1)S(1)} custom-call(s32[3]{0:T(128)S(1)} %pad_add_fusion.place, bf16[256,4096]{1,0:T(8,128)(2,1)S(1)} %get-tuple-element.54.near, bf16[64,4096]{1,0:T(8,128)(2,1)S(1)} %collective-permute-done.10.early.e0, f32[1,256]{1,0:T(1,128)S(1)} %copy-done.2, f32[256,1]{1,0:T(8,128)S(1)} %copy-done.1), custom_call_target="tpu_custom_call" | custom-call | tf_op jit(solution)/shard_map/pallas_call | solution.py:278
  40.5 1.0 %collective-permute-start.12 = (bf16[64,256]{1,0:T(8,128)(2,1)S(1)}, bf16[64,256]{1,0:T(8,128)(2,1)S(1)}, u32[]{:S(2)}, u32[]{:S(2)}) collective-permute-start(bf16[64,256]{1,0:T(8,128)(2,1)S(1)} %shard_map.96), channel_id=1, source_target_pairs={{0,4},{2,6},{4,0},{6,2},{8,12},{10,14},{12,8},{14,10},{1,5},{3,7},... | collective-permute-start | bytes 98312 | tf_op jit(solution)/shard_map/ppermute | solution.py:236
  41.5 3.6 %collective-permute-done.7 = bf16[64,256]{1,0:T(8,128)(2,1)S(1)} collective-permute-done((bf16[64,256]{1,0:T(8,128)(2,1)S(1)}, bf16[64,256]{1,0:T(8,128)(2,1)S(1)}, u32[]{:S(2)}, u32[]{:S(2)}) %collective-permute-start.7) | collective-permute-done | bytes 32800 | tf_op jit(solution)/shard_map/ppermute | solution.py:236
  45.1 1.6 %collective-permute-start.8 = (bf16[64,256]{1,0:T(8,128)(2,1)S(1)}, bf16[64,256]{1,0:T(8,128)(2,1)S(1)}, u32[]{:S(2)}, u32[]{:S(2)}) collective-permute-start(bf16[64,256]{1,0:T(8,128)(2,1)S(1)} %add_convert_fusion.2), channel_id=1, source_target_pairs={{0,1},{1,0},{2,3},{3,2},{4,5},{5,4},{6,7},{7,6},{8,9},{9,8},{10,11... | collective-permute-start | bytes 98312 | tf_op jit(solution)/shard_map/ppermute | solution.py:239
  46.7 9.3 %collective-permute-done.9.late = bf16[64,4096]{1,0:T(8,128)(2,1)S(1)} collective-permute-done((bf16[64,4096]{1,0:T(8,128)(2,1)S(1)}, bf16[64,4096]{1,0:T(8,128)(2,1)S(1)}, u32[]{:S(2)}, u32[]{:S(2)}) %collective-permute-start.9) | collective-permute-done | bytes 524320 | tf_op jit(solution)/shard_map/ppermute | solution.py:236
  56.0 1.6 %shard_map.97 = bf16[64,384]{1,0:T(8,128)(2,1)S(1)} custom-call(s32[3]{0:T(128)S(1)} %pad_add_fusion.place, bf16[256,4096]{1,0:T(8,128)(2,1)S(1)} %get-tuple-element.54.near, bf16[64,4096]{1,0:T(8,128)(2,1)S(1)} %collective-permute-done.9.late, bf16[64,4096]{1,0:T(8,128)(2,1)S(1)} %collective-permute-done.10.early.e0, ...), custom_call_target="tpu_custom_call" | custom-call | flops 20000000000 | tf_op jit(solution)/shard_map/pallas_call | solution.py:278
  57.6 1.6 %collective-permute-start.13 = (bf16[64,384]{1,0:T(8,128)(2,1)S(1)}, bf16[64,384]{1,0:T(8,128)(2,1)S(1)}, u32[]{:S(2)}, u32[]{:S(2)}) collective-permute-start(bf16[64,384]{1,0:T(8,128)(2,1)S(1)} %shard_map.97), channel_id=1, source_target_pairs={{0,1},{1,0},{2,3},{3,2},{4,5},{5,4},{6,7},{7,6},{8,9},{9,8},{10,11... | collective-permute-start | bytes 147464 | tf_op jit(solution)/shard_map/ppermute | solution.py:239
  59.2 2.6 %collective-permute-done.13 = bf16[64,384]{1,0:T(8,128)(2,1)S(1)} collective-permute-done((bf16[64,384]{1,0:T(8,128)(2,1)S(1)}, bf16[64,384]{1,0:T(8,128)(2,1)S(1)}, u32[]{:S(2)}, u32[]{:S(2)}) %collective-permute-start.13) | collective-permute-done | bytes 49184 | tf_op jit(solution)/shard_map/ppermute | solution.py:239
  61.8 0.1 collective-permute-start.17
  61.9 3.3 %collective-permute-start.15 = (bf16[64,640]{1,0:T(8,128)(2,1)S(1)}, bf16[64,640]{1,0:T(8,128)(2,1)S(1)}, u32[]{:S(2)}, u32[]{:S(2)}) collective-permute-start(bf16[64,640]{1,0:T(8,128)(2,1)S(1)} %pad_maximum_fusion.1.refs_0_), channel_id=1, source_target_pairs={{0,4},{2,6},{4,0},{6,2},{8,12},{10,14},{12,8},{14,10},{1,5},{3,7},... | collective-permute-start | bytes 245768 | tf_op jit(solution)/shard_map/ppermute | solution.py:236
  65.2 2.8 %collective-permute-done.17.refs_4_ = bf16[64,640]{1,0:T(8,128)(2,1)S(1)} collective-permute-done((bf16[64,640]{1,0:T(8,128)(2,1)S(1)}, bf16[64,640]{1,0:T(8,128)(2,1)S(1)}, u32[]{:S(2)}, u32[]{:S(2)}) %collective-permute-start.17) | collective-permute-done | bytes 81952 | tf_op jit(solution)/shard_map/ppermute | solution.py:236
  68.0 0.5 collective-permute-start.18
  68.5 0.4 collective-permute-done.15.refs_2_
  68.9 3.6 %collective-permute-done.19.refs_6_ = bf16[64,640]{1,0:T(8,128)(2,1)S(1)} collective-permute-done((bf16[64,640]{1,0:T(8,128)(2,1)S(1)}, bf16[64,640]{1,0:T(8,128)(2,1)S(1)}, u32[]{:S(2)}, u32[]{:S(2)}) %collective-permute-start.19) | collective-permute-done | bytes 81952 | tf_op jit(solution)/shard_map/ppermute | solution.py:236
  72.5 1.3 %collective-permute-done.20.refs_7_ = bf16[64,640]{1,0:T(8,128)(2,1)S(1)} collective-permute-done((bf16[64,640]{1,0:T(8,128)(2,1)S(1)}, bf16[64,640]{1,0:T(8,128)(2,1)S(1)}, u32[]{:S(2)}, u32[]{:S(2)}) %collective-permute-start.20) | collective-permute-done | bytes 81952 | tf_op jit(solution)/shard_map/ppermute | solution.py:236
  73.7 3.7 %shard_map.98 = (f32[16,64,64]{2,1,0:T(8,128)}, f32[1,16]{1,0:T(1,128)}) custom-call(s32[3]{0:T(128)S(1)} %pad_add_fusion.place, bf16[16,64,512]{2,1,0:T(8,128)(2,1)S(1)} %pad_maximum_fusion.w, bf16[64,640]{1,0:T(8,128)(2,1)S(1)} %pad_maximum_fusion.1.refs_0_, bf16[64,640]{1,0:T(8,128)(2,1)S(1)} %collective-permute-done.14.refs_1_, ...), custom_call_target="tpu_custom_call" | custom-call | flops 1000000000 | tf_op jit(solution)/shard_map/pallas_call | solution.py:278
  (35 shorter events, 0.3 us)
Async XLA Ops:
  0.6 1.6 %copy-start = (bf16[64,16384]{1,0:T(8,128)(2,1)S(1)}, bf16[64,16384]{1,0:T(8,128)(2,1)}, u32[]{:S(2)}) copy-start(bf16[64,16384]{1,0:T(8,128)(2,1)} %param.8) | copy-start | bytes 6291460
  0.6 7.6 %copy-start.4 = (s32[512]{0:T(512)S(1)}, s32[512]{0:T(512)}, u32[]{:S(2)}) copy-start(s32[512]{0:T(512)} %constant.123.clone) | copy-start | bytes 6148
  3.1 5.5 %collective-permute-start = (bf16[64,4096]{1,0:T(8,128)(2,1)S(1)}, bf16[64,4096]{1,0:T(8,128)(2,1)}, u32[]{:S(2)}, u32[]{:S(2)}) collective-permute-start(bf16[64,4096]{1,0:T(8,128)(2,1)S(1)} %constant_dynamic-slice_fusion.5.p0), channel_id=1, source_target_pairs={{0,2},{2,0},{4,6},{6,4},{8,10},{10,8},{12,14},{14,12},{1,3},{3,1},... | collective-permute-start | bytes 1572872 | tf_op jit(solution)/shard_map/ppermute | solution.py:236
  3.6 25.0 %collective-permute-start.10 = (bf16[64,4096]{1,0:T(8,128)(2,1)}, bf16[64,4096]{1,0:T(8,128)(2,1)S(1)}, u32[]{:S(2)}, u32[]{:S(2)}) collective-permute-start(bf16[64,4096]{1,0:T(8,128)(2,1)} %constant_dynamic-slice_fusion.6), channel_id=1, source_target_pairs={{0,12},{2,14},{4,8},{6,10},{8,4},{10,6},{12,0},{14,2},{1,13},{3,15... | collective-permute-start | bytes 1572872 | tf_op jit(solution)/shard_map/ppermute | solution.py:236
  8.6 18.2 %copy-start.6 = (s32[32]{0:T(128)S(1)}, s32[32]{0:T(128)}, u32[]{:S(2)}) copy-start(s32[32]{0:T(128)} %param.9) | copy-start | bytes 388
  8.6 18.3 %copy-start.5 = (s32[32]{0:T(128)S(1)}, s32[32]{0:T(128)}, u32[]{:S(2)}) copy-start(s32[32]{0:T(128)} %param.10) | copy-start | bytes 388
  8.6 19.2 %copy-start.7 = (f32[512]{0:T(512)S(1)}, f32[512]{0:T(512)}, u32[]{:S(2)}) copy-start(f32[512]{0:T(512)} %constant.128) | copy-start | bytes 6148
  8.7 18.1 %collective-permute-start.1 = (bf16[64,2048]{1,0:T(8,128)(2,1)S(1)}, bf16[64,2048]{1,0:T(8,128)(2,1)S(1)}, u32[]{:S(2)}, u32[]{:S(2)}) collective-permute-start(bf16[64,2048]{1,0:T(8,128)(2,1)S(1)} %constant_dynamic-slice_fusion.4), channel_id=1, source_target_pairs={{0,4},{2,6},{4,0},{6,2},{8,12},{10,14},{12,8},{14,10},{1,5},{3,7},... | collective-permute-start | bytes 786440 | tf_op jit(solution)/shard_map/ppermute | solution.py:236
  8.8 24.2 %collective-permute-start.3 = (bf16[64,2048]{1,0:T(8,128)(2,1)S(1)}, bf16[64,2048]{1,0:T(8,128)(2,1)S(1)}, u32[]{:S(2)}, u32[]{:S(2)}) collective-permute-start(bf16[64,2048]{1,0:T(8,128)(2,1)S(1)} %constant_dynamic-slice_fusion.3), channel_id=1, source_target_pairs={{0,4},{2,6},{4,0},{6,2},{8,12},{10,14},{12,8},{14,10},{1,5},{3,7},... | collective-permute-start | bytes 786440 | tf_op jit(solution)/shard_map/ppermute | solution.py:236
  11.0 24.3 %copy-start.1 = (f32[256,1]{1,0:T(8,128)S(1)}, f32[256,1]{1,0:T(8,128)}, u32[]{:S(2)}) copy-start(f32[256,1]{1,0:T(8,128)} %constant.126.clone.dcol) | copy-start | bytes 3076
  11.0 24.3 %copy-start.2 = (f32[1,256]{1,0:T(1,128)S(1)}, f32[1,256]{1,0:T(1,128)}, u32[]{:S(2)}) copy-start(f32[1,256]{1,0:T(1,128)} %constant.125.clone.drow) | copy-start | bytes 3076
  11.0 24.3 %copy-start.3 = (f32[2,1,128]{2,1,0:T(1,128)S(1)}, f32[2,1,128]{2,1,0:T(1,128)}, u32[]{:S(2)}) copy-start(f32[2,1,128]{2,1,0:T(1,128)} %constant.127.clone.dpair) | copy-start | bytes 3076
  11.0 24.3 %collective-permute-start.5 = (bf16[64,4096]{1,0:T(8,128)(2,1)S(1)}, bf16[64,4096]{1,0:T(8,128)(2,1)S(1)}, u32[]{:S(2)}, u32[]{:S(2)}) collective-permute-start(bf16[64,4096]{1,0:T(8,128)(2,1)S(1)} %constant_dynamic-slice_fusion.2.f0a), channel_id=1, source_target_pairs={{0,2},{2,0},{4,6},{6,4},{8,10},{10,8},{12,14},{14,12},{1,3},{3,1},... | collective-permute-start | bytes 1572872 | tf_op jit(solution)/shard_map/ppermute | solution.py:236
  11.1 24.2 %collective-permute-start.6 = (bf16[64,4096]{1,0:T(8,128)(2,1)S(1)}, bf16[64,4096]{1,0:T(8,128)(2,1)S(1)}, u32[]{:S(2)}, u32[]{:S(2)}) collective-permute-start(bf16[64,4096]{1,0:T(8,128)(2,1)S(1)} %constant_dynamic-slice_fusion.1.f0b), channel_id=1, source_target_pairs={{0,2},{2,0},{4,6},{6,4},{8,10},{10,8},{12,14},{14,12},{1,3},{3,1},... | collective-permute-start | bytes 1572872 | tf_op jit(solution)/shard_map/ppermute | solution.py:236
  26.8 6.2 %collective-permute-start.2 = (bf16[64,2048]{1,0:T(8,128)(2,1)S(1)}, bf16[64,2048]{1,0:T(8,128)(2,1)S(1)}, u32[]{:S(2)}, u32[]{:S(2)}) collective-permute-start(bf16[64,2048]{1,0:T(8,128)(2,1)S(1)} %collective-permute-done.1.p2a), channel_id=1, source_target_pairs={{0,2},{2,0},{4,6},{6,4},{8,10},{10,8},{12,14},{14,12},{1,3},{3,1},... | collective-permute-start | bytes 786440 | tf_op jit(solution)/shard_map/ppermute | solution.py:236
  28.6 27.3 %collective-permute-start.9 = (bf16[64,4096]{1,0:T(8,128)(2,1)S(1)}, bf16[64,4096]{1,0:T(8,128)(2,1)S(1)}, u32[]{:S(2)}, u32[]{:S(2)}) collective-permute-start(bf16[64,4096]{1,0:T(8,128)(2,1)S(1)} %constant_dynamic-slice_fusion), channel_id=1, source_target_pairs={{0,8},{2,10},{4,12},{6,14},{8,0},{10,2},{12,4},{14,6},{1,9},{3,11}... | collective-permute-start | bytes 1572872 | tf_op jit(solution)/shard_map/ppermute | solution.py:236
  33.0 23.0 %collective-permute-start.11 = (bf16[64,4096]{1,0:T(8,128)(2,1)S(1)}, bf16[64,4096]{1,0:T(8,128)(2,1)S(1)}, u32[]{:S(2)}, u32[]{:S(2)}) collective-permute-start(bf16[64,4096]{1,0:T(8,128)(2,1)S(1)} %collective-permute-done.10.early.e0), channel_id=1, source_target_pairs={{0,2},{2,0},{4,6},{6,4},{8,10},{10,8},{12,14},{14,12},{1,3},{3,1},... | collective-permute-start | bytes 1572872 | tf_op jit(solution)/shard_map/ppermute | solution.py:236
  33.0 2.3 %collective-permute-start.4 = (bf16[64,2048]{1,0:T(8,128)(2,1)S(1)}, bf16[64,2048]{1,0:T(8,128)(2,1)S(1)}, u32[]{:S(2)}, u32[]{:S(2)}) collective-permute-start(bf16[64,2048]{1,0:T(8,128)(2,1)S(1)} %collective-permute-done.3.p2b), channel_id=1, source_target_pairs={{0,2},{2,0},{4,6},{6,4},{8,10},{10,8},{12,14},{14,12},{1,3},{3,1},... | collective-permute-start | bytes 786440 | tf_op jit(solution)/shard_map/ppermute | solution.py:236
  38.1 7.0 %collective-permute-start.7 = (bf16[64,256]{1,0:T(8,128)(2,1)S(1)}, bf16[64,256]{1,0:T(8,128)(2,1)S(1)}, u32[]{:S(2)}, u32[]{:S(2)}) collective-permute-start(bf16[64,256]{1,0:T(8,128)(2,1)S(1)} %get-tuple-element.53), channel_id=1, source_target_pairs={{0,4},{2,6},{4,0},{6,2},{8,12},{10,14},{12,8},{14,10},{1,5},{3,7},... | collective-permute-start | bytes 98312 | tf_op jit(solution)/shard_map/ppermute | solution.py:236
  40.5 15.5 %collective-permute-start.12 = (bf16[64,256]{1,0:T(8,128)(2,1)S(1)}, bf16[64,256]{1,0:T(8,128)(2,1)S(1)}, u32[]{:S(2)}, u32[]{:S(2)}) collective-permute-start(bf16[64,256]{1,0:T(8,128)(2,1)S(1)} %shard_map.96), channel_id=1, source_target_pairs={{0,4},{2,6},{4,0},{6,2},{8,12},{10,14},{12,8},{14,10},{1,5},{3,7},... | collective-permute-start | bytes 98312 | tf_op jit(solution)/shard_map/ppermute | solution.py:236
  45.1 14.1 %collective-permute-start.8 = (bf16[64,256]{1,0:T(8,128)(2,1)S(1)}, bf16[64,256]{1,0:T(8,128)(2,1)S(1)}, u32[]{:S(2)}, u32[]{:S(2)}) collective-permute-start(bf16[64,256]{1,0:T(8,128)(2,1)S(1)} %add_convert_fusion.2), channel_id=1, source_target_pairs={{0,1},{1,0},{2,3},{3,2},{4,5},{5,4},{6,7},{7,6},{8,9},{9,8},{10,11... | collective-permute-start | bytes 98312 | tf_op jit(solution)/shard_map/ppermute | solution.py:239
  57.6 4.2 %collective-permute-start.13 = (bf16[64,384]{1,0:T(8,128)(2,1)S(1)}, bf16[64,384]{1,0:T(8,128)(2,1)S(1)}, u32[]{:S(2)}, u32[]{:S(2)}) collective-permute-start(bf16[64,384]{1,0:T(8,128)(2,1)S(1)} %shard_map.97), channel_id=1, source_target_pairs={{0,1},{1,0},{2,3},{3,2},{4,5},{5,4},{6,7},{7,6},{8,9},{9,8},{10,11... | collective-permute-start | bytes 147464 | tf_op jit(solution)/shard_map/ppermute | solution.py:239
  61.8 6.2 %collective-permute-start.17 = (bf16[64,640]{1,0:T(8,128)(2,1)S(1)}, bf16[64,640]{1,0:T(8,128)(2,1)S(1)}, u32[]{:S(2)}, u32[]{:S(2)}) collective-permute-start(bf16[64,640]{1,0:T(8,128)(2,1)S(1)} %pad_maximum_fusion.1.refs_0_), channel_id=1, source_target_pairs={{0,8},{2,10},{4,12},{6,14},{8,0},{10,2},{12,4},{14,6},{1,9},{3,11}... | collective-permute-start | bytes 245768 | tf_op jit(solution)/shard_map/ppermute | solution.py:236
  61.9 7.0 %collective-permute-start.15 = (bf16[64,640]{1,0:T(8,128)(2,1)S(1)}, bf16[64,640]{1,0:T(8,128)(2,1)S(1)}, u32[]{:S(2)}, u32[]{:S(2)}) collective-permute-start(bf16[64,640]{1,0:T(8,128)(2,1)S(1)} %pad_maximum_fusion.1.refs_0_), channel_id=1, source_target_pairs={{0,4},{2,6},{4,0},{6,2},{8,12},{10,14},{12,8},{14,10},{1,5},{3,7},... | collective-permute-start | bytes 245768 | tf_op jit(solution)/shard_map/ppermute | solution.py:236
  68.0 4.4 %collective-permute-start.19 = (bf16[64,640]{1,0:T(8,128)(2,1)S(1)}, bf16[64,640]{1,0:T(8,128)(2,1)S(1)}, u32[]{:S(2)}, u32[]{:S(2)}) collective-permute-start(bf16[64,640]{1,0:T(8,128)(2,1)S(1)} %collective-permute-done.17.refs_4_), channel_id=1, source_target_pairs={{0,4},{2,6},{4,0},{6,2},{8,12},{10,14},{12,8},{14,10},{1,5},{3,7},... | collective-permute-start | bytes 245768 | tf_op jit(solution)/shard_map/ppermute | solution.py:236
  68.0 4.4 %collective-permute-start.14 = (bf16[64,640]{1,0:T(8,128)(2,1)S(1)}, bf16[64,640]{1,0:T(8,128)(2,1)S(1)}, u32[]{:S(2)}, u32[]{:S(2)}) collective-permute-start(bf16[64,640]{1,0:T(8,128)(2,1)S(1)} %pad_maximum_fusion.1.refs_0_), channel_id=1, source_target_pairs={{0,2},{2,0},{4,6},{6,4},{8,10},{10,8},{12,14},{14,12},{1,3},{3,1},... | collective-permute-start | bytes 245768 | tf_op jit(solution)/shard_map/ppermute | solution.py:236
  68.0 4.5 %collective-permute-start.18 = (bf16[64,640]{1,0:T(8,128)(2,1)S(1)}, bf16[64,640]{1,0:T(8,128)(2,1)S(1)}, u32[]{:S(2)}, u32[]{:S(2)}) collective-permute-start(bf16[64,640]{1,0:T(8,128)(2,1)S(1)} %collective-permute-done.17.refs_4_), channel_id=1, source_target_pairs={{0,2},{2,0},{4,6},{6,4},{8,10},{10,8},{12,14},{14,12},{1,3},{3,1},... | collective-permute-start | bytes 245768 | tf_op jit(solution)/shard_map/ppermute | solution.py:236
  68.9 3.6 %collective-permute-start.16 = (bf16[64,640]{1,0:T(8,128)(2,1)S(1)}, bf16[64,640]{1,0:T(8,128)(2,1)S(1)}, u32[]{:S(2)}, u32[]{:S(2)}) collective-permute-start(bf16[64,640]{1,0:T(8,128)(2,1)S(1)} %collective-permute-done.15.refs_2_), channel_id=1, source_target_pairs={{0,2},{2,0},{4,6},{6,4},{8,10},{10,8},{12,14},{14,12},{1,3},{3,1},... | collective-permute-start | bytes 245768 | tf_op jit(solution)/shard_map/ppermute | solution.py:236
  72.4 1.3 %collective-permute-start.20 = (bf16[64,640]{1,0:T(8,128)(2,1)S(1)}, bf16[64,640]{1,0:T(8,128)(2,1)S(1)}, u32[]{:S(2)}, u32[]{:S(2)}) collective-permute-start(bf16[64,640]{1,0:T(8,128)(2,1)S(1)} %collective-permute-done.19.refs_6_), channel_id=1, source_target_pairs={{0,2},{2,0},{4,6},{6,4},{8,10},{10,8},{12,14},{14,12},{1,3},{3,1},... | collective-permute-start | bytes 245768 | tf_op jit(solution)/shard_map/ppermute | solution.py:236

commit v3 on v2

--- a/solution.py
+++ b/solution.py
@@ -14,7 +14,8 @@
 POWER = 8
 NF = 128
 VMEM_BYTES = 40 * 1024 * 1024
-OWN_FLOPS, EARLY_FLOPS, LATE_FLOPS, FINISH_FLOPS = 0, 0, 20_000_000_000, 1_000_000_000
+OWN_FLOPS, EARLY_FLOPS, PAIR_FLOPS, LATE_FLOPS, FINISH_FLOPS = 0, 0, 0, 4_000_000_000, 1_000_000_000
+EARLY_LEAD = 8
 
 power_eps = 1e-06
 
@@ -154,7 +155,7 @@
     return pl.ds(pl.multiple_of(index * rows, rows), rows)
 
 
-def own_kernel(place, p0, p1, p2a, p2b, p3a, p3b, f0a, f0b, f1a, f1b, drow, dcol, dpair, near, keep, send, pair, strip):
+def own_kernel(place, p0, p1, p2a, p2b, p3a, p3b, far, fp, drow, dcol, dpair, near, keep, send, strip):
     chip, core = place[1], place[2]
     slot = 2 * core + chip
     rows, middle = p2a.shape
@@ -165,27 +166,32 @@
         near[block(slot ^ flip, rows), middle:] = second[...]
     mine = block(core, 2 * rows)
     strip[...] = outer(near[mine, :], near[...]) * (0.5 * dcol[mine, :]) * drow[...]
-    width = f0a.shape[1]
-    for index, first, second in ((core, f0a, f0b), (1 - core, f1a, f1b)):
-        pair[block(index, rows), :width] = first[...]
-        pair[block(index, rows), width:] = second[...]
-    inside = outer(pair[block(core, rows), :], pair[...]) * (0.5 * dcol[block(slot, rows), :]) * dpair[chip]
+    same = 0.5 * outer(far[...], far[...])
+    cross = outer(far[:, block(core, fp.shape[1])], fp[...])
+    inside = jnp.where(core == 0, jnp.concatenate([same, cross], axis=1), jnp.concatenate([cross, same], axis=1))
+    inside = inside * dcol[block(slot, rows), :] * dpair[chip]
     keep[...] = strip[block(chip, rows), :] + spread(inside, chip)
     send[...] = strip[block(1 - chip, rows), :].astype(jnp.bfloat16)
 
 
-def early_kernel(place, near, early, drow, dcol, out):
-    rows = early.shape[0]
+def early_kernel(place, near, ea, eb, drow, dcol, out):
+    rows, cut = ea.shape
     slot = 2 * place[2] + 1 - place[1]
-    out[...] = (outer(early[...], near[...]) * dcol[block(slot, rows), :] * drow[...]).astype(jnp.bfloat16)
-
-
-def late_kernel(place, near, late, e0, e1, before, drow, dcol, dpair, out, pair):
+    value = outer(ea[...], near[:, :cut]) + outer(eb[...], near[:, cut:])
+    out[...] = (value * dcol[block(slot, rows), :] * drow[...]).astype(jnp.bfloat16)
+
+
+def pair_kernel(place, e0a, e0b, e1a, e1b, pair):
+    (rows, cut), core = e0a.shape, place[2]
+    for index, first, second in ((core, e0a, e0b), (1 - core, e1a, e1b)):
+        pair[block(index, rows), :cut] = first[...]
+        pair[block(index, rows), cut:] = second[...]
+
+
+def late_kernel(place, near, late, pair, before, drow, dcol, dpair, out):
     rows, span = late.shape[0], near.shape[0]
     chip, core = place[1], place[2]
     scale = dcol[block(2 * core + chip, rows), :]
-    pair[block(core, rows), :] = e0[...]
-    pair[block(1 - core, rows), :] = e1[...]
     cross = outer(late[...], near[...]) * scale * drow[...] + before[...].astype(jnp.float32)
     out[:, :span] = cross.astype(jnp.bfloat16)
     out[:, span:] = (outer(late[...], pair[...]) * scale * dpair[1 - chip]).astype(jnp.bfloat16)
@@ -241,7 +247,7 @@
 
     def everyone(value):
         s4, s2 = tm_swap(value, 4), tm_swap(value, 2)
-        s6 = tm_swap(s4, 2)
+        s6 = tm_swap(value, 6)
         z = (value, s2, s4, s6)
         return [v for pair in zip(z, [tm_swap(v, 1) for v in z]) for v in pair]
 
@@ -249,23 +255,23 @@
         return lax.optimization_barrier((source, lax.dynamic_slice_in_dim(source, start, count, 1)))
 
     z = me // 2
-    source, far6 = cut(anomaly, (z ^ 3) * part, part)
+    lead = part * EARLY_LEAD // 16
+    source, far6a = cut(anomaly, (z ^ 3) * part, lead)
+    source, far6b = cut(source, (z ^ 3) * part + lead, part - lead)
     source, home = cut(source, z * part, part)
-    early = tm_swap(far6, 6)
+    ea, eb = tm_swap(far6a, 6), tm_swap(far6b, 6)
     p1 = tm_swap(home, 1)
     source, p1 = lax.optimization_barrier((source, p1))
     source, side_a = cut(source, (z ^ 1) * part, part // 2)
     source, side_b = cut(source, (z ^ 1) * part + part // 2, part // 2)
-    source, far_a = cut(source, (1 - half) * 2 * part, part)
-    source, far_b = cut(source, (1 - half) * 2 * part + part, part)
+    source, away = cut(source, (2 * (1 - half) + 1 - core) * part, part)
+    source, far = cut(source, (1 - half) * 2 * part, 2 * part)
+    p2a, p2b = tm_swap(side_a, 2), tm_swap(side_b, 2)
+    fp = tm_swap(away, 1)
     source, far4 = cut(source, (z ^ 2) * part, part)
+    far4, ea = lax.optimization_barrier((far4, ea))
     late = tm_swap(far4, 4)
-    p2a, p2b = tm_swap(side_a, 2), tm_swap(side_b, 2)
-    fa, fb = tm_swap(far_a, 1), tm_swap(far_b, 1)
-    p2a, offsets, taper_index = lax.optimization_barrier((p2a, offsets, taper_index))
-    w = weights(offsets, taper_index, me * freqs, freqs, order)
     p3a, p3b = tm_swap(p2a, 1), tm_swap(p2b, 1)
-    p3a, w = lax.optimization_barrier((p3a, w))
 
     factors = day_factors(span)
     first, second = factors[: 2 * rows].reshape(2, rows), factors[2 * rows :].reshape(2, rows)
@@ -289,21 +295,24 @@
         own_kernel,
         OWN_FLOPS,
         [((span, part), bf16), ((rows, span), jnp.float32), ((rows, span), bf16)],
-        [((2 * rows, 2 * part), bf16), ((2 * rows, span), jnp.float32)],
-        home, p1, p2a, p2b, p3a, p3b, far_a, far_b, fa, fb, drow, dcol, dpair,
+        [((2 * rows, span), jnp.float32)],
+        home, p1, p2a, p2b, p3a, p3b, far, fp, drow, dcol, dpair,
     )
-    mine = pix_sum((keep + tm_swap(send, 2).astype(jnp.float32)).astype(bf16))
-    e1 = tm_swap(early, 1)
-    (cross,) = call(early_kernel, EARLY_FLOPS, [((rows, span), bf16)], [], near, early, drow, dcol)
+    mine = (keep + tm_swap(send, 2).astype(jnp.float32)).astype(bf16)
+    e1a, e1b = tm_swap(ea, 1), tm_swap(eb, 1)
+    (cross,) = call(early_kernel, EARLY_FLOPS, [((rows, span), bf16)], [], near, ea, eb, drow, dcol)
     before = tm_swap(cross, 2)
+    (pair,) = call(pair_kernel, PAIR_FLOPS, [((2 * rows, part), bf16)], [], ea, eb, e1a, e1b)
     (last,) = call(
         late_kernel,
         LATE_FLOPS,
         [((rows, span + 2 * rows), bf16)],
-        [((2 * rows, part), bf16)],
-        near, late, early, e1, before, drow, dcol, dpair,
+        [],
+        near, late, pair, before, drow, dcol, dpair,
     )
-    pieces = everyone(jnp.concatenate([mine, pix_sum(last)], axis=1))
+    last, offsets, taper_index = lax.optimization_barrier((last, offsets, taper_index))
+    w = weights(offsets, taper_index, me * freqs, freqs, order)
+    pieces = everyone(pix_sum(jnp.concatenate([mine, last], axis=1)))
     gram_width = 2 * NB
     total_pixels = width * lax.axis_size("pix")
     gram, energy = call(

time: 77.6 us -> 76.8 us (0.990)
  waiting for transfers between devices: 40 us -> 25.1 us
  starting transfers between devices: 21.9 us -> 28.8 us
  local copies, waits for them, and re-layouts: 2.62 us -> 7.65 us
  Pallas kernels: 9.35 us -> 11.4 us
    ppermute x19 -> x20, waiting for transfers between devices: 37.4 us -> 24 us  [tm_swap(): return lax.ppermute(value, 'tm', [(i, i ^ bit) for i in range(n)])]
    ppermute x19 -> x20, starting transfers between devices: 18.8 us -> 27.2 us  [tm_swap(): return lax.ppermute(value, 'tm', [(i, i ^ bit) for i in range(n)])]
    unnamed x16 -> x24, local copies, waits for them, and re-layouts: 1.59 us -> 4.4 us
    dynamic_slice x7 -> x8, local copies, waits for them, and re-layouts: 1.03 us -> 3.25 us  [cut(): lax.dynamic_slice_in_dim(source, start, count, 1)]
    pallas_call x4 -> x5, Pallas kernels: 9.35 us -> 11.4 us  [call(): pl.pallas_call(kernel, out_shape=[jax.ShapeDtypeStruct(shape, kind) for s...]
    ppermute x2 -> x1, starting transfers between devices: 3.11 us -> 1.55 us  [pix_sum(): other = lax.ppermute(value, 'pix', [(0, 1), (1, 0)])]
    ppermute x2 -> x1, waiting for transfers between devices: 2.59 us -> 1.14 us  [pix_sum(): other = lax.ppermute(value, 'pix', [(0, 1), (1, 0)])]
  transfers between devices with their start and end apart: 21 -> 21, of which waited for: 9 -> 9; matrix products, arithmetic and copies ran while one was open for 4% -> 6% of each run, Pallas kernels for 7% -> 10%
where the time goes in v3:
time: 76.8 us; the launch traced here: 76.4 us
  starting transfers between devices  28.8 us (38%)
  waiting for transfers between devices  25.1 us (33%)
  Pallas kernels  11.4 us (15%)
  local copies, waits for them, and re-layouts  7.65 us (10%)
  other arithmetic  2.6 us (3%)
  between operations  0.93 us (1%)
    ppermute x20, starting transfers between devices, tm_swap(): return lax.ppermute(value, 'tm', [(i, i ^ bit) for i in range(n)])  27.2 us
    ppermute x20, waiting for transfers between devices, tm_swap(): return lax.ppermute(value, 'tm', [(i, i ^ bit) for i in range(n)])  24 us
    pallas_call x5, Pallas kernels, call(): pl.pallas_call(kernel, out_shape=[jax.ShapeDtypeStruct(shape, kind) for s...  11.4 us
    unnamed x24, local copies, waits for them, and re-layouts  4.4 us
    dynamic_slice x8, local copies, waits for them, and re-layouts, cut(): lax.dynamic_slice_in_dim(source, start, count, 1)  3.25 us
    ppermute x1, starting transfers between devices, pix_sum(): other = lax.ppermute(value, 'pix', [(0, 1), (1, 0)])  1.55 us
  transfers between devices with their start and end apart: 21, of which 9 were waited for; matrix products, arithmetic and copies ran while one was open for 6% of the time, Pallas kernels for 10%

profile of v3, /device:TPU:0, one launch (start us, length us, event | category | flops | bytes accessed | tf_op | source)
XLA Modules:
  0.0 76.4 jit_solution(2683354055323656744)
XLA Ops:
  0.6 0.0 copy-start
  0.7 1.6 %copy-done = bf16[64,16384]{1,0:T(8,128)(2,1)S(1)} copy-done((bf16[64,16384]{1,0:T(8,128)(2,1)S(1)}, bf16[64,16384]{1,0:T(8,128)(2,1)}, u32[]{:S(2)}) %copy-start) | copy-done | bytes 2097176
  2.2 0.7 constant_dynamic-slice_fusion.7
  2.9 0.7 constant_dynamic-slice_fusion.6
  3.7 0.5 collective-permute-start
  4.2 4.7 %collective-permute-start.6 = (bf16[64,2048]{1,0:T(8,128)(2,1)}, bf16[64,2048]{1,0:T(8,128)(2,1)S(1)}, u32[]{:S(2)}, u32[]{:S(2)}) collective-permute-start(bf16[64,2048]{1,0:T(8,128)(2,1)} %constant_dynamic-slice_fusion.7), channel_id=1, source_target_pairs={{0,12},{2,14},{4,8},{6,10},{8,4},{10,6},{12,0},{14,2},{1,13},{3,15... | collective-permute-start | bytes 786440 | tf_op jit(solution)/shard_map/ppermute | solution.py:242
  8.9 0.1 collective-permute-start.8
  9.1 0.7 copy-done.3
  9.8 0.8 %constant_dynamic-slice_fusion.2 = bf16[64,4096]{1,0:T(8,128)(2,1)} fusion(bf16[64,16384]{1,0:T(8,128)(2,1)S(1)} %copy-done, s32[]{:T(128)S(6)} %select_n.81), kind=kLoop, calls=%fused_computation.56 | loop fusion | bytes 1048580 | tf_op jit(solution)/shard_map/dynamic_slice | solution.py:255
  10.6 0.1 constant_dynamic-slice_fusion.1.far
  10.7 0.2 collective-permute-start.5
  10.9 2.0 %collective-permute-start.1 = (bf16[64,2048]{1,0:T(8,128)(2,1)S(1)}, bf16[64,2048]{1,0:T(8,128)(2,1)}, u32[]{:S(2)}, u32[]{:S(2)}) collective-permute-start(bf16[64,2048]{1,0:T(8,128)(2,1)S(1)} %constant_dynamic-slice_fusion.4), channel_id=1, source_target_pairs={{0,4},{2,6},{4,0},{6,2},{8,12},{10,14},{12,8},{14,10},{1,5},{3,7},... | collective-permute-start | bytes 786440 | tf_op jit(solution)/shard_map/ppermute | solution.py:242
  12.9 0.8 %constant_dynamic-slice_fusion = bf16[64,4096]{1,0:T(8,128)(2,1)} fusion(bf16[64,16384]{1,0:T(8,128)(2,1)S(1)} %copy-done, s32[]{:T(128)S(6)} %select_n.83), kind=kLoop, calls=%fused_computation.54 | loop fusion | bytes 1048580 | tf_op jit(solution)/shard_map/dynamic_slice | solution.py:255
  13.7 2.8 %collective-permute-done.6.e0a.ea = bf16[64,2048]{1,0:T(8,128)(2,1)S(1)} collective-permute-done((bf16[64,2048]{1,0:T(8,128)(2,1)}, bf16[64,2048]{1,0:T(8,128)(2,1)S(1)}, u32[]{:S(2)}, u32[]{:S(2)}) %collective-permute-start.6) | collective-permute-done | bytes 262176 | tf_op jit(solution)/shard_map/ppermute | solution.py:242
  16.5 12.0 %collective-permute-start.7 = (bf16[64,4096]{1,0:T(8,128)(2,1)}, bf16[64,4096]{1,0:T(8,128)(2,1)}, u32[]{:S(2)}, u32[]{:S(2)}) collective-permute-start(bf16[64,4096]{1,0:T(8,128)(2,1)} %constant_dynamic-slice_fusion), channel_id=1, source_target_pairs={{0,8},{2,10},{4,12},{6,14},{8,0},{10,2},{12,4},{14,6},{1,9},{3,11}... | collective-permute-start | bytes 1572872 | tf_op jit(solution)/shard_map/ppermute | solution.py:242
  28.4 5.6 %collective-permute-done.1.p2a = bf16[64,2048]{1,0:T(8,128)(2,1)} collective-permute-done((bf16[64,2048]{1,0:T(8,128)(2,1)S(1)}, bf16[64,2048]{1,0:T(8,128)(2,1)}, u32[]{:S(2)}, u32[]{:S(2)}) %collective-permute-start.1) | collective-permute-done | bytes 262176 | tf_op jit(solution)/shard_map/ppermute | solution.py:242
  34.1 0.1 collective-permute-start.3
  34.2 0.4 collective-permute-start.10
  34.6 0.1 collective-permute-start.9
  34.7 0.1 pad_add_fusion.place
  34.8 1.2 %collective-permute-done.3.p3a = bf16[64,2048]{1,0:T(8,128)(2,1)} collective-permute-done((bf16[64,2048]{1,0:T(8,128)(2,1)}, bf16[64,2048]{1,0:T(8,128)(2,1)}, u32[]{:S(2)}, u32[]{:S(2)}) %collective-permute-start.3) | collective-permute-done | bytes 262176 | tf_op jit(solution)/shard_map/ppermute | solution.py:242
  36.0 1.0 %copy-done.2 = bf16[64,4096]{1,0:T(8,128)(2,1)S(1)} copy-done((bf16[64,4096]{1,0:T(8,128)(2,1)S(1)}, bf16[64,4096]{1,0:T(8,128)(2,1)}, u32[]{:S(2)}) %copy-start.2) | copy-done | bytes 524312
  37.0 1.0 %copy-done.4 = bf16[64,4096]{1,0:T(8,128)(2,1)S(1)} copy-done((bf16[64,4096]{1,0:T(8,128)(2,1)S(1)}, bf16[64,4096]{1,0:T(8,128)(2,1)}, u32[]{:S(2)}) %copy-start.4) | copy-done | bytes 524312
  38.1 2.8 %shard_map.95 = (bf16[256,4096]{1,0:T(8,128)(2,1)S(1)}, f32[64,256]{1,0:T(8,128)S(1)}, bf16[64,256]{1,0:T(8,128)(2,1)S(1)}) custom-call(s32[3]{0:T(128)S(1)} %pad_add_fusion.place, bf16[64,4096]{1,0:T(8,128)(2,1)S(1)} %copy-done.2, bf16[64,4096]{1,0:T(8,128)(2,1)S(1)} %copy-done.4, bf16[64,2048]{1,0:T(8,128)(2,1)} %collective-permute-done.1.p2a, ...), custom_call_target="tpu_custom_call" | custom-call | tf_op jit(solution)/shard_map/pallas_call | solution.py:284
  40.9 1.7 %shard_map.97 = bf16[64,256]{1,0:T(8,128)(2,1)S(1)} custom-call(s32[3]{0:T(128)S(1)} %pad_add_fusion.place, bf16[256,4096]{1,0:T(8,128)(2,1)S(1)} %get-tuple-element.46.near, bf16[64,2048]{1,0:T(8,128)(2,1)S(1)} %collective-permute-done.6.e0a.ea, bf16[64,2048]{1,0:T(8,128)(2,1)} %collective-permute-done.8.e0b.eb, f32[1,256]{1,0:T(1,128)S(1)} %copy-done.6, ...), custom_call_target="tpu_custom_call" | custom-call | tf_op jit(solution)/shard_map/pallas_call | solution.py:284
  42.6 1.2 %collective-permute-start.11 = (bf16[64,256]{1,0:T(8,128)(2,1)S(1)}, bf16[64,256]{1,0:T(8,128)(2,1)S(1)}, u32[]{:S(2)}, u32[]{:S(2)}) collective-permute-start(bf16[64,256]{1,0:T(8,128)(2,1)S(1)} %shard_map.97), channel_id=1, source_target_pairs={{0,4},{2,6},{4,0},{6,2},{8,12},{10,14},{12,8},{14,10},{1,5},{3,7},... | collective-permute-start | bytes 98312 | tf_op jit(solution)/shard_map/ppermute | solution.py:242
  43.9 0.2 fusion.26
  44.1 1.0 %shard_map.96.pair = bf16[128,4096]{1,0:T(8,128)(2,1)S(1)} custom-call(s32[3]{0:T(128)S(1)} %pad_add_fusion.place, bf16[64,2048]{1,0:T(8,128)(2,1)S(1)} %collective-permute-done.6.e0a.ea, bf16[64,2048]{1,0:T(8,128)(2,1)} %collective-permute-done.8.e0b.eb, bf16[64,2048]{1,0:T(8,128)(2,1)S(1)} %collective-permute-done.9.e1a, ...), custom_call_target="tpu_custom_call" | custom-call | tf_op jit(solution)/shard_map/pallas_call | solution.py:284
  45.2 0.9 %collective-permute-start.12 = (bf16[64,256]{1,0:T(8,128)(2,1)S(1)}, bf16[64,256]{1,0:T(8,128)(2,1)S(1)}, u32[]{:S(2)}, u32[]{:S(2)}) collective-permute-start(bf16[64,256]{1,0:T(8,128)(2,1)S(1)} %get-tuple-element.60), channel_id=1, source_target_pairs={{0,4},{2,6},{4,0},{6,2},{8,12},{10,14},{12,8},{14,10},{1,5},{3,7},... | collective-permute-start | bytes 98312 | tf_op jit(solution)/shard_map/ppermute | solution.py:242
  46.1 8.6 %collective-permute-done.7.late = bf16[64,4096]{1,0:T(8,128)(2,1)} collective-permute-done((bf16[64,4096]{1,0:T(8,128)(2,1)}, bf16[64,4096]{1,0:T(8,128)(2,1)}, u32[]{:S(2)}, u32[]{:S(2)}) %collective-permute-start.7) | collective-permute-done | bytes 524320 | tf_op jit(solution)/shard_map/ppermute | solution.py:242
  54.7 0.6 collective-permute-done.11.before
  55.3 2.1 %shard_map.98 = bf16[64,384]{1,0:T(8,128)(2,1)S(1)} custom-call(s32[3]{0:T(128)S(1)} %pad_add_fusion.place, bf16[256,4096]{1,0:T(8,128)(2,1)S(1)} %get-tuple-element.46.near, bf16[64,4096]{1,0:T(8,128)(2,1)} %collective-permute-done.7.late, bf16[128,4096]{1,0:T(8,128)(2,1)S(1)} %shard_map.96.pair, bf16[64,256]{1,0:T(8,128)(2,1)S(1)} %collective-permute-done.11.before, ...), custom_call_target="tpu_custom_call" | custom-call | flops 4000000000 | tf_op jit(solution)/shard_map/pallas_call | solution.py:284
  57.5 1.6 %collective-permute-start.13 = (bf16[64,640]{1,0:T(8,128)(2,1)S(1)}, bf16[64,640]{1,0:T(8,128)(2,1)S(1)}, u32[]{:S(2)}, u32[]{:S(2)}) collective-permute-start(bf16[64,640]{1,0:T(8,128)(2,1)S(1)} %pad_maximum_fusion.1), channel_id=1, source_target_pairs={{0,1},{1,0},{2,3},{3,2},{4,5},{5,4},{6,7},{7,6},{8,9},{9,8},{10,11... | collective-permute-start | bytes 245768 | tf_op jit(solution)/shard_map/ppermute | solution.py:245
  59.0 0.9 %multiply_reduce_fusion = f32[32]{0:T(128)S(1)} fusion(pred[32]{0:T(512)(128)(4,1)S(1)} %get-tuple-element.71, pred[32]{0:T(512)(128)(4,1)S(1)} %get-tuple-element.72, pred[32]{0:T(512)(128)(4,1)S(1)} %get-tuple-element.73, pred[32]{0:T(512)(128)(4,1)S(1)} %get-tuple-element.70, s32[32]{0:T(128)S(1)} %copy-done.10, s32[512]{0:T(512)S(1)} %copy-done.8), kind=kLoop, calls=%fused_computation.32 | loop fusion | flops 425952 | bytes 2432 | tf_op jit(solution)/shard_map/reduce_sum | solution.py:121
  59.9 0.8 %multiply_multiply_fusion = f32[32,512]{1,0:T(8,128)S(1)} fusion(f32[512]{0:T(512)S(1)} %copy-done.11, f32[32]{0:T(128)S(1)} %sqrt.3, pred[32]{0:T(512)(128)(4,1)S(1)} %get-tuple-element.71, pred[32]{0:T(512)(128)(4,1)S(1)} %get-tuple-element.72, pred[32]{0:T(512)(128)(4,1)S(1)} %get-tuple-element.73, pred[32]{0:T(512)(128)(4,1)S(1)} %get-tuple-element.70, ...), kind=kLoop, calls=%fused_computation.31 | loop fusion | flops 425984 | bytes 70016 | tf_op jit(solution)/shard_map/mul | solution.py:123
  60.7 0.1 fusion.31
  60.8 1.1 %collective-permute-done.13 = bf16[64,640]{1,0:T(8,128)(2,1)S(1)} collective-permute-done((bf16[64,640]{1,0:T(8,128)(2,1)S(1)}, bf16[64,640]{1,0:T(8,128)(2,1)S(1)}, u32[]{:S(2)}, u32[]{:S(2)}) %collective-permute-start.13) | collective-permute-done | bytes 81952 | tf_op jit(solution)/shard_map/ppermute | solution.py:245
  62.0 0.1 collective-permute-start.15
  62.1 3.1 %collective-permute-start.17 = (bf16[64,640]{1,0:T(8,128)(2,1)S(1)}, bf16[64,640]{1,0:T(8,128)(2,1)S(1)}, u32[]{:S(2)}, u32[]{:S(2)}) collective-permute-start(bf16[64,640]{1,0:T(8,128)(2,1)S(1)} %add_convert_fusion.refs_0_), channel_id=1, source_target_pairs={{0,8},{2,10},{4,12},{6,14},{8,0},{10,2},{12,4},{14,6},{1,9},{3,11}... | collective-permute-start | bytes 245768 | tf_op jit(solution)/shard_map/ppermute | solution.py:242
  65.2 1.3 %collective-permute-start.19 = (bf16[64,640]{1,0:T(8,128)(2,1)S(1)}, bf16[64,640]{1,0:T(8,128)(2,1)S(1)}, u32[]{:S(2)}, u32[]{:S(2)}) collective-permute-start(bf16[64,640]{1,0:T(8,128)(2,1)S(1)} %add_convert_fusion.refs_0_), channel_id=1, source_target_pairs={{0,12},{2,14},{4,8},{6,10},{8,4},{10,6},{12,0},{14,2},{1,13},{3,15... | collective-permute-start | bytes 245768 | tf_op jit(solution)/shard_map/ppermute | solution.py:242
  66.5 0.4 multiply_convert_fusion.1
  66.9 0.1 collective-permute-start.14
  67.0 0.5 collective-permute-start.16
  67.4 2.5 %collective-permute-done.17.refs_4_ = bf16[64,640]{1,0:T(8,128)(2,1)S(1)} collective-permute-done((bf16[64,640]{1,0:T(8,128)(2,1)S(1)}, bf16[64,640]{1,0:T(8,128)(2,1)S(1)}, u32[]{:S(2)}, u32[]{:S(2)}) %collective-permute-start.17) | collective-permute-done | bytes 81952 | tf_op jit(solution)/shard_map/ppermute | solution.py:242
  69.9 1.6 %collective-permute-done.19.refs_6_ = bf16[64,640]{1,0:T(8,128)(2,1)S(1)} collective-permute-done((bf16[64,640]{1,0:T(8,128)(2,1)S(1)}, bf16[64,640]{1,0:T(8,128)(2,1)S(1)}, u32[]{:S(2)}, u32[]{:S(2)}) %collective-permute-start.19) | collective-permute-done | bytes 81952 | tf_op jit(solution)/shard_map/ppermute | solution.py:242
  71.5 0.1 pad_maximum_fusion.w
  71.6 1.1 %collective-permute-done.20.refs_7_ = bf16[64,640]{1,0:T(8,128)(2,1)S(1)} collective-permute-done((bf16[64,640]{1,0:T(8,128)(2,1)S(1)}, bf16[64,640]{1,0:T(8,128)(2,1)S(1)}, u32[]{:S(2)}, u32[]{:S(2)}) %collective-permute-start.20) | collective-permute-done | bytes 81952 | tf_op jit(solution)/shard_map/ppermute | solution.py:242
  72.8 3.7 %shard_map.99 = (f32[16,64,64]{2,1,0:T(8,128)}, f32[1,16]{1,0:T(1,128)}) custom-call(s32[3]{0:T(128)S(1)} %pad_add_fusion.place, bf16[16,64,512]{2,1,0:T(8,128)(2,1)S(1)} %pad_maximum_fusion.w, bf16[64,640]{1,0:T(8,128)(2,1)S(1)} %add_convert_fusion.refs_0_, bf16[64,640]{1,0:T(8,128)(2,1)S(1)} %collective-permute-done.14.refs_1_, ...), custom_call_target="tpu_custom_call" | custom-call | flops 1000000000 | tf_op jit(solution)/shard_map/pallas_call | solution.py:284
  (44 shorter events, 0.2 us)
Async XLA Ops:
  0.6 1.6 %copy-start = (bf16[64,16384]{1,0:T(8,128)(2,1)S(1)}, bf16[64,16384]{1,0:T(8,128)(2,1)}, u32[]{:S(2)}) copy-start(bf16[64,16384]{1,0:T(8,128)(2,1)} %param.8) | copy-start | bytes 6291460
  3.7 5.4 %copy-start.1 = (bf16[64,4096]{1,0:T(8,128)(2,1)}, bf16[64,4096]{1,0:T(8,128)(2,1)S(1)}, u32[]{:S(2)}) copy-start(bf16[64,4096]{1,0:T(8,128)(2,1)S(1)} %constant_dynamic-slice_fusion.5.p0) | copy-start | bytes 1572868
  3.7 5.3 %collective-permute-start = (bf16[64,4096]{1,0:T(8,128)(2,1)S(1)}, bf16[64,4096]{1,0:T(8,128)(2,1)S(1)}, u32[]{:S(2)}, u32[]{:S(2)}) collective-permute-start(bf16[64,4096]{1,0:T(8,128)(2,1)S(1)} %constant_dynamic-slice_fusion.5.p0), channel_id=1, source_target_pairs={{0,2},{2,0},{4,6},{6,4},{8,10},{10,8},{12,14},{14,12},{1,3},{3,1},... | collective-permute-start | bytes 1572872 | tf_op jit(solution)/shard_map/ppermute | solution.py:242
  4.2 12.2 %collective-permute-start.6 = (bf16[64,2048]{1,0:T(8,128)(2,1)}, bf16[64,2048]{1,0:T(8,128)(2,1)S(1)}, u32[]{:S(2)}, u32[]{:S(2)}) collective-permute-start(bf16[64,2048]{1,0:T(8,128)(2,1)} %constant_dynamic-slice_fusion.7), channel_id=1, source_target_pairs={{0,12},{2,14},{4,8},{6,10},{8,4},{10,6},{12,0},{14,2},{1,13},{3,15... | collective-permute-start | bytes 786440 | tf_op jit(solution)/shard_map/ppermute | solution.py:242
  8.9 25.3 %collective-permute-start.8 = (bf16[64,2048]{1,0:T(8,128)(2,1)}, bf16[64,2048]{1,0:T(8,128)(2,1)}, u32[]{:S(2)}, u32[]{:S(2)}) collective-permute-start(bf16[64,2048]{1,0:T(8,128)(2,1)} %constant_dynamic-slice_fusion.6), channel_id=1, source_target_pairs={{0,12},{2,14},{4,8},{6,10},{8,4},{10,6},{12,0},{14,2},{1,13},{3,15... | collective-permute-start | bytes 786440 | tf_op jit(solution)/shard_map/ppermute | solution.py:242
  9.0 0.8 %copy-start.3 = (bf16[64,4096]{1,0:T(8,128)(2,1)}, bf16[64,4096]{1,0:T(8,128)(2,1)S(1)}, u32[]{:S(2)}) copy-start(bf16[64,4096]{1,0:T(8,128)(2,1)S(1)} %collective-permute-done.p1) | copy-start | bytes 1572868
  9.8 26.2 %copy-start.5 = (f32[256,1]{1,0:T(8,128)S(1)}, f32[256,1]{1,0:T(8,128)}, u32[]{:S(2)}) copy-start(f32[256,1]{1,0:T(8,128)} %constant.123.clone.dcol) | copy-start | bytes 3076
  9.8 26.2 %copy-start.6 = (f32[1,256]{1,0:T(1,128)S(1)}, f32[1,256]{1,0:T(1,128)}, u32[]{:S(2)}) copy-start(f32[1,256]{1,0:T(1,128)} %constant.122.clone.drow) | copy-start | bytes 3076
  9.8 26.2 %copy-start.7 = (f32[2,1,128]{2,1,0:T(1,128)S(1)}, f32[2,1,128]{2,1,0:T(1,128)}, u32[]{:S(2)}) copy-start(f32[2,1,128]{2,1,0:T(1,128)} %constant.124.clone.dpair) | copy-start | bytes 3076
  10.7 23.9 %collective-permute-start.5 = (bf16[64,4096]{1,0:T(8,128)(2,1)}, bf16[64,4096]{1,0:T(8,128)(2,1)}, u32[]{:S(2)}, u32[]{:S(2)}) collective-permute-start(bf16[64,4096]{1,0:T(8,128)(2,1)} %constant_dynamic-slice_fusion.2), channel_id=1, source_target_pairs={{0,2},{2,0},{4,6},{6,4},{8,10},{10,8},{12,14},{14,12},{1,3},{3,1},... | collective-permute-start | bytes 1572872 | tf_op jit(solution)/shard_map/ppermute | solution.py:242
  10.9 17.6 %collective-permute-start.2 = (bf16[64,2048]{1,0:T(8,128)(2,1)S(1)}, bf16[64,2048]{1,0:T(8,128)(2,1)}, u32[]{:S(2)}, u32[]{:S(2)}) collective-permute-start(bf16[64,2048]{1,0:T(8,128)(2,1)S(1)} %constant_dynamic-slice_fusion.3), channel_id=1, source_target_pairs={{0,4},{2,6},{4,0},{6,2},{8,12},{10,14},{12,8},{14,10},{1,5},{3,7},... | collective-permute-start | bytes 786440 | tf_op jit(solution)/shard_map/ppermute | solution.py:242
  10.9 23.2 %collective-permute-start.1 = (bf16[64,2048]{1,0:T(8,128)(2,1)S(1)}, bf16[64,2048]{1,0:T(8,128)(2,1)}, u32[]{:S(2)}, u32[]{:S(2)}) collective-permute-start(bf16[64,2048]{1,0:T(8,128)(2,1)S(1)} %constant_dynamic-slice_fusion.4), channel_id=1, source_target_pairs={{0,4},{2,6},{4,0},{6,2},{8,12},{10,14},{12,8},{14,10},{1,5},{3,7},... | collective-permute-start | bytes 786440 | tf_op jit(solution)/shard_map/ppermute | solution.py:242
  16.5 38.2 %collective-permute-start.7 = (bf16[64,4096]{1,0:T(8,128)(2,1)}, bf16[64,4096]{1,0:T(8,128)(2,1)}, u32[]{:S(2)}, u32[]{:S(2)}) collective-permute-start(bf16[64,4096]{1,0:T(8,128)(2,1)} %constant_dynamic-slice_fusion), channel_id=1, source_target_pairs={{0,8},{2,10},{4,12},{6,14},{8,0},{10,2},{12,4},{14,6},{1,9},{3,11}... | collective-permute-start | bytes 1572872 | tf_op jit(solution)/shard_map/ppermute | solution.py:242
  28.4 6.3 %collective-permute-start.4 = (bf16[64,2048]{1,0:T(8,128)(2,1)}, bf16[64,2048]{1,0:T(8,128)(2,1)}, u32[]{:S(2)}, u32[]{:S(2)}) collective-permute-start(bf16[64,2048]{1,0:T(8,128)(2,1)} %collective-permute-done.2.p2b), channel_id=1, source_target_pairs={{0,2},{2,0},{4,6},{6,4},{8,10},{10,8},{12,14},{14,12},{1,3},{3,1},... | collective-permute-start | bytes 786440 | tf_op jit(solution)/shard_map/ppermute | solution.py:242
  34.1 1.9 %collective-permute-start.3 = (bf16[64,2048]{1,0:T(8,128)(2,1)}, bf16[64,2048]{1,0:T(8,128)(2,1)}, u32[]{:S(2)}, u32[]{:S(2)}) collective-permute-start(bf16[64,2048]{1,0:T(8,128)(2,1)} %collective-permute-done.1.p2a), channel_id=1, source_target_pairs={{0,2},{2,0},{4,6},{6,4},{8,10},{10,8},{12,14},{14,12},{1,3},{3,1},... | collective-permute-start | bytes 786440 | tf_op jit(solution)/shard_map/ppermute | solution.py:242
  34.2 9.9 %collective-permute-start.10 = (bf16[64,2048]{1,0:T(8,128)(2,1)}, bf16[64,2048]{1,0:T(8,128)(2,1)S(1)}, u32[]{:S(2)}, u32[]{:S(2)}) collective-permute-start(bf16[64,2048]{1,0:T(8,128)(2,1)} %collective-permute-done.8.e0b.eb), channel_id=1, source_target_pairs={{0,2},{2,0},{4,6},{6,4},{8,10},{10,8},{12,14},{14,12},{1,3},{3,1},... | collective-permute-start | bytes 786440 | tf_op jit(solution)/shard_map/ppermute | solution.py:242
  34.6 9.5 %collective-permute-start.9 = (bf16[64,2048]{1,0:T(8,128)(2,1)S(1)}, bf16[64,2048]{1,0:T(8,128)(2,1)S(1)}, u32[]{:S(2)}, u32[]{:S(2)}) collective-permute-start(bf16[64,2048]{1,0:T(8,128)(2,1)S(1)} %collective-permute-done.6.e0a.ea), channel_id=1, source_target_pairs={{0,2},{2,0},{4,6},{6,4},{8,10},{10,8},{12,14},{14,12},{1,3},{3,1},... | collective-permute-start | bytes 786440 | tf_op jit(solution)/shard_map/ppermute | solution.py:242
  36.0 1.0 %copy-start.2 = (bf16[64,4096]{1,0:T(8,128)(2,1)S(1)}, bf16[64,4096]{1,0:T(8,128)(2,1)}, u32[]{:S(2)}) copy-start(bf16[64,4096]{1,0:T(8,128)(2,1)} %copy-done.1) | copy-start | bytes 1572868
  37.0 1.0 %copy-start.4 = (bf16[64,4096]{1,0:T(8,128)(2,1)S(1)}, bf16[64,4096]{1,0:T(8,128)(2,1)}, u32[]{:S(2)}) copy-start(bf16[64,4096]{1,0:T(8,128)(2,1)} %copy-done.3) | copy-start | bytes 1572868
  40.9 3.0 %copy-start.8 = (s32[512]{0:T(512)S(1)}, s32[512]{0:T(512)}, u32[]{:S(2)}) copy-start(s32[512]{0:T(512)} %constant.125.clone) | copy-start | bytes 6148
  42.6 12.7 %collective-permute-start.11 = (bf16[64,256]{1,0:T(8,128)(2,1)S(1)}, bf16[64,256]{1,0:T(8,128)(2,1)S(1)}, u32[]{:S(2)}, u32[]{:S(2)}) collective-permute-start(bf16[64,256]{1,0:T(8,128)(2,1)S(1)} %shard_map.97), channel_id=1, source_target_pairs={{0,4},{2,6},{4,0},{6,2},{8,12},{10,14},{12,8},{14,10},{1,5},{3,7},... | collective-permute-start | bytes 98312 | tf_op jit(solution)/shard_map/ppermute | solution.py:242
  45.1 13.9 %copy-start.9 = (s32[32]{0:T(128)S(1)}, s32[32]{0:T(128)}, u32[]{:S(2)}) copy-start(s32[32]{0:T(128)} %param.10) | copy-start | bytes 388
  45.1 13.9 %copy-start.10 = (s32[32]{0:T(128)S(1)}, s32[32]{0:T(128)}, u32[]{:S(2)}) copy-start(s32[32]{0:T(128)} %param.9) | copy-start | bytes 388
  45.2 14.8 %copy-start.11 = (f32[512]{0:T(512)S(1)}, f32[512]{0:T(512)}, u32[]{:S(2)}) copy-start(f32[512]{0:T(512)} %constant.127) | copy-start | bytes 6148
  45.2 12.3 %collective-permute-start.12 = (bf16[64,256]{1,0:T(8,128)(2,1)S(1)}, bf16[64,256]{1,0:T(8,128)(2,1)S(1)}, u32[]{:S(2)}, u32[]{:S(2)}) collective-permute-start(bf16[64,256]{1,0:T(8,128)(2,1)S(1)} %get-tuple-element.60), channel_id=1, source_target_pairs={{0,4},{2,6},{4,0},{6,2},{8,12},{10,14},{12,8},{14,10},{1,5},{3,7},... | collective-permute-start | bytes 98312 | tf_op jit(solution)/shard_map/ppermute | solution.py:242
  57.5 4.5 %collective-permute-start.13 = (bf16[64,640]{1,0:T(8,128)(2,1)S(1)}, bf16[64,640]{1,0:T(8,128)(2,1)S(1)}, u32[]{:S(2)}, u32[]{:S(2)}) collective-permute-start(bf16[64,640]{1,0:T(8,128)(2,1)S(1)} %pad_maximum_fusion.1), channel_id=1, source_target_pairs={{0,1},{1,0},{2,3},{3,2},{4,5},{5,4},{6,7},{7,6},{8,9},{9,8},{10,11... | collective-permute-start | bytes 245768 | tf_op jit(solution)/shard_map/ppermute | solution.py:245
  62.0 4.9 %collective-permute-start.15 = (bf16[64,640]{1,0:T(8,128)(2,1)S(1)}, bf16[64,640]{1,0:T(8,128)(2,1)S(1)}, u32[]{:S(2)}, u32[]{:S(2)}) collective-permute-start(bf16[64,640]{1,0:T(8,128)(2,1)S(1)} %add_convert_fusion.refs_0_), channel_id=1, source_target_pairs={{0,4},{2,6},{4,0},{6,2},{8,12},{10,14},{12,8},{14,10},{1,5},{3,7},... | collective-permute-start | bytes 245768 | tf_op jit(solution)/shard_map/ppermute | solution.py:242
  62.1 7.9 %collective-permute-start.17 = (bf16[64,640]{1,0:T(8,128)(2,1)S(1)}, bf16[64,640]{1,0:T(8,128)(2,1)S(1)}, u32[]{:S(2)}, u32[]{:S(2)}) collective-permute-start(bf16[64,640]{1,0:T(8,128)(2,1)S(1)} %add_convert_fusion.refs_0_), channel_id=1, source_target_pairs={{0,8},{2,10},{4,12},{6,14},{8,0},{10,2},{12,4},{14,6},{1,9},{3,11}... | collective-permute-start | bytes 245768 | tf_op jit(solution)/shard_map/ppermute | solution.py:242
  65.2 6.3 %collective-permute-start.19 = (bf16[64,640]{1,0:T(8,128)(2,1)S(1)}, bf16[64,640]{1,0:T(8,128)(2,1)S(1)}, u32[]{:S(2)}, u32[]{:S(2)}) collective-permute-start(bf16[64,640]{1,0:T(8,128)(2,1)S(1)} %add_convert_fusion.refs_0_), channel_id=1, source_target_pairs={{0,12},{2,14},{4,8},{6,10},{8,4},{10,6},{12,0},{14,2},{1,13},{3,15... | collective-permute-start | bytes 245768 | tf_op jit(solution)/shard_map/ppermute | solution.py:242
  66.9 4.7 %collective-permute-start.14 = (bf16[64,640]{1,0:T(8,128)(2,1)S(1)}, bf16[64,640]{1,0:T(8,128)(2,1)S(1)}, u32[]{:S(2)}, u32[]{:S(2)}) collective-permute-start(bf16[64,640]{1,0:T(8,128)(2,1)S(1)} %add_convert_fusion.refs_0_), channel_id=1, source_target_pairs={{0,2},{2,0},{4,6},{6,4},{8,10},{10,8},{12,14},{14,12},{1,3},{3,1},... | collective-permute-start | bytes 245768 | tf_op jit(solution)/shard_map/ppermute | solution.py:242
  67.0 4.7 %collective-permute-start.16 = (bf16[64,640]{1,0:T(8,128)(2,1)S(1)}, bf16[64,640]{1,0:T(8,128)(2,1)S(1)}, u32[]{:S(2)}, u32[]{:S(2)}) collective-permute-start(bf16[64,640]{1,0:T(8,128)(2,1)S(1)} %collective-permute-done.15.refs_2_), channel_id=1, source_target_pairs={{0,2},{2,0},{4,6},{6,4},{8,10},{10,8},{12,14},{14,12},{1,3},{3,1},... | collective-permute-start | bytes 245768 | tf_op jit(solution)/shard_map/ppermute | solution.py:242
  69.9 1.7 %collective-permute-start.18 = (bf16[64,640]{1,0:T(8,128)(2,1)S(1)}, bf16[64,640]{1,0:T(8,128)(2,1)S(1)}, u32[]{:S(2)}, u32[]{:S(2)}) collective-permute-start(bf16[64,640]{1,0:T(8,128)(2,1)S(1)} %collective-permute-done.17.refs_4_), channel_id=1, source_target_pairs={{0,2},{2,0},{4,6},{6,4},{8,10},{10,8},{12,14},{14,12},{1,3},{3,1},... | collective-permute-start | bytes 245768 | tf_op jit(solution)/shard_map/ppermute | solution.py:242
  71.5 1.3 %collective-permute-start.20 = (bf16[64,640]{1,0:T(8,128)(2,1)S(1)}, bf16[64,640]{1,0:T(8,128)(2,1)S(1)}, u32[]{:S(2)}, u32[]{:S(2)}) collective-permute-start(bf16[64,640]{1,0:T(8,128)(2,1)S(1)} %collective-permute-done.19.refs_6_), channel_id=1, source_target_pairs={{0,2},{2,0},{4,6},{6,4},{8,10},{10,8},{12,14},{14,12},{1,3},{3,1},... | collective-permute-start | bytes 245768 | tf_op jit(solution)/shard_map/ppermute | solution.py:242

commit v4 on v3

--- a/solution.py
+++ b/solution.py
@@ -15,7 +15,7 @@
 NF = 128
 VMEM_BYTES = 40 * 1024 * 1024
 OWN_FLOPS, EARLY_FLOPS, PAIR_FLOPS, LATE_FLOPS, FINISH_FLOPS = 0, 0, 0, 4_000_000_000, 1_000_000_000
-EARLY_LEAD = 8
+EARLY_LEAD = 4
 
 power_eps = 1e-06
 
@@ -256,12 +256,13 @@
 
     z = me // 2
     lead = part * EARLY_LEAD // 16
-    source, far6a = cut(anomaly, (z ^ 3) * part, lead)
-    source, far6b = cut(source, (z ^ 3) * part + lead, part - lead)
-    source, home = cut(source, z * part, part)
-    ea, eb = tm_swap(far6a, 6), tm_swap(far6b, 6)
+    source, home = cut(anomaly, z * part, part)
+    source, far6a = cut(source, (z ^ 3) * part, lead)
+    ea = tm_swap(far6a, 6)
     p1 = tm_swap(home, 1)
     source, p1 = lax.optimization_barrier((source, p1))
+    source, far6b = cut(source, (z ^ 3) * part + lead, part - lead)
+    eb = tm_swap(far6b, 6)
     source, side_a = cut(source, (z ^ 1) * part, part // 2)
     source, side_b = cut(source, (z ^ 1) * part + part // 2, part // 2)
     source, away = cut(source, (2 * (1 - half) + 1 - core) * part, part)

time: 76.8 us -> 75.6 us (0.984)
  waiting for transfers between devices: 25.1 us -> 41.4 us
  starting transfers between devices: 28.8 us -> 19.4 us
  local copies, waits for them, and re-layouts: 7.65 us -> 1.89 us
  Pallas kernels: 11.4 us -> 9.19 us
    ppermute x20, waiting for transfers between devices: 24 us -> 40.3 us  [tm_swap(): return lax.ppermute(value, 'tm', [(i, i ^ bit) for i in range(n)])]
    ppermute x20, starting transfers between devices: 27.2 us -> 17.8 us  [tm_swap(): return lax.ppermute(value, 'tm', [(i, i ^ bit) for i in range(n)])]
    dynamic_slice x8, local copies, waits for them, and re-layouts: 3.25 us -> 0.27 us  [cut(): lax.dynamic_slice_in_dim(source, start, count, 1)]
    unnamed x24 -> x16, local copies, waits for them, and re-layouts: 4.4 us -> 1.62 us
    pallas_call x5, Pallas kernels: 11.4 us -> 9.19 us  [call(): pl.pallas_call(kernel, out_shape=[jax.ShapeDtypeStruct(shape, kind) for s...]
  transfers between devices with their start and end apart: 21 -> 21, of which waited for: 9 -> 10; matrix products, arithmetic and copies ran while one was open for 6% -> 4% of each run, Pallas kernels for 10% -> 5%
where the time goes in v4:
time: 75.6 us; the launch traced here: 75.5 us
  waiting for transfers between devices  41.4 us (55%)
  starting transfers between devices  19.4 us (26%)
  Pallas kernels  9.19 us (12%)
  other arithmetic  2.58 us (3%)
  local copies, waits for them, and re-layouts  1.89 us (2%)
  between operations  0.97 us (1%)
    ppermute x20, waiting for transfers between devices, tm_swap(): return lax.ppermute(value, 'tm', [(i, i ^ bit) for i in range(n)])  40.3 us
    ppermute x20, starting transfers between devices, tm_swap(): return lax.ppermute(value, 'tm', [(i, i ^ bit) for i in range(n)])  17.8 us
    pallas_call x5, Pallas kernels, call(): pl.pallas_call(kernel, out_shape=[jax.ShapeDtypeStruct(shape, kind) for s...  9.19 us
    unnamed x16, local copies, waits for them, and re-layouts  1.62 us
    ppermute x1, starting transfers between devices, pix_sum(): other = lax.ppermute(value, 'pix', [(0, 1), (1, 0)])  1.56 us
  transfers between devices with their start and end apart: 21, of which 10 were waited for; matrix products, arithmetic and copies ran while one was open for 4% of the time, Pallas kernels for 5%

profile of v4, /device:TPU:0, one launch (start us, length us, event | category | flops | bytes accessed | tf_op | source)
XLA Modules:
  0.0 75.5 jit_solution(13192827996138553581)
XLA Ops:
  0.6 0.0 copy-start
  0.7 1.6 %copy-done = bf16[64,16384]{1,0:T(8,128)(2,1)S(1)} copy-done((bf16[64,16384]{1,0:T(8,128)(2,1)S(1)}, bf16[64,16384]{1,0:T(8,128)(2,1)}, u32[]{:S(2)}) %copy-start) | copy-done | bytes 2097176
  2.3 0.5 collective-permute-start
  2.8 4.7 %collective-permute-start.6 = (bf16[64,1024]{1,0:T(8,128)(2,1)S(1)}, bf16[64,1024]{1,0:T(8,128)(2,1)S(1)}, u32[]{:S(2)}, u32[]{:S(2)}) collective-permute-start(bf16[64,1024]{1,0:T(8,128)(2,1)S(1)} %constant_dynamic-slice_fusion.6), channel_id=1, source_target_pairs={{0,12},{2,14},{4,8},{6,10},{8,4},{10,6},{12,0},{14,2},{1,13},{3,15... | collective-permute-start | bytes 393224 | tf_op jit(solution)/shard_map/ppermute | solution.py:242
  7.6 0.0 copy-start.1
  7.6 0.0 copy-start.2
  7.6 0.0 copy-start.3
  7.7 0.1 collective-permute-start.2
  7.8 2.0 %collective-permute-start.1 = (bf16[64,2048]{1,0:T(8,128)(2,1)S(1)}, bf16[64,2048]{1,0:T(8,128)(2,1)S(1)}, u32[]{:S(2)}, u32[]{:S(2)}) collective-permute-start(bf16[64,2048]{1,0:T(8,128)(2,1)S(1)} %constant_dynamic-slice_fusion.4), channel_id=1, source_target_pairs={{0,4},{2,6},{4,0},{6,2},{8,12},{10,14},{12,8},{14,10},{1,5},{3,7},... | collective-permute-start | bytes 786440 | tf_op jit(solution)/shard_map/ppermute | solution.py:242
  9.8 0.1 constant_dynamic-slice_fusion.1.far
  9.9 0.1 collective-permute-start.5
  9.9 1.9 %collective-permute-start.8 = (bf16[64,3072]{1,0:T(8,128)(2,1)S(1)}, bf16[64,3072]{1,0:T(8,128)(2,1)S(1)}, u32[]{:S(2)}, u32[]{:S(2)}) collective-permute-start(bf16[64,3072]{1,0:T(8,128)(2,1)S(1)} %constant_dynamic-slice_fusion.5), channel_id=1, source_target_pairs={{0,12},{2,14},{4,8},{6,10},{8,4},{10,6},{12,0},{14,2},{1,13},{3,15... | collective-permute-start | bytes 1179656 | tf_op jit(solution)/shard_map/ppermute | solution.py:242
  11.8 5.6 %collective-permute-done.2.p2b = bf16[64,2048]{1,0:T(8,128)(2,1)S(1)} collective-permute-done((bf16[64,2048]{1,0:T(8,128)(2,1)S(1)}, bf16[64,2048]{1,0:T(8,128)(2,1)S(1)}, u32[]{:S(2)}, u32[]{:S(2)}) %collective-permute-start.2) | collective-permute-done | bytes 262176 | tf_op jit(solution)/shard_map/ppermute | solution.py:242
  17.4 5.8 %collective-permute-done.1.p2a = bf16[64,2048]{1,0:T(8,128)(2,1)S(1)} collective-permute-done((bf16[64,2048]{1,0:T(8,128)(2,1)S(1)}, bf16[64,2048]{1,0:T(8,128)(2,1)S(1)}, u32[]{:S(2)}, u32[]{:S(2)}) %collective-permute-start.1) | collective-permute-done | bytes 262176 | tf_op jit(solution)/shard_map/ppermute | solution.py:242
  23.2 0.0 collective-permute-start.3
  23.2 0.0 copy-start.4
  23.3 1.4 %collective-permute-start.7 = (bf16[64,4096]{1,0:T(8,128)(2,1)S(1)}, bf16[64,4096]{1,0:T(8,128)(2,1)S(1)}, u32[]{:S(2)}, u32[]{:S(2)}) collective-permute-start(bf16[64,4096]{1,0:T(8,128)(2,1)S(1)} %constant_dynamic-slice_fusion), channel_id=1, source_target_pairs={{0,8},{2,10},{4,12},{6,14},{8,0},{10,2},{12,4},{14,6},{1,9},{3,11}... | collective-permute-start | bytes 1572872 | tf_op jit(solution)/shard_map/ppermute | solution.py:242
  24.7 0.1 pad_add_fusion.place
  24.8 6.9 %collective-permute-done.8.e0b.eb = bf16[64,3072]{1,0:T(8,128)(2,1)S(1)} collective-permute-done((bf16[64,3072]{1,0:T(8,128)(2,1)S(1)}, bf16[64,3072]{1,0:T(8,128)(2,1)S(1)}, u32[]{:S(2)}, u32[]{:S(2)}) %collective-permute-start.8) | collective-permute-done | bytes 393248 | tf_op jit(solution)/shard_map/ppermute | solution.py:242
  31.7 2.0 %shard_map.95 = (bf16[256,4096]{1,0:T(8,128)(2,1)S(1)}, f32[64,256]{1,0:T(8,128)S(1)}, bf16[64,256]{1,0:T(8,128)(2,1)S(1)}) custom-call(s32[3]{0:T(128)S(1)} %pad_add_fusion.place, bf16[64,4096]{1,0:T(8,128)(2,1)S(1)} %constant_dynamic-slice_fusion.7.p0, bf16[64,4096]{1,0:T(8,128)(2,1)S(1)} %collective-permute-done.p1, ...), custom_call_target="tpu_custom_call" | custom-call | tf_op jit(solution)/shard_map/pallas_call | solution.py:285
  33.7 0.1 collective-permute-start.12
  33.8 0.2 fusion.26
  34.0 0.6 collective-permute-start.9
  34.6 1.3 %shard_map.97 = bf16[64,256]{1,0:T(8,128)(2,1)S(1)} custom-call(s32[3]{0:T(128)S(1)} %pad_add_fusion.place, bf16[256,4096]{1,0:T(8,128)(2,1)S(1)} %get-tuple-element.46.near, bf16[64,1024]{1,0:T(8,128)(2,1)S(1)} %collective-permute-done.6.e0a.ea, bf16[64,3072]{1,0:T(8,128)(2,1)S(1)} %collective-permute-done.8.e0b.eb, f32[1,256]{1,0:T(1,128)S(1)} %copy-done.2, ...), custom_call_target="tpu_custom_call" | custom-call | tf_op jit(solution)/shard_map/pallas_call | solution.py:285
  35.9 1.8 %collective-permute-start.11 = (bf16[64,256]{1,0:T(8,128)(2,1)S(1)}, bf16[64,256]{1,0:T(8,128)(2,1)S(1)}, u32[]{:S(2)}, u32[]{:S(2)}) collective-permute-start(bf16[64,256]{1,0:T(8,128)(2,1)S(1)} %shard_map.97), channel_id=1, source_target_pairs={{0,4},{2,6},{4,0},{6,2},{8,12},{10,14},{12,8},{14,10},{1,5},{3,7},... | collective-permute-start | bytes 98312 | tf_op jit(solution)/shard_map/ppermute | solution.py:242
  37.6 5.3 %collective-permute-done.12 = bf16[64,256]{1,0:T(8,128)(2,1)S(1)} collective-permute-done((bf16[64,256]{1,0:T(8,128)(2,1)S(1)}, bf16[64,256]{1,0:T(8,128)(2,1)S(1)}, u32[]{:S(2)}, u32[]{:S(2)}) %collective-permute-start.12) | collective-permute-done | bytes 32800 | tf_op jit(solution)/shard_map/ppermute | solution.py:242
  43.0 0.6 shard_map.96.pair
  43.6 0.0 copy-start.5
  43.6 0.0 copy-start.7
  43.6 10.2 %collective-permute-done.7.late = bf16[64,4096]{1,0:T(8,128)(2,1)S(1)} collective-permute-done((bf16[64,4096]{1,0:T(8,128)(2,1)S(1)}, bf16[64,4096]{1,0:T(8,128)(2,1)S(1)}, u32[]{:S(2)}, u32[]{:S(2)}) %collective-permute-start.7) | collective-permute-done | bytes 524320 | tf_op jit(solution)/shard_map/ppermute | solution.py:242
  53.8 1.6 %shard_map.98 = bf16[64,384]{1,0:T(8,128)(2,1)S(1)} custom-call(s32[3]{0:T(128)S(1)} %pad_add_fusion.place, bf16[256,4096]{1,0:T(8,128)(2,1)S(1)} %get-tuple-element.46.near, bf16[64,4096]{1,0:T(8,128)(2,1)S(1)} %collective-permute-done.7.late, bf16[128,4096]{1,0:T(8,128)(2,1)S(1)} %shard_map.96.pair, bf16[64,256]{1,0:T(8,128)(2,1)S(1)} %collective-permute-done.11.before, ...), custom_call_target="tpu_custom_call" | custom-call | flops 4000000000 | tf_op jit(solution)/shard_map/pallas_call | solution.py:285
  55.5 1.6 %collective-permute-start.13 = (bf16[64,640]{1,0:T(8,128)(2,1)S(1)}, bf16[64,640]{1,0:T(8,128)(2,1)S(1)}, u32[]{:S(2)}, u32[]{:S(2)}) collective-permute-start(bf16[64,640]{1,0:T(8,128)(2,1)S(1)} %pad_maximum_fusion.1), channel_id=1, source_target_pairs={{0,1},{1,0},{2,3},{3,2},{4,5},{5,4},{6,7},{7,6},{8,9},{9,8},{10,11... | collective-permute-start | bytes 245768 | tf_op jit(solution)/shard_map/ppermute | solution.py:245
  57.0 0.9 %multiply_reduce_fusion = f32[32]{0:T(128)S(1)} fusion(pred[32]{0:T(512)(128)(4,1)S(1)} %get-tuple-element.71, pred[32]{0:T(512)(128)(4,1)S(1)} %get-tuple-element.72, pred[32]{0:T(512)(128)(4,1)S(1)} %get-tuple-element.73, pred[32]{0:T(512)(128)(4,1)S(1)} %get-tuple-element.70, s32[32]{0:T(128)S(1)} %copy-done.6, s32[512]{0:T(512)S(1)} %copy-done.4), kind=kLoop, calls=%fused_computation.32 | loop fusion | flops 425952 | bytes 2432 | tf_op jit(solution)/shard_map/reduce_sum | solution.py:121
  57.9 0.8 %multiply_multiply_fusion = f32[32,512]{1,0:T(8,128)S(1)} fusion(f32[512]{0:T(512)S(1)} %copy-done.7, f32[32]{0:T(128)S(1)} %sqrt.3, pred[32]{0:T(512)(128)(4,1)S(1)} %get-tuple-element.71, pred[32]{0:T(512)(128)(4,1)S(1)} %get-tuple-element.72, pred[32]{0:T(512)(128)(4,1)S(1)} %get-tuple-element.73, pred[32]{0:T(512)(128)(4,1)S(1)} %get-tuple-element.70, ...), kind=kLoop, calls=%fused_computation.31 | loop fusion | flops 425984 | bytes 70016 | tf_op jit(solution)/shard_map/mul | solution.py:123
  58.7 0.1 fusion.31
  58.8 1.1 %collective-permute-done.13 = bf16[64,640]{1,0:T(8,128)(2,1)S(1)} collective-permute-done((bf16[64,640]{1,0:T(8,128)(2,1)S(1)}, bf16[64,640]{1,0:T(8,128)(2,1)S(1)}, u32[]{:S(2)}, u32[]{:S(2)}) %collective-permute-start.13) | collective-permute-done | bytes 81952 | tf_op jit(solution)/shard_map/ppermute | solution.py:245
  60.0 0.8 %collective-permute-start.15 = (bf16[64,640]{1,0:T(8,128)(2,1)S(1)}, bf16[64,640]{1,0:T(8,128)(2,1)S(1)}, u32[]{:S(2)}, u32[]{:S(2)}) collective-permute-start(bf16[64,640]{1,0:T(8,128)(2,1)S(1)} %add_convert_fusion.refs_0_), channel_id=1, source_target_pairs={{0,4},{2,6},{4,0},{6,2},{8,12},{10,14},{12,8},{14,10},{1,5},{3,7},... | collective-permute-start | bytes 245768 | tf_op jit(solution)/shard_map/ppermute | solution.py:242
  60.8 3.4 %collective-permute-start.17 = (bf16[64,640]{1,0:T(8,128)(2,1)S(1)}, bf16[64,640]{1,0:T(8,128)(2,1)S(1)}, u32[]{:S(2)}, u32[]{:S(2)}) collective-permute-start(bf16[64,640]{1,0:T(8,128)(2,1)S(1)} %add_convert_fusion.refs_0_), channel_id=1, source_target_pairs={{0,8},{2,10},{4,12},{6,14},{8,0},{10,2},{12,4},{14,6},{1,9},{3,11}... | collective-permute-start | bytes 245768 | tf_op jit(solution)/shard_map/ppermute | solution.py:242
  64.2 0.3 collective-permute-start.19
  64.4 0.4 multiply_convert_fusion.1
  64.9 0.1 collective-permute-start.14
  64.9 0.3 collective-permute-done.15.refs_2_
  65.2 0.2 collective-permute-start.16
  65.4 3.5 %collective-permute-done.17.refs_4_ = bf16[64,640]{1,0:T(8,128)(2,1)S(1)} collective-permute-done((bf16[64,640]{1,0:T(8,128)(2,1)S(1)}, bf16[64,640]{1,0:T(8,128)(2,1)S(1)}, u32[]{:S(2)}, u32[]{:S(2)}) %collective-permute-start.17) | collective-permute-done | bytes 81952 | tf_op jit(solution)/shard_map/ppermute | solution.py:242
  68.9 1.6 %collective-permute-done.19.refs_6_ = bf16[64,640]{1,0:T(8,128)(2,1)S(1)} collective-permute-done((bf16[64,640]{1,0:T(8,128)(2,1)S(1)}, bf16[64,640]{1,0:T(8,128)(2,1)S(1)}, u32[]{:S(2)}, u32[]{:S(2)}) %collective-permute-start.19) | collective-permute-done | bytes 81952 | tf_op jit(solution)/shard_map/ppermute | solution.py:242
  70.5 0.1 pad_maximum_fusion.w
  70.6 1.2 %collective-permute-done.20.refs_7_ = bf16[64,640]{1,0:T(8,128)(2,1)S(1)} collective-permute-done((bf16[64,640]{1,0:T(8,128)(2,1)S(1)}, bf16[64,640]{1,0:T(8,128)(2,1)S(1)}, u32[]{:S(2)}, u32[]{:S(2)}) %collective-permute-start.20) | collective-permute-done | bytes 81952 | tf_op jit(solution)/shard_map/ppermute | solution.py:242
  71.8 3.7 %shard_map.99 = (f32[16,64,64]{2,1,0:T(8,128)}, f32[1,16]{1,0:T(1,128)}) custom-call(s32[3]{0:T(128)S(1)} %pad_add_fusion.place, bf16[16,64,512]{2,1,0:T(8,128)(2,1)S(1)} %pad_maximum_fusion.w, bf16[64,640]{1,0:T(8,128)(2,1)S(1)} %add_convert_fusion.refs_0_, bf16[64,640]{1,0:T(8,128)(2,1)S(1)} %collective-permute-done.14.refs_1_, ...), custom_call_target="tpu_custom_call" | custom-call | flops 1000000000 | tf_op jit(solution)/shard_map/pallas_call | solution.py:285
  (36 shorter events, 0.3 us)
Async XLA Ops:
  0.6 1.6 %copy-start = (bf16[64,16384]{1,0:T(8,128)(2,1)S(1)}, bf16[64,16384]{1,0:T(8,128)(2,1)}, u32[]{:S(2)}) copy-start(bf16[64,16384]{1,0:T(8,128)(2,1)} %param.8) | copy-start | bytes 6291460
  2.3 5.2 %collective-permute-start = (bf16[64,4096]{1,0:T(8,128)(2,1)S(1)}, bf16[64,4096]{1,0:T(8,128)(2,1)S(1)}, u32[]{:S(2)}, u32[]{:S(2)}) collective-permute-start(bf16[64,4096]{1,0:T(8,128)(2,1)S(1)} %constant_dynamic-slice_fusion.7.p0), channel_id=1, source_target_pairs={{0,2},{2,0},{4,6},{6,4},{8,10},{10,8},{12,14},{14,12},{1,3},{3,1},... | collective-permute-start | bytes 1572872 | tf_op jit(solution)/shard_map/ppermute | solution.py:242
  2.8 20.5 %collective-permute-start.6 = (bf16[64,1024]{1,0:T(8,128)(2,1)S(1)}, bf16[64,1024]{1,0:T(8,128)(2,1)S(1)}, u32[]{:S(2)}, u32[]{:S(2)}) collective-permute-start(bf16[64,1024]{1,0:T(8,128)(2,1)S(1)} %constant_dynamic-slice_fusion.6), channel_id=1, source_target_pairs={{0,12},{2,14},{4,8},{6,10},{8,4},{10,6},{12,0},{14,2},{1,13},{3,15... | collective-permute-start | bytes 393224 | tf_op jit(solution)/shard_map/ppermute | solution.py:242
  7.6 24.1 %copy-start.1 = (f32[256,1]{1,0:T(8,128)S(1)}, f32[256,1]{1,0:T(8,128)}, u32[]{:S(2)}) copy-start(f32[256,1]{1,0:T(8,128)} %constant.126.clone.dcol) | copy-start | bytes 3076
  7.6 24.1 %copy-start.2 = (f32[1,256]{1,0:T(1,128)S(1)}, f32[1,256]{1,0:T(1,128)}, u32[]{:S(2)}) copy-start(f32[1,256]{1,0:T(1,128)} %constant.125.clone.drow) | copy-start | bytes 3076
  7.6 24.1 %copy-start.3 = (f32[2,1,128]{2,1,0:T(1,128)S(1)}, f32[2,1,128]{2,1,0:T(1,128)}, u32[]{:S(2)}) copy-start(f32[2,1,128]{2,1,0:T(1,128)} %constant.127.clone.dpair) | copy-start | bytes 3076
  7.7 9.7 %collective-permute-start.2 = (bf16[64,2048]{1,0:T(8,128)(2,1)S(1)}, bf16[64,2048]{1,0:T(8,128)(2,1)S(1)}, u32[]{:S(2)}, u32[]{:S(2)}) collective-permute-start(bf16[64,2048]{1,0:T(8,128)(2,1)S(1)} %constant_dynamic-slice_fusion.3), channel_id=1, source_target_pairs={{0,4},{2,6},{4,0},{6,2},{8,12},{10,14},{12,8},{14,10},{1,5},{3,7},... | collective-permute-start | bytes 786440 | tf_op jit(solution)/shard_map/ppermute | solution.py:242
  7.8 15.4 %collective-permute-start.1 = (bf16[64,2048]{1,0:T(8,128)(2,1)S(1)}, bf16[64,2048]{1,0:T(8,128)(2,1)S(1)}, u32[]{:S(2)}, u32[]{:S(2)}) collective-permute-start(bf16[64,2048]{1,0:T(8,128)(2,1)S(1)} %constant_dynamic-slice_fusion.4), channel_id=1, source_target_pairs={{0,4},{2,6},{4,0},{6,2},{8,12},{10,14},{12,8},{14,10},{1,5},{3,7},... | collective-permute-start | bytes 786440 | tf_op jit(solution)/shard_map/ppermute | solution.py:242
  9.9 21.8 %collective-permute-start.5 = (bf16[64,4096]{1,0:T(8,128)(2,1)S(1)}, bf16[64,4096]{1,0:T(8,128)(2,1)S(1)}, u32[]{:S(2)}, u32[]{:S(2)}) collective-permute-start(bf16[64,4096]{1,0:T(8,128)(2,1)S(1)} %constant_dynamic-slice_fusion.2), channel_id=1, source_target_pairs={{0,2},{2,0},{4,6},{6,4},{8,10},{10,8},{12,14},{14,12},{1,3},{3,1},... | collective-permute-start | bytes 1572872 | tf_op jit(solution)/shard_map/ppermute | solution.py:242
  9.9 21.7 %collective-permute-start.8 = (bf16[64,3072]{1,0:T(8,128)(2,1)S(1)}, bf16[64,3072]{1,0:T(8,128)(2,1)S(1)}, u32[]{:S(2)}, u32[]{:S(2)}) collective-permute-start(bf16[64,3072]{1,0:T(8,128)(2,1)S(1)} %constant_dynamic-slice_fusion.5), channel_id=1, source_target_pairs={{0,12},{2,14},{4,8},{6,10},{8,4},{10,6},{12,0},{14,2},{1,13},{3,15... | collective-permute-start | bytes 1179656 | tf_op jit(solution)/shard_map/ppermute | solution.py:242
  17.4 14.2 %collective-permute-start.4 = (bf16[64,2048]{1,0:T(8,128)(2,1)S(1)}, bf16[64,2048]{1,0:T(8,128)(2,1)S(1)}, u32[]{:S(2)}, u32[]{:S(2)}) collective-permute-start(bf16[64,2048]{1,0:T(8,128)(2,1)S(1)} %collective-permute-done.2.p2b), channel_id=1, source_target_pairs={{0,2},{2,0},{4,6},{6,4},{8,10},{10,8},{12,14},{14,12},{1,3},{3,1},... | collective-permute-start | bytes 786440 | tf_op jit(solution)/shard_map/ppermute | solution.py:242
  23.2 8.5 %collective-permute-start.3 = (bf16[64,2048]{1,0:T(8,128)(2,1)S(1)}, bf16[64,2048]{1,0:T(8,128)(2,1)S(1)}, u32[]{:S(2)}, u32[]{:S(2)}) collective-permute-start(bf16[64,2048]{1,0:T(8,128)(2,1)S(1)} %collective-permute-done.1.p2a), channel_id=1, source_target_pairs={{0,2},{2,0},{4,6},{6,4},{8,10},{10,8},{12,14},{14,12},{1,3},{3,1},... | collective-permute-start | bytes 786440 | tf_op jit(solution)/shard_map/ppermute | solution.py:242
  23.2 10.5 %copy-start.4 = (s32[512]{0:T(512)S(1)}, s32[512]{0:T(512)}, u32[]{:S(2)}) copy-start(s32[512]{0:T(512)} %constant.128.clone) | copy-start | bytes 6148
  23.3 30.5 %collective-permute-start.7 = (bf16[64,4096]{1,0:T(8,128)(2,1)S(1)}, bf16[64,4096]{1,0:T(8,128)(2,1)S(1)}, u32[]{:S(2)}, u32[]{:S(2)}) collective-permute-start(bf16[64,4096]{1,0:T(8,128)(2,1)S(1)} %constant_dynamic-slice_fusion), channel_id=1, source_target_pairs={{0,8},{2,10},{4,12},{6,14},{8,0},{10,2},{12,4},{14,6},{1,9},{3,11}... | collective-permute-start | bytes 1572872 | tf_op jit(solution)/shard_map/ppermute | solution.py:242
  31.6 11.3 %collective-permute-start.10 = (bf16[64,3072]{1,0:T(8,128)(2,1)S(1)}, bf16[64,3072]{1,0:T(8,128)(2,1)S(1)}, u32[]{:S(2)}, u32[]{:S(2)}) collective-permute-start(bf16[64,3072]{1,0:T(8,128)(2,1)S(1)} %collective-permute-done.8.e0b.eb), channel_id=1, source_target_pairs={{0,2},{2,0},{4,6},{6,4},{8,10},{10,8},{12,14},{14,12},{1,3},{3,1},... | collective-permute-start | bytes 1179656 | tf_op jit(solution)/shard_map/ppermute | solution.py:242
  33.7 9.3 %collective-permute-start.12 = (bf16[64,256]{1,0:T(8,128)(2,1)S(1)}, bf16[64,256]{1,0:T(8,128)(2,1)S(1)}, u32[]{:S(2)}, u32[]{:S(2)}) collective-permute-start(bf16[64,256]{1,0:T(8,128)(2,1)S(1)} %get-tuple-element.60), channel_id=1, source_target_pairs={{0,4},{2,6},{4,0},{6,2},{8,12},{10,14},{12,8},{14,10},{1,5},{3,7},... | collective-permute-start | bytes 98312 | tf_op jit(solution)/shard_map/ppermute | solution.py:242
  34.0 9.0 %collective-permute-start.9 = (bf16[64,1024]{1,0:T(8,128)(2,1)S(1)}, bf16[64,1024]{1,0:T(8,128)(2,1)S(1)}, u32[]{:S(2)}, u32[]{:S(2)}) collective-permute-start(bf16[64,1024]{1,0:T(8,128)(2,1)S(1)} %collective-permute-done.6.e0a.ea), channel_id=1, source_target_pairs={{0,2},{2,0},{4,6},{6,4},{8,10},{10,8},{12,14},{14,12},{1,3},{3,1},... | collective-permute-start | bytes 393224 | tf_op jit(solution)/shard_map/ppermute | solution.py:242
  35.9 18.0 %collective-permute-start.11 = (bf16[64,256]{1,0:T(8,128)(2,1)S(1)}, bf16[64,256]{1,0:T(8,128)(2,1)S(1)}, u32[]{:S(2)}, u32[]{:S(2)}) collective-permute-start(bf16[64,256]{1,0:T(8,128)(2,1)S(1)} %shard_map.97), channel_id=1, source_target_pairs={{0,4},{2,6},{4,0},{6,2},{8,12},{10,14},{12,8},{14,10},{1,5},{3,7},... | collective-permute-start | bytes 98312 | tf_op jit(solution)/shard_map/ppermute | solution.py:242
  43.6 13.4 %copy-start.5 = (s32[32]{0:T(128)S(1)}, s32[32]{0:T(128)}, u32[]{:S(2)}) copy-start(s32[32]{0:T(128)} %param.10) | copy-start | bytes 388
  43.6 13.4 %copy-start.6 = (s32[32]{0:T(128)S(1)}, s32[32]{0:T(128)}, u32[]{:S(2)}) copy-start(s32[32]{0:T(128)} %param.9) | copy-start | bytes 388
  43.6 14.3 %copy-start.7 = (f32[512]{0:T(512)S(1)}, f32[512]{0:T(512)}, u32[]{:S(2)}) copy-start(f32[512]{0:T(512)} %constant.130) | copy-start | bytes 6148
  55.5 4.5 %collective-permute-start.13 = (bf16[64,640]{1,0:T(8,128)(2,1)S(1)}, bf16[64,640]{1,0:T(8,128)(2,1)S(1)}, u32[]{:S(2)}, u32[]{:S(2)}) collective-permute-start(bf16[64,640]{1,0:T(8,128)(2,1)S(1)} %pad_maximum_fusion.1), channel_id=1, source_target_pairs={{0,1},{1,0},{2,3},{3,2},{4,5},{5,4},{6,7},{7,6},{8,9},{9,8},{10,11... | collective-permute-start | bytes 245768 | tf_op jit(solution)/shard_map/ppermute | solution.py:245
  60.0 5.2 %collective-permute-start.15 = (bf16[64,640]{1,0:T(8,128)(2,1)S(1)}, bf16[64,640]{1,0:T(8,128)(2,1)S(1)}, u32[]{:S(2)}, u32[]{:S(2)}) collective-permute-start(bf16[64,640]{1,0:T(8,128)(2,1)S(1)} %add_convert_fusion.refs_0_), channel_id=1, source_target_pairs={{0,4},{2,6},{4,0},{6,2},{8,12},{10,14},{12,8},{14,10},{1,5},{3,7},... | collective-permute-start | bytes 245768 | tf_op jit(solution)/shard_map/ppermute | solution.py:242
  60.8 8.1 %collective-permute-start.17 = (bf16[64,640]{1,0:T(8,128)(2,1)S(1)}, bf16[64,640]{1,0:T(8,128)(2,1)S(1)}, u32[]{:S(2)}, u32[]{:S(2)}) collective-permute-start(bf16[64,640]{1,0:T(8,128)(2,1)S(1)} %add_convert_fusion.refs_0_), channel_id=1, source_target_pairs={{0,8},{2,10},{4,12},{6,14},{8,0},{10,2},{12,4},{14,6},{1,9},{3,11}... | collective-permute-start | bytes 245768 | tf_op jit(solution)/shard_map/ppermute | solution.py:242
  64.2 6.3 %collective-permute-start.19 = (bf16[64,640]{1,0:T(8,128)(2,1)S(1)}, bf16[64,640]{1,0:T(8,128)(2,1)S(1)}, u32[]{:S(2)}, u32[]{:S(2)}) collective-permute-start(bf16[64,640]{1,0:T(8,128)(2,1)S(1)} %add_convert_fusion.refs_0_), channel_id=1, source_target_pairs={{0,12},{2,14},{4,8},{6,10},{8,4},{10,6},{12,0},{14,2},{1,13},{3,15... | collective-permute-start | bytes 245768 | tf_op jit(solution)/shard_map/ppermute | solution.py:242
  64.9 5.7 %collective-permute-start.14 = (bf16[64,640]{1,0:T(8,128)(2,1)S(1)}, bf16[64,640]{1,0:T(8,128)(2,1)S(1)}, u32[]{:S(2)}, u32[]{:S(2)}) collective-permute-start(bf16[64,640]{1,0:T(8,128)(2,1)S(1)} %add_convert_fusion.refs_0_), channel_id=1, source_target_pairs={{0,2},{2,0},{4,6},{6,4},{8,10},{10,8},{12,14},{14,12},{1,3},{3,1},... | collective-permute-start | bytes 245768 | tf_op jit(solution)/shard_map/ppermute | solution.py:242
  65.2 5.4 %collective-permute-start.16 = (bf16[64,640]{1,0:T(8,128)(2,1)S(1)}, bf16[64,640]{1,0:T(8,128)(2,1)S(1)}, u32[]{:S(2)}, u32[]{:S(2)}) collective-permute-start(bf16[64,640]{1,0:T(8,128)(2,1)S(1)} %collective-permute-done.15.refs_2_), channel_id=1, source_target_pairs={{0,2},{2,0},{4,6},{6,4},{8,10},{10,8},{12,14},{14,12},{1,3},{3,1},... | collective-permute-start | bytes 245768 | tf_op jit(solution)/shard_map/ppermute | solution.py:242
  68.9 1.7 %collective-permute-start.18 = (bf16[64,640]{1,0:T(8,128)(2,1)S(1)}, bf16[64,640]{1,0:T(8,128)(2,1)S(1)}, u32[]{:S(2)}, u32[]{:S(2)}) collective-permute-start(bf16[64,640]{1,0:T(8,128)(2,1)S(1)} %collective-permute-done.17.refs_4_), channel_id=1, source_target_pairs={{0,2},{2,0},{4,6},{6,4},{8,10},{10,8},{12,14},{14,12},{1,3},{3,1},... | collective-permute-start | bytes 245768 | tf_op jit(solution)/shard_map/ppermute | solution.py:242
  70.5 1.3 %collective-permute-start.20 = (bf16[64,640]{1,0:T(8,128)(2,1)S(1)}, bf16[64,640]{1,0:T(8,128)(2,1)S(1)}, u32[]{:S(2)}, u32[]{:S(2)}) collective-permute-start(bf16[64,640]{1,0:T(8,128)(2,1)S(1)} %collective-permute-done.19.refs_6_), channel_id=1, source_target_pairs={{0,2},{2,0},{4,6},{6,4},{8,10},{10,8},{12,14},{14,12},{1,3},{3,1},... | collective-permute-start | bytes 245768 | tf_op jit(solution)/shard_map/ppermute | solution.py:242

commit v5 on v4

--- a/solution.py
+++ b/solution.py
@@ -16,6 +16,7 @@
 VMEM_BYTES = 40 * 1024 * 1024
 OWN_FLOPS, EARLY_FLOPS, PAIR_FLOPS, LATE_FLOPS, FINISH_FLOPS = 0, 0, 0, 4_000_000_000, 1_000_000_000
 EARLY_LEAD = 4
+SEATS = (0, 1, 4, 5, 6, 7, 2, 3)
 
 power_eps = 1e-06
 
@@ -202,7 +203,7 @@
     rows, span = pieces[0].shape[0], table.shape[0] // 2
     for d in range(8):
         half, chip, core = place[0] ^ (d >> 2), place[1] ^ ((d >> 1) & 1), place[2] ^ (d & 1)
-        mine, other = pieces[d], pieces[d ^ 4]
+        mine, other = pieces[SEATS.index(d)], pieces[SEATS.index(d ^ 4)]
         at = block(4 * half + 2 * core + chip, rows)
         extra = spread(other[:, 2 * span :].astype(jnp.float32), 1 - chip)
         table[at, block(half, span)] = (mine[:, :span].astype(jnp.float32) + extra).astype(jnp.bfloat16)
@@ -246,10 +247,10 @@
         return (value.astype(jnp.float32) + other.astype(jnp.float32)).astype(bf16)
 
     def everyone(value):
-        s4, s2 = tm_swap(value, 4), tm_swap(value, 2)
-        s6 = tm_swap(value, 6)
-        z = (value, s2, s4, s6)
-        return [v for pair in zip(z, [tm_swap(v, 1) for v in z]) for v in pair]
+        return [v for bits in SEATS[::2] for v in with_core(value if bits == 0 else tm_swap(value, bits))]
+
+    def with_core(value):
+        return value, tm_swap(value, 1)
 
     def cut(source, start, count):
         return lax.optimization_barrier((source, lax.dynamic_slice_in_dim(source, start, count, 1)))

time: 75.6 us -> 74.2 us (0.981)
  waiting for transfers between devices: 41.4 us -> 40 us
    ppermute x20, waiting for transfers between devices: 40.3 us -> 38.9 us  [tm_swap(): return lax.ppermute(value, 'tm', [(i, i ^ bit) for i in range(n)])]
where the time goes in v5:
time: 74.2 us; the launch traced here: 74.1 us
  waiting for transfers between devices  40 us (54%)
  starting transfers between devices  19.4 us (26%)
  Pallas kernels  9.19 us (12%)
  other arithmetic  2.58 us (3%)
  local copies, waits for them, and re-layouts  1.89 us (3%)
  between operations  0.96 us (1%)
    ppermute x20, waiting for transfers between devices, tm_swap(): return lax.ppermute(value, 'tm', [(i, i ^ bit) for i in range(n)])  38.9 us
    ppermute x20, starting transfers between devices, tm_swap(): return lax.ppermute(value, 'tm', [(i, i ^ bit) for i in range(n)])  17.9 us
    pallas_call x5, Pallas kernels, call(): pl.pallas_call(kernel, out_shape=[jax.ShapeDtypeStruct(shape, kind) for s...  9.19 us
    unnamed x16, local copies, waits for them, and re-layouts  1.62 us
    ppermute x1, starting transfers between devices, pix_sum(): other = lax.ppermute(value, 'pix', [(0, 1), (1, 0)])  1.56 us
  transfers between devices with their start and end apart: 21, of which 10 were waited for; matrix products, arithmetic and copies ran while one was open for 4% of the time, Pallas kernels for 5%

profile of v5, /device:TPU:0, one launch (start us, length us, event | category | flops | bytes accessed | tf_op | source)
XLA Modules:
  0.0 74.1 jit_solution(13824749361502377497)
XLA Ops:
  0.6 0.0 copy-start
  0.7 1.6 %copy-done = bf16[64,16384]{1,0:T(8,128)(2,1)S(1)} copy-done((bf16[64,16384]{1,0:T(8,128)(2,1)S(1)}, bf16[64,16384]{1,0:T(8,128)(2,1)}, u32[]{:S(2)}) %copy-start) | copy-done | bytes 2097176
  2.3 0.5 collective-permute-start
  2.8 4.7 %collective-permute-start.6 = (bf16[64,1024]{1,0:T(8,128)(2,1)S(1)}, bf16[64,1024]{1,0:T(8,128)(2,1)S(1)}, u32[]{:S(2)}, u32[]{:S(2)}) collective-permute-start(bf16[64,1024]{1,0:T(8,128)(2,1)S(1)} %constant_dynamic-slice_fusion.6), channel_id=1, source_target_pairs={{0,12},{2,14},{4,8},{6,10},{8,4},{10,6},{12,0},{14,2},{1,13},{3,15... | collective-permute-start | bytes 393224 | tf_op jit(solution)/shard_map/ppermute | solution.py:243
  7.6 0.0 copy-start.1
  7.6 0.0 copy-start.2
  7.6 0.0 copy-start.3
  7.7 0.1 collective-permute-start.2
  7.8 2.0 %collective-permute-start.1 = (bf16[64,2048]{1,0:T(8,128)(2,1)S(1)}, bf16[64,2048]{1,0:T(8,128)(2,1)S(1)}, u32[]{:S(2)}, u32[]{:S(2)}) collective-permute-start(bf16[64,2048]{1,0:T(8,128)(2,1)S(1)} %constant_dynamic-slice_fusion.4), channel_id=1, source_target_pairs={{0,4},{2,6},{4,0},{6,2},{8,12},{10,14},{12,8},{14,10},{1,5},{3,7},... | collective-permute-start | bytes 786440 | tf_op jit(solution)/shard_map/ppermute | solution.py:243
  9.8 0.1 constant_dynamic-slice_fusion.1.far
  9.9 0.1 collective-permute-start.5
  9.9 1.9 %collective-permute-start.8 = (bf16[64,3072]{1,0:T(8,128)(2,1)S(1)}, bf16[64,3072]{1,0:T(8,128)(2,1)S(1)}, u32[]{:S(2)}, u32[]{:S(2)}) collective-permute-start(bf16[64,3072]{1,0:T(8,128)(2,1)S(1)} %constant_dynamic-slice_fusion.5), channel_id=1, source_target_pairs={{0,12},{2,14},{4,8},{6,10},{8,4},{10,6},{12,0},{14,2},{1,13},{3,15... | collective-permute-start | bytes 1179656 | tf_op jit(solution)/shard_map/ppermute | solution.py:243
  11.8 5.6 %collective-permute-done.2.p2b = bf16[64,2048]{1,0:T(8,128)(2,1)S(1)} collective-permute-done((bf16[64,2048]{1,0:T(8,128)(2,1)S(1)}, bf16[64,2048]{1,0:T(8,128)(2,1)S(1)}, u32[]{:S(2)}, u32[]{:S(2)}) %collective-permute-start.2) | collective-permute-done | bytes 262176 | tf_op jit(solution)/shard_map/ppermute | solution.py:243
  17.4 5.8 %collective-permute-done.1.p2a = bf16[64,2048]{1,0:T(8,128)(2,1)S(1)} collective-permute-done((bf16[64,2048]{1,0:T(8,128)(2,1)S(1)}, bf16[64,2048]{1,0:T(8,128)(2,1)S(1)}, u32[]{:S(2)}, u32[]{:S(2)}) %collective-permute-start.1) | collective-permute-done | bytes 262176 | tf_op jit(solution)/shard_map/ppermute | solution.py:243
  23.2 0.0 collective-permute-start.3
  23.2 0.0 copy-start.4
  23.3 1.4 %collective-permute-start.7 = (bf16[64,4096]{1,0:T(8,128)(2,1)S(1)}, bf16[64,4096]{1,0:T(8,128)(2,1)S(1)}, u32[]{:S(2)}, u32[]{:S(2)}) collective-permute-start(bf16[64,4096]{1,0:T(8,128)(2,1)S(1)} %constant_dynamic-slice_fusion), channel_id=1, source_target_pairs={{0,8},{2,10},{4,12},{6,14},{8,0},{10,2},{12,4},{14,6},{1,9},{3,11}... | collective-permute-start | bytes 1572872 | tf_op jit(solution)/shard_map/ppermute | solution.py:243
  24.7 0.1 pad_add_fusion.place
  24.8 6.9 %collective-permute-done.8.e0b.eb = bf16[64,3072]{1,0:T(8,128)(2,1)S(1)} collective-permute-done((bf16[64,3072]{1,0:T(8,128)(2,1)S(1)}, bf16[64,3072]{1,0:T(8,128)(2,1)S(1)}, u32[]{:S(2)}, u32[]{:S(2)}) %collective-permute-start.8) | collective-permute-done | bytes 393248 | tf_op jit(solution)/shard_map/ppermute | solution.py:243
  31.7 2.0 %shard_map.95 = (bf16[256,4096]{1,0:T(8,128)(2,1)S(1)}, f32[64,256]{1,0:T(8,128)S(1)}, bf16[64,256]{1,0:T(8,128)(2,1)S(1)}) custom-call(s32[3]{0:T(128)S(1)} %pad_add_fusion.place, bf16[64,4096]{1,0:T(8,128)(2,1)S(1)} %constant_dynamic-slice_fusion.7.p0, bf16[64,4096]{1,0:T(8,128)(2,1)S(1)} %collective-permute-done.p1, ...), custom_call_target="tpu_custom_call" | custom-call | tf_op jit(solution)/shard_map/pallas_call | solution.py:286
  33.7 0.1 collective-permute-start.12
  33.8 0.2 fusion.26
  34.0 0.6 collective-permute-start.9
  34.6 1.3 %shard_map.97 = bf16[64,256]{1,0:T(8,128)(2,1)S(1)} custom-call(s32[3]{0:T(128)S(1)} %pad_add_fusion.place, bf16[256,4096]{1,0:T(8,128)(2,1)S(1)} %get-tuple-element.46.near, bf16[64,1024]{1,0:T(8,128)(2,1)S(1)} %collective-permute-done.6.e0a.ea, bf16[64,3072]{1,0:T(8,128)(2,1)S(1)} %collective-permute-done.8.e0b.eb, f32[1,256]{1,0:T(1,128)S(1)} %copy-done.2, ...), custom_call_target="tpu_custom_call" | custom-call | tf_op jit(solution)/shard_map/pallas_call | solution.py:286
  35.9 1.8 %collective-permute-start.11 = (bf16[64,256]{1,0:T(8,128)(2,1)S(1)}, bf16[64,256]{1,0:T(8,128)(2,1)S(1)}, u32[]{:S(2)}, u32[]{:S(2)}) collective-permute-start(bf16[64,256]{1,0:T(8,128)(2,1)S(1)} %shard_map.97), channel_id=1, source_target_pairs={{0,4},{2,6},{4,0},{6,2},{8,12},{10,14},{12,8},{14,10},{1,5},{3,7},... | collective-permute-start | bytes 98312 | tf_op jit(solution)/shard_map/ppermute | solution.py:243
  37.6 5.3 %collective-permute-done.12 = bf16[64,256]{1,0:T(8,128)(2,1)S(1)} collective-permute-done((bf16[64,256]{1,0:T(8,128)(2,1)S(1)}, bf16[64,256]{1,0:T(8,128)(2,1)S(1)}, u32[]{:S(2)}, u32[]{:S(2)}) %collective-permute-start.12) | collective-permute-done | bytes 32800 | tf_op jit(solution)/shard_map/ppermute | solution.py:243
  43.0 0.6 shard_map.96.pair
  43.6 0.0 copy-start.7
  43.6 10.2 %collective-permute-done.7.late = bf16[64,4096]{1,0:T(8,128)(2,1)S(1)} collective-permute-done((bf16[64,4096]{1,0:T(8,128)(2,1)S(1)}, bf16[64,4096]{1,0:T(8,128)(2,1)S(1)}, u32[]{:S(2)}, u32[]{:S(2)}) %collective-permute-start.7) | collective-permute-done | bytes 524320 | tf_op jit(solution)/shard_map/ppermute | solution.py:243
  53.8 1.6 %shard_map.98 = bf16[64,384]{1,0:T(8,128)(2,1)S(1)} custom-call(s32[3]{0:T(128)S(1)} %pad_add_fusion.place, bf16[256,4096]{1,0:T(8,128)(2,1)S(1)} %get-tuple-element.46.near, bf16[64,4096]{1,0:T(8,128)(2,1)S(1)} %collective-permute-done.7.late, bf16[128,4096]{1,0:T(8,128)(2,1)S(1)} %shard_map.96.pair, bf16[64,256]{1,0:T(8,128)(2,1)S(1)} %collective-permute-done.11.before, ...), custom_call_target="tpu_custom_call" | custom-call | flops 4000000000 | tf_op jit(solution)/shard_map/pallas_call | solution.py:286
  55.5 1.6 %collective-permute-start.13 = (bf16[64,640]{1,0:T(8,128)(2,1)S(1)}, bf16[64,640]{1,0:T(8,128)(2,1)S(1)}, u32[]{:S(2)}, u32[]{:S(2)}) collective-permute-start(bf16[64,640]{1,0:T(8,128)(2,1)S(1)} %pad_maximum_fusion.1), channel_id=1, source_target_pairs={{0,1},{1,0},{2,3},{3,2},{4,5},{5,4},{6,7},{7,6},{8,9},{9,8},{10,11... | collective-permute-start | bytes 245768 | tf_op jit(solution)/shard_map/ppermute | solution.py:246
  57.0 0.9 %multiply_reduce_fusion = f32[32]{0:T(128)S(1)} fusion(pred[32]{0:T(512)(128)(4,1)S(1)} %get-tuple-element.71, pred[32]{0:T(512)(128)(4,1)S(1)} %get-tuple-element.72, pred[32]{0:T(512)(128)(4,1)S(1)} %get-tuple-element.73, pred[32]{0:T(512)(128)(4,1)S(1)} %get-tuple-element.70, s32[32]{0:T(128)S(1)} %copy-done.6, s32[512]{0:T(512)S(1)} %copy-done.4), kind=kLoop, calls=%fused_computation.32 | loop fusion | flops 425952 | bytes 2432 | tf_op jit(solution)/shard_map/reduce_sum | solution.py:122
  57.9 0.8 %multiply_multiply_fusion = f32[32,512]{1,0:T(8,128)S(1)} fusion(f32[512]{0:T(512)S(1)} %copy-done.7, f32[32]{0:T(128)S(1)} %sqrt.3, pred[32]{0:T(512)(128)(4,1)S(1)} %get-tuple-element.71, pred[32]{0:T(512)(128)(4,1)S(1)} %get-tuple-element.72, pred[32]{0:T(512)(128)(4,1)S(1)} %get-tuple-element.73, pred[32]{0:T(512)(128)(4,1)S(1)} %get-tuple-element.70, ...), kind=kLoop, calls=%fused_computation.31 | loop fusion | flops 425984 | bytes 70016 | tf_op jit(solution)/shard_map/mul | solution.py:124
  58.7 0.1 fusion.31
  58.8 1.1 %collective-permute-done.13 = bf16[64,640]{1,0:T(8,128)(2,1)S(1)} collective-permute-done((bf16[64,640]{1,0:T(8,128)(2,1)S(1)}, bf16[64,640]{1,0:T(8,128)(2,1)S(1)}, u32[]{:S(2)}, u32[]{:S(2)}) %collective-permute-start.13) | collective-permute-done | bytes 81952 | tf_op jit(solution)/shard_map/ppermute | solution.py:246
  60.0 0.1 collective-permute-start.15
  60.1 3.6 %collective-permute-start.17 = (bf16[64,640]{1,0:T(8,128)(2,1)S(1)}, bf16[64,640]{1,0:T(8,128)(2,1)S(1)}, u32[]{:S(2)}, u32[]{:S(2)}) collective-permute-start(bf16[64,640]{1,0:T(8,128)(2,1)S(1)} %add_convert_fusion.refs_0_), channel_id=1, source_target_pairs={{0,12},{2,14},{4,8},{6,10},{8,4},{10,6},{12,0},{14,2},{1,13},{3,15... | collective-permute-start | bytes 245768 | tf_op jit(solution)/shard_map/ppermute | solution.py:243
  63.7 0.5 collective-permute-start.19
  64.2 0.4 multiply_convert_fusion.1
  64.6 0.1 collective-permute-start.14
  64.7 4.0 %collective-permute-done.15.refs_2_ = bf16[64,640]{1,0:T(8,128)(2,1)S(1)} collective-permute-done((bf16[64,640]{1,0:T(8,128)(2,1)S(1)}, bf16[64,640]{1,0:T(8,128)(2,1)S(1)}, u32[]{:S(2)}, u32[]{:S(2)}) %collective-permute-start.15) | collective-permute-done | bytes 81952 | tf_op jit(solution)/shard_map/ppermute | solution.py:243
  68.6 0.5 collective-permute-start.18
  69.1 0.1 collective-permute-start.20
  69.2 0.1 pad_maximum_fusion.w
  69.3 0.6 collective-permute-done.16.refs_3_
  69.9 0.2 collective-permute-done.18.refs_5_
  70.1 0.4 collective-permute-done.20.refs_7_
  70.4 3.7 %shard_map.99 = (f32[16,64,64]{2,1,0:T(8,128)}, f32[1,16]{1,0:T(1,128)}) custom-call(s32[3]{0:T(128)S(1)} %pad_add_fusion.place, bf16[16,64,512]{2,1,0:T(8,128)(2,1)S(1)} %pad_maximum_fusion.w, bf16[64,640]{1,0:T(8,128)(2,1)S(1)} %add_convert_fusion.refs_0_, bf16[64,640]{1,0:T(8,128)(2,1)S(1)} %collective-permute-done.14.refs_1_, ...), custom_call_target="tpu_custom_call" | custom-call | flops 1000000000 | tf_op jit(solution)/shard_map/pallas_call | solution.py:286
  (36 shorter events, 0.3 us)
Async XLA Ops:
  0.6 1.6 %copy-start = (bf16[64,16384]{1,0:T(8,128)(2,1)S(1)}, bf16[64,16384]{1,0:T(8,128)(2,1)}, u32[]{:S(2)}) copy-start(bf16[64,16384]{1,0:T(8,128)(2,1)} %param.8) | copy-start | bytes 6291460
  2.3 5.2 %collective-permute-start = (bf16[64,4096]{1,0:T(8,128)(2,1)S(1)}, bf16[64,4096]{1,0:T(8,128)(2,1)S(1)}, u32[]{:S(2)}, u32[]{:S(2)}) collective-permute-start(bf16[64,4096]{1,0:T(8,128)(2,1)S(1)} %constant_dynamic-slice_fusion.7.p0), channel_id=1, source_target_pairs={{0,2},{2,0},{4,6},{6,4},{8,10},{10,8},{12,14},{14,12},{1,3},{3,1},... | collective-permute-start | bytes 1572872 | tf_op jit(solution)/shard_map/ppermute | solution.py:243
  2.8 20.5 %collective-permute-start.6 = (bf16[64,1024]{1,0:T(8,128)(2,1)S(1)}, bf16[64,1024]{1,0:T(8,128)(2,1)S(1)}, u32[]{:S(2)}, u32[]{:S(2)}) collective-permute-start(bf16[64,1024]{1,0:T(8,128)(2,1)S(1)} %constant_dynamic-slice_fusion.6), channel_id=1, source_target_pairs={{0,12},{2,14},{4,8},{6,10},{8,4},{10,6},{12,0},{14,2},{1,13},{3,15... | collective-permute-start | bytes 393224 | tf_op jit(solution)/shard_map/ppermute | solution.py:243
  7.6 24.1 %copy-start.1 = (f32[256,1]{1,0:T(8,128)S(1)}, f32[256,1]{1,0:T(8,128)}, u32[]{:S(2)}) copy-start(f32[256,1]{1,0:T(8,128)} %constant.126.clone.dcol) | copy-start | bytes 3076
  7.6 24.1 %copy-start.2 = (f32[1,256]{1,0:T(1,128)S(1)}, f32[1,256]{1,0:T(1,128)}, u32[]{:S(2)}) copy-start(f32[1,256]{1,0:T(1,128)} %constant.125.clone.drow) | copy-start | bytes 3076
  7.6 24.1 %copy-start.3 = (f32[2,1,128]{2,1,0:T(1,128)S(1)}, f32[2,1,128]{2,1,0:T(1,128)}, u32[]{:S(2)}) copy-start(f32[2,1,128]{2,1,0:T(1,128)} %constant.127.clone.dpair) | copy-start | bytes 3076
  7.7 9.7 %collective-permute-start.2 = (bf16[64,2048]{1,0:T(8,128)(2,1)S(1)}, bf16[64,2048]{1,0:T(8,128)(2,1)S(1)}, u32[]{:S(2)}, u32[]{:S(2)}) collective-permute-start(bf16[64,2048]{1,0:T(8,128)(2,1)S(1)} %constant_dynamic-slice_fusion.3), channel_id=1, source_target_pairs={{0,4},{2,6},{4,0},{6,2},{8,12},{10,14},{12,8},{14,10},{1,5},{3,7},... | collective-permute-start | bytes 786440 | tf_op jit(solution)/shard_map/ppermute | solution.py:243
  7.8 15.4 %collective-permute-start.1 = (bf16[64,2048]{1,0:T(8,128)(2,1)S(1)}, bf16[64,2048]{1,0:T(8,128)(2,1)S(1)}, u32[]{:S(2)}, u32[]{:S(2)}) collective-permute-start(bf16[64,2048]{1,0:T(8,128)(2,1)S(1)} %constant_dynamic-slice_fusion.4), channel_id=1, source_target_pairs={{0,4},{2,6},{4,0},{6,2},{8,12},{10,14},{12,8},{14,10},{1,5},{3,7},... | collective-permute-start | bytes 786440 | tf_op jit(solution)/shard_map/ppermute | solution.py:243
  9.9 21.8 %collective-permute-start.5 = (bf16[64,4096]{1,0:T(8,128)(2,1)S(1)}, bf16[64,4096]{1,0:T(8,128)(2,1)S(1)}, u32[]{:S(2)}, u32[]{:S(2)}) collective-permute-start(bf16[64,4096]{1,0:T(8,128)(2,1)S(1)} %constant_dynamic-slice_fusion.2), channel_id=1, source_target_pairs={{0,2},{2,0},{4,6},{6,4},{8,10},{10,8},{12,14},{14,12},{1,3},{3,1},... | collective-permute-start | bytes 1572872 | tf_op jit(solution)/shard_map/ppermute | solution.py:243
  9.9 21.7 %collective-permute-start.8 = (bf16[64,3072]{1,0:T(8,128)(2,1)S(1)}, bf16[64,3072]{1,0:T(8,128)(2,1)S(1)}, u32[]{:S(2)}, u32[]{:S(2)}) collective-permute-start(bf16[64,3072]{1,0:T(8,128)(2,1)S(1)} %constant_dynamic-slice_fusion.5), channel_id=1, source_target_pairs={{0,12},{2,14},{4,8},{6,10},{8,4},{10,6},{12,0},{14,2},{1,13},{3,15... | collective-permute-start | bytes 1179656 | tf_op jit(solution)/shard_map/ppermute | solution.py:243
  17.4 14.2 %collective-permute-start.4 = (bf16[64,2048]{1,0:T(8,128)(2,1)S(1)}, bf16[64,2048]{1,0:T(8,128)(2,1)S(1)}, u32[]{:S(2)}, u32[]{:S(2)}) collective-permute-start(bf16[64,2048]{1,0:T(8,128)(2,1)S(1)} %collective-permute-done.2.p2b), channel_id=1, source_target_pairs={{0,2},{2,0},{4,6},{6,4},{8,10},{10,8},{12,14},{14,12},{1,3},{3,1},... | collective-permute-start | bytes 786440 | tf_op jit(solution)/shard_map/ppermute | solution.py:243
  23.2 8.5 %collective-permute-start.3 = (bf16[64,2048]{1,0:T(8,128)(2,1)S(1)}, bf16[64,2048]{1,0:T(8,128)(2,1)S(1)}, u32[]{:S(2)}, u32[]{:S(2)}) collective-permute-start(bf16[64,2048]{1,0:T(8,128)(2,1)S(1)} %collective-permute-done.1.p2a), channel_id=1, source_target_pairs={{0,2},{2,0},{4,6},{6,4},{8,10},{10,8},{12,14},{14,12},{1,3},{3,1},... | collective-permute-start | bytes 786440 | tf_op jit(solution)/shard_map/ppermute | solution.py:243
  23.2 10.5 %copy-start.4 = (s32[512]{0:T(512)S(1)}, s32[512]{0:T(512)}, u32[]{:S(2)}) copy-start(s32[512]{0:T(512)} %constant.128.clone) | copy-start | bytes 6148
  23.3 30.5 %collective-permute-start.7 = (bf16[64,4096]{1,0:T(8,128)(2,1)S(1)}, bf16[64,4096]{1,0:T(8,128)(2,1)S(1)}, u32[]{:S(2)}, u32[]{:S(2)}) collective-permute-start(bf16[64,4096]{1,0:T(8,128)(2,1)S(1)} %constant_dynamic-slice_fusion), channel_id=1, source_target_pairs={{0,8},{2,10},{4,12},{6,14},{8,0},{10,2},{12,4},{14,6},{1,9},{3,11}... | collective-permute-start | bytes 1572872 | tf_op jit(solution)/shard_map/ppermute | solution.py:243
  31.6 11.3 %collective-permute-start.10 = (bf16[64,3072]{1,0:T(8,128)(2,1)S(1)}, bf16[64,3072]{1,0:T(8,128)(2,1)S(1)}, u32[]{:S(2)}, u32[]{:S(2)}) collective-permute-start(bf16[64,3072]{1,0:T(8,128)(2,1)S(1)} %collective-permute-done.8.e0b.eb), channel_id=1, source_target_pairs={{0,2},{2,0},{4,6},{6,4},{8,10},{10,8},{12,14},{14,12},{1,3},{3,1},... | collective-permute-start | bytes 1179656 | tf_op jit(solution)/shard_map/ppermute | solution.py:243
  33.7 9.3 %collective-permute-start.12 = (bf16[64,256]{1,0:T(8,128)(2,1)S(1)}, bf16[64,256]{1,0:T(8,128)(2,1)S(1)}, u32[]{:S(2)}, u32[]{:S(2)}) collective-permute-start(bf16[64,256]{1,0:T(8,128)(2,1)S(1)} %get-tuple-element.60), channel_id=1, source_target_pairs={{0,4},{2,6},{4,0},{6,2},{8,12},{10,14},{12,8},{14,10},{1,5},{3,7},... | collective-permute-start | bytes 98312 | tf_op jit(solution)/shard_map/ppermute | solution.py:243
  34.0 9.0 %collective-permute-start.9 = (bf16[64,1024]{1,0:T(8,128)(2,1)S(1)}, bf16[64,1024]{1,0:T(8,128)(2,1)S(1)}, u32[]{:S(2)}, u32[]{:S(2)}) collective-permute-start(bf16[64,1024]{1,0:T(8,128)(2,1)S(1)} %collective-permute-done.6.e0a.ea), channel_id=1, source_target_pairs={{0,2},{2,0},{4,6},{6,4},{8,10},{10,8},{12,14},{14,12},{1,3},{3,1},... | collective-permute-start | bytes 393224 | tf_op jit(solution)/shard_map/ppermute | solution.py:243
  35.9 18.0 %collective-permute-start.11 = (bf16[64,256]{1,0:T(8,128)(2,1)S(1)}, bf16[64,256]{1,0:T(8,128)(2,1)S(1)}, u32[]{:S(2)}, u32[]{:S(2)}) collective-permute-start(bf16[64,256]{1,0:T(8,128)(2,1)S(1)} %shard_map.97), channel_id=1, source_target_pairs={{0,4},{2,6},{4,0},{6,2},{8,12},{10,14},{12,8},{14,10},{1,5},{3,7},... | collective-permute-start | bytes 98312 | tf_op jit(solution)/shard_map/ppermute | solution.py:243
  43.6 13.4 %copy-start.5 = (s32[32]{0:T(128)S(1)}, s32[32]{0:T(128)}, u32[]{:S(2)}) copy-start(s32[32]{0:T(128)} %param.10) | copy-start | bytes 388
  43.6 13.4 %copy-start.6 = (s32[32]{0:T(128)S(1)}, s32[32]{0:T(128)}, u32[]{:S(2)}) copy-start(s32[32]{0:T(128)} %param.9) | copy-start | bytes 388
  43.6 14.3 %copy-start.7 = (f32[512]{0:T(512)S(1)}, f32[512]{0:T(512)}, u32[]{:S(2)}) copy-start(f32[512]{0:T(512)} %constant.130) | copy-start | bytes 6148
  55.5 4.5 %collective-permute-start.13 = (bf16[64,640]{1,0:T(8,128)(2,1)S(1)}, bf16[64,640]{1,0:T(8,128)(2,1)S(1)}, u32[]{:S(2)}, u32[]{:S(2)}) collective-permute-start(bf16[64,640]{1,0:T(8,128)(2,1)S(1)} %pad_maximum_fusion.1), channel_id=1, source_target_pairs={{0,1},{1,0},{2,3},{3,2},{4,5},{5,4},{6,7},{7,6},{8,9},{9,8},{10,11... | collective-permute-start | bytes 245768 | tf_op jit(solution)/shard_map/ppermute | solution.py:246
  60.0 8.6 %collective-permute-start.15 = (bf16[64,640]{1,0:T(8,128)(2,1)S(1)}, bf16[64,640]{1,0:T(8,128)(2,1)S(1)}, u32[]{:S(2)}, u32[]{:S(2)}) collective-permute-start(bf16[64,640]{1,0:T(8,128)(2,1)S(1)} %add_convert_fusion.refs_0_), channel_id=1, source_target_pairs={{0,8},{2,10},{4,12},{6,14},{8,0},{10,2},{12,4},{14,6},{1,9},{3,11}... | collective-permute-start | bytes 245768 | tf_op jit(solution)/shard_map/ppermute | solution.py:243
  60.1 8.5 %collective-permute-start.17 = (bf16[64,640]{1,0:T(8,128)(2,1)S(1)}, bf16[64,640]{1,0:T(8,128)(2,1)S(1)}, u32[]{:S(2)}, u32[]{:S(2)}) collective-permute-start(bf16[64,640]{1,0:T(8,128)(2,1)S(1)} %add_convert_fusion.refs_0_), channel_id=1, source_target_pairs={{0,12},{2,14},{4,8},{6,10},{8,4},{10,6},{12,0},{14,2},{1,13},{3,15... | collective-permute-start | bytes 245768 | tf_op jit(solution)/shard_map/ppermute | solution.py:243
  63.7 5.5 %collective-permute-start.19 = (bf16[64,640]{1,0:T(8,128)(2,1)S(1)}, bf16[64,640]{1,0:T(8,128)(2,1)S(1)}, u32[]{:S(2)}, u32[]{:S(2)}) collective-permute-start(bf16[64,640]{1,0:T(8,128)(2,1)S(1)} %add_convert_fusion.refs_0_), channel_id=1, source_target_pairs={{0,4},{2,6},{4,0},{6,2},{8,12},{10,14},{12,8},{14,10},{1,5},{3,7},... | collective-permute-start | bytes 245768 | tf_op jit(solution)/shard_map/ppermute | solution.py:243
  64.6 4.7 %collective-permute-start.14 = (bf16[64,640]{1,0:T(8,128)(2,1)S(1)}, bf16[64,640]{1,0:T(8,128)(2,1)S(1)}, u32[]{:S(2)}, u32[]{:S(2)}) collective-permute-start(bf16[64,640]{1,0:T(8,128)(2,1)S(1)} %add_convert_fusion.refs_0_), channel_id=1, source_target_pairs={{0,2},{2,0},{4,6},{6,4},{8,10},{10,8},{12,14},{14,12},{1,3},{3,1},... | collective-permute-start | bytes 245768 | tf_op jit(solution)/shard_map/ppermute | solution.py:243
  68.6 1.3 %collective-permute-start.16 = (bf16[64,640]{1,0:T(8,128)(2,1)S(1)}, bf16[64,640]{1,0:T(8,128)(2,1)S(1)}, u32[]{:S(2)}, u32[]{:S(2)}) collective-permute-start(bf16[64,640]{1,0:T(8,128)(2,1)S(1)} %collective-permute-done.15.refs_2_), channel_id=1, source_target_pairs={{0,2},{2,0},{4,6},{6,4},{8,10},{10,8},{12,14},{14,12},{1,3},{3,1},... | collective-permute-start | bytes 245768 | tf_op jit(solution)/shard_map/ppermute | solution.py:243
  68.6 1.4 %collective-permute-start.18 = (bf16[64,640]{1,0:T(8,128)(2,1)S(1)}, bf16[64,640]{1,0:T(8,128)(2,1)S(1)}, u32[]{:S(2)}, u32[]{:S(2)}) collective-permute-start(bf16[64,640]{1,0:T(8,128)(2,1)S(1)} %collective-permute-done.17.refs_4_), channel_id=1, source_target_pairs={{0,2},{2,0},{4,6},{6,4},{8,10},{10,8},{12,14},{14,12},{1,3},{3,1},... | collective-permute-start | bytes 245768 | tf_op jit(solution)/shard_map/ppermute | solution.py:243
  69.1 1.3 %collective-permute-start.20 = (bf16[64,640]{1,0:T(8,128)(2,1)S(1)}, bf16[64,640]{1,0:T(8,128)(2,1)S(1)}, u32[]{:S(2)}, u32[]{:S(2)}) collective-permute-start(bf16[64,640]{1,0:T(8,128)(2,1)S(1)} %collective-permute-done.19.refs_6_), channel_id=1, source_target_pairs={{0,2},{2,0},{4,6},{6,4},{8,10},{10,8},{12,14},{14,12},{1,3},{3,1},... | collective-permute-start | bytes 245768 | tf_op jit(solution)/shard_map/ppermute | solution.py:243

commit v6 on v5

--- a/solution.py
+++ b/solution.py
@@ -199,7 +199,7 @@
 
 
 def finish_kernel(scale, place, w, *refs):
-    pieces, (gram, energy, table, y) = refs[:8], refs[8:]
+    pieces, (gram, energy, table, y, packed) = refs[:8], refs[8:]
     rows, span = pieces[0].shape[0], table.shape[0] // 2
     for d in range(8):
         half, chip, core = place[0] ^ (d >> 2), place[1] ^ ((d >> 1) & 1), place[2] ^ (d & 1)
@@ -211,21 +211,37 @@
     freqs, width, days = w.shape
     flat = w[...].reshape(freqs * width, days)
     y[...] = jnp.dot(flat, table[...], preferred_element_type=jnp.float32).astype(jnp.bfloat16)
-    for f in range(freqs):
-        part = outer(y[f * width : (f + 1) * width, :], w[f]) * scale
-        gram[f] = part + part.T
-    g = gram[...]
-    vector = jnp.ones((freqs, 1, width), jnp.float32)
-    along = 2
+    pair = 2 * width
+    low = lax.broadcasted_iota(jnp.int32, (1, 1, pair), 2) < width
+    for k in range(freqs // 2):
+        rows_k = slice(k * pair, (k + 1) * pair)
+        part = outer(y[rows_k, :], flat[rows_k, :]) * scale
+        part = part + part.T
+        top, bottom = part[:width, :], part[width:, :]
+        packed[k] = jnp.where(low[0], top, bottom)
+        gram[2 * k] = top[:, :width]
+        gram[2 * k + 1] = pltpu.roll(bottom, width, 1)[:, :width]
+
+    def halves(value):
+        left = jnp.sum(jnp.where(low, value, 0.0), axis=2, keepdims=True)
+        return left, jnp.sum(jnp.where(low, 0.0, value), axis=2, keepdims=True)
+
+    g = packed[...]
+    vector = jnp.ones((freqs // 2, 1, pair), jnp.float32)
     for step in range(POWER + 1):
-        applied = jnp.sum(g * vector, axis=along, keepdims=True)
-        along = 3 - along
-        mean = jnp.sum(applied * applied, axis=along, keepdims=True) * (1.0 / width)
-        if step < POWER:
-            vector = applied / jnp.sqrt(mean + power_eps)
-    lane = lax.broadcasted_iota(jnp.int32, (freqs, 1, freqs), 2)
-    own = lax.broadcasted_iota(jnp.int32, (freqs, 1, freqs), 0)
-    energy[...] = jnp.sum(jnp.where(lane == own, jnp.sqrt(mean), 0.0), axis=0)
+        if step % 2 == 0:
+            applied = jnp.sum(g * vector, axis=1, keepdims=True)
+            first, second = (m * (1.0 / width) for m in halves(applied * applied))
+            vector = applied * lax.rsqrt(jnp.where(low, first, second) + power_eps)
+        else:
+            left, right = halves(g * vector)
+            first = jnp.sum(left * left, axis=1, keepdims=True) * (1.0 / width)
+            second = jnp.sum(right * right, axis=1, keepdims=True) * (1.0 / width)
+            vector = jnp.where(low, left * lax.rsqrt(first + power_eps), right * lax.rsqrt(second + power_eps))
+    lane = lax.broadcasted_iota(jnp.int32, (freqs // 2, 1, freqs), 2)
+    even = 2 * lax.broadcasted_iota(jnp.int32, (freqs // 2, 1, freqs), 0)
+    both = jnp.where(lane == even, jnp.sqrt(first), 0.0) + jnp.where(lane == even + 1, jnp.sqrt(second), 0.0)
+    energy[...] = jnp.sum(both, axis=0)
 
 
 def covariance_shards(anomaly, offsets, taper_index):
@@ -321,7 +337,11 @@
         functools.partial(finish_kernel, 1.0 / total_pixels),
         FINISH_FLOPS,
         [((freqs, gram_width, gram_width), jnp.float32), ((1, freqs), jnp.float32)],
-        [((2 * span, 2 * span), bf16), ((freqs * gram_width, 2 * span), bf16)],
+        [
+            ((2 * span, 2 * span), bf16),
+            ((freqs * gram_width, 2 * span), bf16),
+            ((freqs // 2, gram_width, 2 * gram_width), jnp.float32),
+        ],
         w, *pieces,
     )
     return gram, energy.reshape(freqs)

time: 74.2 us -> 74.1 us (level)
  no operation moved by 1% of the time
where the time goes in v6:
time: 74.1 us; the launch traced here: 73.9 us
  waiting for transfers between devices  40 us (54%)
  starting transfers between devices  19.4 us (26%)
  Pallas kernels  9.06 us (12%)
  other arithmetic  2.58 us (3%)
  local copies, waits for them, and re-layouts  1.89 us (3%)
  between operations  0.96 us (1%)
    ppermute x20, waiting for transfers between devices, tm_swap(): return lax.ppermute(value, 'tm', [(i, i ^ bit) for i in range(n)])  38.9 us
    ppermute x20, starting transfers between devices, tm_swap(): return lax.ppermute(value, 'tm', [(i, i ^ bit) for i in range(n)])  17.9 us
    pallas_call x5, Pallas kernels, call(): pl.pallas_call(kernel, out_shape=[jax.ShapeDtypeStruct(shape, kind) for s...  9.06 us
    unnamed x16, local copies, waits for them, and re-layouts  1.62 us
    ppermute x1, starting transfers between devices, pix_sum(): other = lax.ppermute(value, 'pix', [(0, 1), (1, 0)])  1.56 us
  transfers between devices with their start and end apart: 21, of which 10 were waited for; matrix products, arithmetic and copies ran while one was open for 4% of the time, Pallas kernels for 5%

profile of v6, /device:TPU:0, one launch (start us, length us, event | category | flops | bytes accessed | tf_op | source)
XLA Modules:
  0.0 73.9 jit_solution(14185521850764115206)
XLA Ops:
  0.6 0.0 copy-start
  0.7 1.6 %copy-done = bf16[64,16384]{1,0:T(8,128)(2,1)S(1)} copy-done((bf16[64,16384]{1,0:T(8,128)(2,1)S(1)}, bf16[64,16384]{1,0:T(8,128)(2,1)}, u32[]{:S(2)}) %copy-start) | copy-done | bytes 2097176
  2.3 0.5 collective-permute-start
  2.8 4.7 %collective-permute-start.6 = (bf16[64,1024]{1,0:T(8,128)(2,1)S(1)}, bf16[64,1024]{1,0:T(8,128)(2,1)S(1)}, u32[]{:S(2)}, u32[]{:S(2)}) collective-permute-start(bf16[64,1024]{1,0:T(8,128)(2,1)S(1)} %constant_dynamic-slice_fusion.6), channel_id=1, source_target_pairs={{0,12},{2,14},{4,8},{6,10},{8,4},{10,6},{12,0},{14,2},{1,13},{3,15... | collective-permute-start | bytes 393224 | tf_op jit(solution)/shard_map/ppermute | solution.py:259
  7.6 0.0 copy-start.1
  7.6 0.0 copy-start.2
  7.6 0.0 copy-start.3
  7.7 0.1 collective-permute-start.2
  7.8 2.0 %collective-permute-start.1 = (bf16[64,2048]{1,0:T(8,128)(2,1)S(1)}, bf16[64,2048]{1,0:T(8,128)(2,1)S(1)}, u32[]{:S(2)}, u32[]{:S(2)}) collective-permute-start(bf16[64,2048]{1,0:T(8,128)(2,1)S(1)} %constant_dynamic-slice_fusion.4), channel_id=1, source_target_pairs={{0,4},{2,6},{4,0},{6,2},{8,12},{10,14},{12,8},{14,10},{1,5},{3,7},... | collective-permute-start | bytes 786440 | tf_op jit(solution)/shard_map/ppermute | solution.py:259
  9.8 0.1 constant_dynamic-slice_fusion.1.far
  9.9 0.1 collective-permute-start.5
  9.9 1.9 %collective-permute-start.8 = (bf16[64,3072]{1,0:T(8,128)(2,1)S(1)}, bf16[64,3072]{1,0:T(8,128)(2,1)S(1)}, u32[]{:S(2)}, u32[]{:S(2)}) collective-permute-start(bf16[64,3072]{1,0:T(8,128)(2,1)S(1)} %constant_dynamic-slice_fusion.5), channel_id=1, source_target_pairs={{0,12},{2,14},{4,8},{6,10},{8,4},{10,6},{12,0},{14,2},{1,13},{3,15... | collective-permute-start | bytes 1179656 | tf_op jit(solution)/shard_map/ppermute | solution.py:259
  11.8 5.6 %collective-permute-done.2.p2b = bf16[64,2048]{1,0:T(8,128)(2,1)S(1)} collective-permute-done((bf16[64,2048]{1,0:T(8,128)(2,1)S(1)}, bf16[64,2048]{1,0:T(8,128)(2,1)S(1)}, u32[]{:S(2)}, u32[]{:S(2)}) %collective-permute-start.2) | collective-permute-done | bytes 262176 | tf_op jit(solution)/shard_map/ppermute | solution.py:259
  17.4 5.8 %collective-permute-done.1.p2a = bf16[64,2048]{1,0:T(8,128)(2,1)S(1)} collective-permute-done((bf16[64,2048]{1,0:T(8,128)(2,1)S(1)}, bf16[64,2048]{1,0:T(8,128)(2,1)S(1)}, u32[]{:S(2)}, u32[]{:S(2)}) %collective-permute-start.1) | collective-permute-done | bytes 262176 | tf_op jit(solution)/shard_map/ppermute | solution.py:259
  23.2 0.0 collective-permute-start.3
  23.2 0.0 copy-start.4
  23.3 1.4 %collective-permute-start.7 = (bf16[64,4096]{1,0:T(8,128)(2,1)S(1)}, bf16[64,4096]{1,0:T(8,128)(2,1)S(1)}, u32[]{:S(2)}, u32[]{:S(2)}) collective-permute-start(bf16[64,4096]{1,0:T(8,128)(2,1)S(1)} %constant_dynamic-slice_fusion), channel_id=1, source_target_pairs={{0,8},{2,10},{4,12},{6,14},{8,0},{10,2},{12,4},{14,6},{1,9},{3,11}... | collective-permute-start | bytes 1572872 | tf_op jit(solution)/shard_map/ppermute | solution.py:259
  24.7 0.1 pad_add_fusion.place
  24.8 6.9 %collective-permute-done.8.e0b.eb = bf16[64,3072]{1,0:T(8,128)(2,1)S(1)} collective-permute-done((bf16[64,3072]{1,0:T(8,128)(2,1)S(1)}, bf16[64,3072]{1,0:T(8,128)(2,1)S(1)}, u32[]{:S(2)}, u32[]{:S(2)}) %collective-permute-start.8) | collective-permute-done | bytes 393248 | tf_op jit(solution)/shard_map/ppermute | solution.py:259
  31.7 2.0 %shard_map.95 = (bf16[256,4096]{1,0:T(8,128)(2,1)S(1)}, f32[64,256]{1,0:T(8,128)S(1)}, bf16[64,256]{1,0:T(8,128)(2,1)S(1)}) custom-call(s32[3]{0:T(128)S(1)} %pad_add_fusion.place, bf16[64,4096]{1,0:T(8,128)(2,1)S(1)} %constant_dynamic-slice_fusion.7.p0, bf16[64,4096]{1,0:T(8,128)(2,1)S(1)} %collective-permute-done.p1, ...), custom_call_target="tpu_custom_call" | custom-call | tf_op jit(solution)/shard_map/pallas_call | solution.py:302
  33.7 0.1 collective-permute-start.12
  33.8 0.2 fusion.26
  34.0 0.6 collective-permute-start.9
  34.6 1.3 %shard_map.97 = bf16[64,256]{1,0:T(8,128)(2,1)S(1)} custom-call(s32[3]{0:T(128)S(1)} %pad_add_fusion.place, bf16[256,4096]{1,0:T(8,128)(2,1)S(1)} %get-tuple-element.46.near, bf16[64,1024]{1,0:T(8,128)(2,1)S(1)} %collective-permute-done.6.e0a.ea, bf16[64,3072]{1,0:T(8,128)(2,1)S(1)} %collective-permute-done.8.e0b.eb, f32[1,256]{1,0:T(1,128)S(1)} %copy-done.2, ...), custom_call_target="tpu_custom_call" | custom-call | tf_op jit(solution)/shard_map/pallas_call | solution.py:302
  35.9 1.8 %collective-permute-start.11 = (bf16[64,256]{1,0:T(8,128)(2,1)S(1)}, bf16[64,256]{1,0:T(8,128)(2,1)S(1)}, u32[]{:S(2)}, u32[]{:S(2)}) collective-permute-start(bf16[64,256]{1,0:T(8,128)(2,1)S(1)} %shard_map.97), channel_id=1, source_target_pairs={{0,4},{2,6},{4,0},{6,2},{8,12},{10,14},{12,8},{14,10},{1,5},{3,7},... | collective-permute-start | bytes 98312 | tf_op jit(solution)/shard_map/ppermute | solution.py:259
  37.6 5.3 %collective-permute-done.12 = bf16[64,256]{1,0:T(8,128)(2,1)S(1)} collective-permute-done((bf16[64,256]{1,0:T(8,128)(2,1)S(1)}, bf16[64,256]{1,0:T(8,128)(2,1)S(1)}, u32[]{:S(2)}, u32[]{:S(2)}) %collective-permute-start.12) | collective-permute-done | bytes 32800 | tf_op jit(solution)/shard_map/ppermute | solution.py:259
  43.0 0.6 shard_map.96.pair
  43.6 0.0 copy-start.7
  43.6 10.2 %collective-permute-done.7.late = bf16[64,4096]{1,0:T(8,128)(2,1)S(1)} collective-permute-done((bf16[64,4096]{1,0:T(8,128)(2,1)S(1)}, bf16[64,4096]{1,0:T(8,128)(2,1)S(1)}, u32[]{:S(2)}, u32[]{:S(2)}) %collective-permute-start.7) | collective-permute-done | bytes 524320 | tf_op jit(solution)/shard_map/ppermute | solution.py:259
  53.8 1.6 %shard_map.98 = bf16[64,384]{1,0:T(8,128)(2,1)S(1)} custom-call(s32[3]{0:T(128)S(1)} %pad_add_fusion.place, bf16[256,4096]{1,0:T(8,128)(2,1)S(1)} %get-tuple-element.46.near, bf16[64,4096]{1,0:T(8,128)(2,1)S(1)} %collective-permute-done.7.late, bf16[128,4096]{1,0:T(8,128)(2,1)S(1)} %shard_map.96.pair, bf16[64,256]{1,0:T(8,128)(2,1)S(1)} %collective-permute-done.11.before, ...), custom_call_target="tpu_custom_call" | custom-call | flops 4000000000 | tf_op jit(solution)/shard_map/pallas_call | solution.py:302
  55.5 1.6 %collective-permute-start.13 = (bf16[64,640]{1,0:T(8,128)(2,1)S(1)}, bf16[64,640]{1,0:T(8,128)(2,1)S(1)}, u32[]{:S(2)}, u32[]{:S(2)}) collective-permute-start(bf16[64,640]{1,0:T(8,128)(2,1)S(1)} %pad_maximum_fusion.1), channel_id=1, source_target_pairs={{0,1},{1,0},{2,3},{3,2},{4,5},{5,4},{6,7},{7,6},{8,9},{9,8},{10,11... | collective-permute-start | bytes 245768 | tf_op jit(solution)/shard_map/ppermute | solution.py:262
  57.0 0.9 %multiply_reduce_fusion = f32[32]{0:T(128)S(1)} fusion(pred[32]{0:T(512)(128)(4,1)S(1)} %get-tuple-element.71, pred[32]{0:T(512)(128)(4,1)S(1)} %get-tuple-element.72, pred[32]{0:T(512)(128)(4,1)S(1)} %get-tuple-element.73, pred[32]{0:T(512)(128)(4,1)S(1)} %get-tuple-element.70, s32[32]{0:T(128)S(1)} %copy-done.6, s32[512]{0:T(512)S(1)} %copy-done.4), kind=kLoop, calls=%fused_computation.32 | loop fusion | flops 425952 | bytes 2432 | tf_op jit(solution)/shard_map/reduce_sum | solution.py:122
  57.9 0.8 %multiply_multiply_fusion = f32[32,512]{1,0:T(8,128)S(1)} fusion(f32[512]{0:T(512)S(1)} %copy-done.7, f32[32]{0:T(128)S(1)} %sqrt.3, pred[32]{0:T(512)(128)(4,1)S(1)} %get-tuple-element.71, pred[32]{0:T(512)(128)(4,1)S(1)} %get-tuple-element.72, pred[32]{0:T(512)(128)(4,1)S(1)} %get-tuple-element.73, pred[32]{0:T(512)(128)(4,1)S(1)} %get-tuple-element.70, ...), kind=kLoop, calls=%fused_computation.31 | loop fusion | flops 425984 | bytes 70016 | tf_op jit(solution)/shard_map/mul | solution.py:124
  58.7 0.1 fusion.31
  58.8 1.1 %collective-permute-done.13 = bf16[64,640]{1,0:T(8,128)(2,1)S(1)} collective-permute-done((bf16[64,640]{1,0:T(8,128)(2,1)S(1)}, bf16[64,640]{1,0:T(8,128)(2,1)S(1)}, u32[]{:S(2)}, u32[]{:S(2)}) %collective-permute-start.13) | collective-permute-done | bytes 81952 | tf_op jit(solution)/shard_map/ppermute | solution.py:262
  60.0 0.1 collective-permute-start.15
  60.1 3.6 %collective-permute-start.17 = (bf16[64,640]{1,0:T(8,128)(2,1)S(1)}, bf16[64,640]{1,0:T(8,128)(2,1)S(1)}, u32[]{:S(2)}, u32[]{:S(2)}) collective-permute-start(bf16[64,640]{1,0:T(8,128)(2,1)S(1)} %add_convert_fusion.refs_0_), channel_id=1, source_target_pairs={{0,12},{2,14},{4,8},{6,10},{8,4},{10,6},{12,0},{14,2},{1,13},{3,15... | collective-permute-start | bytes 245768 | tf_op jit(solution)/shard_map/ppermute | solution.py:259
  63.7 0.5 collective-permute-start.19
  64.2 0.4 multiply_convert_fusion.1
  64.6 0.1 collective-permute-start.14
  64.7 4.0 %collective-permute-done.15.refs_2_ = bf16[64,640]{1,0:T(8,128)(2,1)S(1)} collective-permute-done((bf16[64,640]{1,0:T(8,128)(2,1)S(1)}, bf16[64,640]{1,0:T(8,128)(2,1)S(1)}, u32[]{:S(2)}, u32[]{:S(2)}) %collective-permute-start.15) | collective-permute-done | bytes 81952 | tf_op jit(solution)/shard_map/ppermute | solution.py:259
  68.6 0.5 collective-permute-start.18
  69.1 0.1 collective-permute-start.20
  69.2 0.1 pad_maximum_fusion.w
  69.3 0.6 collective-permute-done.16.refs_3_
  69.9 0.2 collective-permute-done.18.refs_5_
  70.1 0.4 collective-permute-done.20.refs_7_
  70.4 3.5 %shard_map.99 = (f32[16,64,64]{2,1,0:T(8,128)}, f32[1,16]{1,0:T(1,128)}) custom-call(s32[3]{0:T(128)S(1)} %pad_add_fusion.place, bf16[16,64,512]{2,1,0:T(8,128)(2,1)S(1)} %pad_maximum_fusion.w, bf16[64,640]{1,0:T(8,128)(2,1)S(1)} %add_convert_fusion.refs_0_, bf16[64,640]{1,0:T(8,128)(2,1)S(1)} %collective-permute-done.14.refs_1_, ...), custom_call_target="tpu_custom_call" | custom-call | flops 1000000000 | tf_op jit(solution)/shard_map/pallas_call | solution.py:302
  (36 shorter events, 0.3 us)
Async XLA Ops:
  0.6 1.6 %copy-start = (bf16[64,16384]{1,0:T(8,128)(2,1)S(1)}, bf16[64,16384]{1,0:T(8,128)(2,1)}, u32[]{:S(2)}) copy-start(bf16[64,16384]{1,0:T(8,128)(2,1)} %param.8) | copy-start | bytes 6291460
  2.3 5.2 %collective-permute-start = (bf16[64,4096]{1,0:T(8,128)(2,1)S(1)}, bf16[64,4096]{1,0:T(8,128)(2,1)S(1)}, u32[]{:S(2)}, u32[]{:S(2)}) collective-permute-start(bf16[64,4096]{1,0:T(8,128)(2,1)S(1)} %constant_dynamic-slice_fusion.7.p0), channel_id=1, source_target_pairs={{0,2},{2,0},{4,6},{6,4},{8,10},{10,8},{12,14},{14,12},{1,3},{3,1},... | collective-permute-start | bytes 1572872 | tf_op jit(solution)/shard_map/ppermute | solution.py:259
  2.8 20.5 %collective-permute-start.6 = (bf16[64,1024]{1,0:T(8,128)(2,1)S(1)}, bf16[64,1024]{1,0:T(8,128)(2,1)S(1)}, u32[]{:S(2)}, u32[]{:S(2)}) collective-permute-start(bf16[64,1024]{1,0:T(8,128)(2,1)S(1)} %constant_dynamic-slice_fusion.6), channel_id=1, source_target_pairs={{0,12},{2,14},{4,8},{6,10},{8,4},{10,6},{12,0},{14,2},{1,13},{3,15... | collective-permute-start | bytes 393224 | tf_op jit(solution)/shard_map/ppermute | solution.py:259
  7.6 24.1 %copy-start.1 = (f32[256,1]{1,0:T(8,128)S(1)}, f32[256,1]{1,0:T(8,128)}, u32[]{:S(2)}) copy-start(f32[256,1]{1,0:T(8,128)} %constant.126.clone.dcol) | copy-start | bytes 3076
  7.6 24.1 %copy-start.2 = (f32[1,256]{1,0:T(1,128)S(1)}, f32[1,256]{1,0:T(1,128)}, u32[]{:S(2)}) copy-start(f32[1,256]{1,0:T(1,128)} %constant.125.clone.drow) | copy-start | bytes 3076
  7.6 24.1 %copy-start.3 = (f32[2,1,128]{2,1,0:T(1,128)S(1)}, f32[2,1,128]{2,1,0:T(1,128)}, u32[]{:S(2)}) copy-start(f32[2,1,128]{2,1,0:T(1,128)} %constant.127.clone.dpair) | copy-start | bytes 3076
  7.7 9.7 %collective-permute-start.2 = (bf16[64,2048]{1,0:T(8,128)(2,1)S(1)}, bf16[64,2048]{1,0:T(8,128)(2,1)S(1)}, u32[]{:S(2)}, u32[]{:S(2)}) collective-permute-start(bf16[64,2048]{1,0:T(8,128)(2,1)S(1)} %constant_dynamic-slice_fusion.3), channel_id=1, source_target_pairs={{0,4},{2,6},{4,0},{6,2},{8,12},{10,14},{12,8},{14,10},{1,5},{3,7},... | collective-permute-start | bytes 786440 | tf_op jit(solution)/shard_map/ppermute | solution.py:259
  7.8 15.4 %collective-permute-start.1 = (bf16[64,2048]{1,0:T(8,128)(2,1)S(1)}, bf16[64,2048]{1,0:T(8,128)(2,1)S(1)}, u32[]{:S(2)}, u32[]{:S(2)}) collective-permute-start(bf16[64,2048]{1,0:T(8,128)(2,1)S(1)} %constant_dynamic-slice_fusion.4), channel_id=1, source_target_pairs={{0,4},{2,6},{4,0},{6,2},{8,12},{10,14},{12,8},{14,10},{1,5},{3,7},... | collective-permute-start | bytes 786440 | tf_op jit(solution)/shard_map/ppermute | solution.py:259
  9.9 21.8 %collective-permute-start.5 = (bf16[64,4096]{1,0:T(8,128)(2,1)S(1)}, bf16[64,4096]{1,0:T(8,128)(2,1)S(1)}, u32[]{:S(2)}, u32[]{:S(2)}) collective-permute-start(bf16[64,4096]{1,0:T(8,128)(2,1)S(1)} %constant_dynamic-slice_fusion.2), channel_id=1, source_target_pairs={{0,2},{2,0},{4,6},{6,4},{8,10},{10,8},{12,14},{14,12},{1,3},{3,1},... | collective-permute-start | bytes 1572872 | tf_op jit(solution)/shard_map/ppermute | solution.py:259
  9.9 21.7 %collective-permute-start.8 = (bf16[64,3072]{1,0:T(8,128)(2,1)S(1)}, bf16[64,3072]{1,0:T(8,128)(2,1)S(1)}, u32[]{:S(2)}, u32[]{:S(2)}) collective-permute-start(bf16[64,3072]{1,0:T(8,128)(2,1)S(1)} %constant_dynamic-slice_fusion.5), channel_id=1, source_target_pairs={{0,12},{2,14},{4,8},{6,10},{8,4},{10,6},{12,0},{14,2},{1,13},{3,15... | collective-permute-start | bytes 1179656 | tf_op jit(solution)/shard_map/ppermute | solution.py:259
  17.4 14.2 %collective-permute-start.4 = (bf16[64,2048]{1,0:T(8,128)(2,1)S(1)}, bf16[64,2048]{1,0:T(8,128)(2,1)S(1)}, u32[]{:S(2)}, u32[]{:S(2)}) collective-permute-start(bf16[64,2048]{1,0:T(8,128)(2,1)S(1)} %collective-permute-done.2.p2b), channel_id=1, source_target_pairs={{0,2},{2,0},{4,6},{6,4},{8,10},{10,8},{12,14},{14,12},{1,3},{3,1},... | collective-permute-start | bytes 786440 | tf_op jit(solution)/shard_map/ppermute | solution.py:259
  23.2 8.5 %collective-permute-start.3 = (bf16[64,2048]{1,0:T(8,128)(2,1)S(1)}, bf16[64,2048]{1,0:T(8,128)(2,1)S(1)}, u32[]{:S(2)}, u32[]{:S(2)}) collective-permute-start(bf16[64,2048]{1,0:T(8,128)(2,1)S(1)} %collective-permute-done.1.p2a), channel_id=1, source_target_pairs={{0,2},{2,0},{4,6},{6,4},{8,10},{10,8},{12,14},{14,12},{1,3},{3,1},... | collective-permute-start | bytes 786440 | tf_op jit(solution)/shard_map/ppermute | solution.py:259
  23.2 10.5 %copy-start.4 = (s32[512]{0:T(512)S(1)}, s32[512]{0:T(512)}, u32[]{:S(2)}) copy-start(s32[512]{0:T(512)} %constant.128.clone) | copy-start | bytes 6148
  23.3 30.5 %collective-permute-start.7 = (bf16[64,4096]{1,0:T(8,128)(2,1)S(1)}, bf16[64,4096]{1,0:T(8,128)(2,1)S(1)}, u32[]{:S(2)}, u32[]{:S(2)}) collective-permute-start(bf16[64,4096]{1,0:T(8,128)(2,1)S(1)} %constant_dynamic-slice_fusion), channel_id=1, source_target_pairs={{0,8},{2,10},{4,12},{6,14},{8,0},{10,2},{12,4},{14,6},{1,9},{3,11}... | collective-permute-start | bytes 1572872 | tf_op jit(solution)/shard_map/ppermute | solution.py:259
  31.6 11.3 %collective-permute-start.10 = (bf16[64,3072]{1,0:T(8,128)(2,1)S(1)}, bf16[64,3072]{1,0:T(8,128)(2,1)S(1)}, u32[]{:S(2)}, u32[]{:S(2)}) collective-permute-start(bf16[64,3072]{1,0:T(8,128)(2,1)S(1)} %collective-permute-done.8.e0b.eb), channel_id=1, source_target_pairs={{0,2},{2,0},{4,6},{6,4},{8,10},{10,8},{12,14},{14,12},{1,3},{3,1},... | collective-permute-start | bytes 1179656 | tf_op jit(solution)/shard_map/ppermute | solution.py:259
  33.7 9.3 %collective-permute-start.12 = (bf16[64,256]{1,0:T(8,128)(2,1)S(1)}, bf16[64,256]{1,0:T(8,128)(2,1)S(1)}, u32[]{:S(2)}, u32[]{:S(2)}) collective-permute-start(bf16[64,256]{1,0:T(8,128)(2,1)S(1)} %get-tuple-element.60), channel_id=1, source_target_pairs={{0,4},{2,6},{4,0},{6,2},{8,12},{10,14},{12,8},{14,10},{1,5},{3,7},... | collective-permute-start | bytes 98312 | tf_op jit(solution)/shard_map/ppermute | solution.py:259
  34.0 9.0 %collective-permute-start.9 = (bf16[64,1024]{1,0:T(8,128)(2,1)S(1)}, bf16[64,1024]{1,0:T(8,128)(2,1)S(1)}, u32[]{:S(2)}, u32[]{:S(2)}) collective-permute-start(bf16[64,1024]{1,0:T(8,128)(2,1)S(1)} %collective-permute-done.6.e0a.ea), channel_id=1, source_target_pairs={{0,2},{2,0},{4,6},{6,4},{8,10},{10,8},{12,14},{14,12},{1,3},{3,1},... | collective-permute-start | bytes 393224 | tf_op jit(solution)/shard_map/ppermute | solution.py:259
  35.9 18.0 %collective-permute-start.11 = (bf16[64,256]{1,0:T(8,128)(2,1)S(1)}, bf16[64,256]{1,0:T(8,128)(2,1)S(1)}, u32[]{:S(2)}, u32[]{:S(2)}) collective-permute-start(bf16[64,256]{1,0:T(8,128)(2,1)S(1)} %shard_map.97), channel_id=1, source_target_pairs={{0,4},{2,6},{4,0},{6,2},{8,12},{10,14},{12,8},{14,10},{1,5},{3,7},... | collective-permute-start | bytes 98312 | tf_op jit(solution)/shard_map/ppermute | solution.py:259
  43.6 13.4 %copy-start.5 = (s32[32]{0:T(128)S(1)}, s32[32]{0:T(128)}, u32[]{:S(2)}) copy-start(s32[32]{0:T(128)} %param.10) | copy-start | bytes 388
  43.6 13.4 %copy-start.6 = (s32[32]{0:T(128)S(1)}, s32[32]{0:T(128)}, u32[]{:S(2)}) copy-start(s32[32]{0:T(128)} %param.9) | copy-start | bytes 388
  43.6 14.3 %copy-start.7 = (f32[512]{0:T(512)S(1)}, f32[512]{0:T(512)}, u32[]{:S(2)}) copy-start(f32[512]{0:T(512)} %constant.130) | copy-start | bytes 6148
  55.5 4.5 %collective-permute-start.13 = (bf16[64,640]{1,0:T(8,128)(2,1)S(1)}, bf16[64,640]{1,0:T(8,128)(2,1)S(1)}, u32[]{:S(2)}, u32[]{:S(2)}) collective-permute-start(bf16[64,640]{1,0:T(8,128)(2,1)S(1)} %pad_maximum_fusion.1), channel_id=1, source_target_pairs={{0,1},{1,0},{2,3},{3,2},{4,5},{5,4},{6,7},{7,6},{8,9},{9,8},{10,11... | collective-permute-start | bytes 245768 | tf_op jit(solution)/shard_map/ppermute | solution.py:262
  60.0 8.6 %collective-permute-start.15 = (bf16[64,640]{1,0:T(8,128)(2,1)S(1)}, bf16[64,640]{1,0:T(8,128)(2,1)S(1)}, u32[]{:S(2)}, u32[]{:S(2)}) collective-permute-start(bf16[64,640]{1,0:T(8,128)(2,1)S(1)} %add_convert_fusion.refs_0_), channel_id=1, source_target_pairs={{0,8},{2,10},{4,12},{6,14},{8,0},{10,2},{12,4},{14,6},{1,9},{3,11}... | collective-permute-start | bytes 245768 | tf_op jit(solution)/shard_map/ppermute | solution.py:259
  60.1 8.5 %collective-permute-start.17 = (bf16[64,640]{1,0:T(8,128)(2,1)S(1)}, bf16[64,640]{1,0:T(8,128)(2,1)S(1)}, u32[]{:S(2)}, u32[]{:S(2)}) collective-permute-start(bf16[64,640]{1,0:T(8,128)(2,1)S(1)} %add_convert_fusion.refs_0_), channel_id=1, source_target_pairs={{0,12},{2,14},{4,8},{6,10},{8,4},{10,6},{12,0},{14,2},{1,13},{3,15... | collective-permute-start | bytes 245768 | tf_op jit(solution)/shard_map/ppermute | solution.py:259
  63.7 5.5 %collective-permute-start.19 = (bf16[64,640]{1,0:T(8,128)(2,1)S(1)}, bf16[64,640]{1,0:T(8,128)(2,1)S(1)}, u32[]{:S(2)}, u32[]{:S(2)}) collective-permute-start(bf16[64,640]{1,0:T(8,128)(2,1)S(1)} %add_convert_fusion.refs_0_), channel_id=1, source_target_pairs={{0,4},{2,6},{4,0},{6,2},{8,12},{10,14},{12,8},{14,10},{1,5},{3,7},... | collective-permute-start | bytes 245768 | tf_op jit(solution)/shard_map/ppermute | solution.py:259
  64.6 4.7 %collective-permute-start.14 = (bf16[64,640]{1,0:T(8,128)(2,1)S(1)}, bf16[64,640]{1,0:T(8,128)(2,1)S(1)}, u32[]{:S(2)}, u32[]{:S(2)}) collective-permute-start(bf16[64,640]{1,0:T(8,128)(2,1)S(1)} %add_convert_fusion.refs_0_), channel_id=1, source_target_pairs={{0,2},{2,0},{4,6},{6,4},{8,10},{10,8},{12,14},{14,12},{1,3},{3,1},... | collective-permute-start | bytes 245768 | tf_op jit(solution)/shard_map/ppermute | solution.py:259
  68.6 1.3 %collective-permute-start.16 = (bf16[64,640]{1,0:T(8,128)(2,1)S(1)}, bf16[64,640]{1,0:T(8,128)(2,1)S(1)}, u32[]{:S(2)}, u32[]{:S(2)}) collective-permute-start(bf16[64,640]{1,0:T(8,128)(2,1)S(1)} %collective-permute-done.15.refs_2_), channel_id=1, source_target_pairs={{0,2},{2,0},{4,6},{6,4},{8,10},{10,8},{12,14},{14,12},{1,3},{3,1},... | collective-permute-start | bytes 245768 | tf_op jit(solution)/shard_map/ppermute | solution.py:259
  68.6 1.4 %collective-permute-start.18 = (bf16[64,640]{1,0:T(8,128)(2,1)S(1)}, bf16[64,640]{1,0:T(8,128)(2,1)S(1)}, u32[]{:S(2)}, u32[]{:S(2)}) collective-permute-start(bf16[64,640]{1,0:T(8,128)(2,1)S(1)} %collective-permute-done.17.refs_4_), channel_id=1, source_target_pairs={{0,2},{2,0},{4,6},{6,4},{8,10},{10,8},{12,14},{14,12},{1,3},{3,1},... | collective-permute-start | bytes 245768 | tf_op jit(solution)/shard_map/ppermute | solution.py:259
  69.1 1.3 %collective-permute-start.20 = (bf16[64,640]{1,0:T(8,128)(2,1)S(1)}, bf16[64,640]{1,0:T(8,128)(2,1)S(1)}, u32[]{:S(2)}, u32[]{:S(2)}) collective-permute-start(bf16[64,640]{1,0:T(8,128)(2,1)S(1)} %collective-permute-done.19.refs_6_), channel_id=1, source_target_pairs={{0,2},{2,0},{4,6},{6,4},{8,10},{10,8},{12,14},{14,12},{1,3},{3,1},... | collective-permute-start | bytes 245768 | tf_op jit(solution)/shard_map/ppermute | solution.py:259
